TPU v7x, 128 devices: a whole 4x4x4 slice. The times are simulated.
128 devices in a mesh: seqa: 16 (over x, z_hi, core), seqb: 8 (over y, z_lo).
Axes of the slice: x: 4, y: 4, z: 4 (z_hi: 2, z_lo: 2; z = z_hi * 2 + z_lo), core: 2. Of those that a mesh axis runs over, the one named last changes fastest.
Arguments:
- queries: bfloat16 [131072, 1024], P(('seqa', 'seqb')), may hold values from -6 to 6
- keys: bfloat16 [131072, 1024], P(('seqa', 'seqb')), may hold values from -6 to 6
- values: bfloat16 [131072, 1024], P(('seqa', 'seqb')), may hold values from -6 to 6
- grad_out: bfloat16 [131072, 1024], P(('seqa', 'seqb')), may hold values from -6 to 6
Outputs:
- attended: bfloat16 [131072, 1024], P(('seqa', 'seqb'))
- grad_queries: bfloat16 [131072, 1024], P(('seqa', 'seqb'))
- grad_keys: bfloat16 [131072, 1024], P(('seqa', 'seqb'))
- grad_values: bfloat16 [131072, 1024], P(('seqa', 'seqb'))
All inputs are finite; a program needn't handle non-finite values.
Results may differ from a plain program's by a relative error of at most 0.03.
Values may be sent and summed in bfloat16 or wider, within the bound.
No kernel may reach another device: no remote copies, remote signals or barrier semaphores. Data moves between devices by JAX's collectives and lax.ppermute only.
A program may use at most 256 MiB of HBM per device.

v0:
```python
import math

import jax
import jax.numpy as jnp
from jax import lax
from jax.sharding import PartitionSpec as P

HEAD_DIM = 64
BLOCK = 256


LOG_TWO = math.log(2.0)


def shifted(array, axis, by):
    size = lax.axis_size(axis)
    pairs = [(i, i + by) for i in range(size) if 0 <= i + by < size]
    return lax.ppermute(array, axis, pairs)


def coarsen(pieces, stride):
    shaped = pieces.astype(jnp.float32).reshape(pieces.shape[0] // stride, stride, pieces.shape[1])
    return shaped.mean(axis=1).astype(jnp.bfloat16)


def layout(block_number, block_size, half_size):
    if block_number % 2 == 0:
        fine_spans = (block_number, block_number + 4, block_number + 5)
    else:
        fine_spans = (block_number - 1, block_number, block_number + 4)
    if block_number // 2 % 2 == 0:
        wide_spans = (0, 4, 5)
    else:
        wide_spans = (0, 1, 5)
    return (
        (0, block_size, (block_number, block_number + 1, block_number + 2)),
        (1, half_size, fine_spans),
        (2, half_size, wide_spans),
        (3, half_size, (0, 1, 2)),
    )


def assemble(arrays, block_number, block_size, half_size):
    part_list = []
    for level_number, height, span_list in layout(block_number, block_size, half_size):
        for span_number in span_list:
            part_list.append(
                arrays[level_number][span_number * height : (span_number + 1) * height]
            )
    return jnp.concatenate(part_list, 0)


def spread(totals, gradients, block_number, block_size, half_size):
    totals = list(totals)
    offset = 0
    for level_number, height, span_list in layout(block_number, block_size, half_size):
        for span_number in span_list:
            totals[level_number] = (
                totals[level_number]
                .at[span_number * height : (span_number + 1) * height]
                .add(gradients[offset : offset + height])
            )
            offset += height
    return totals


def row_mask(validity, block_number, block_size, half_size):
    part_list = []
    for level_number, height, span_list in layout(block_number, block_size, half_size):
        for span_number in span_list:
            part_list.append(jnp.broadcast_to(validity[level_number][span_number], (height,)))
    return jnp.concatenate(part_list)


def row_bias(block_size, half_size):
    part_list = []
    for level_number, height, span_list in layout(0, block_size, half_size):
        for span_number in span_list:
            part_list.append(jnp.full((height,), level_number * LOG_TWO, jnp.float32))
    return jnp.concatenate(part_list)


def inside(first_index, amount, bound_value):
    row_index = first_index + jnp.arange(amount, dtype=jnp.int32)
    return (row_index >= 0) & (row_index < bound_value)


def neighbour_levels(pieces, fine_one, fine_two, block_size, half_size):
    lower_side = shifted(
        (pieces[-block_size:], fine_one[-2 * half_size :], fine_two), ("seqa", "seqb"), 1
    )
    upper_side = shifted(
        (pieces[:block_size], fine_one[: 2 * half_size], fine_two), ("seqa", "seqb"), -1
    )
    return (lower_side, upper_side)


def far_spans(coarsest):
    from_below = {}
    from_above = {}
    for distance in (2, 3):
        from_below[distance] = shifted(coarsest, ("seqa", "seqb"), distance)
        from_above[distance] = shifted(coarsest, ("seqa", "seqb"), -distance)
    return jnp.concatenate([from_below[3], from_below[2], from_above[2], from_above[3]], 0)


def far_returns(gradients, half_size):
    span_list = [
        gradients[slot_index * half_size : (slot_index + 1) * half_size] for slot_index in range(4)
    ]
    carried_sum = jnp.zeros_like(span_list[0])
    for distance, slot_index in ((2, 1), (3, 0)):
        carried_sum = carried_sum + shifted(
            span_list[slot_index].astype(jnp.bfloat16), ("seqa", "seqb"), -distance
        ).astype(jnp.float32)
    for distance, slot_index in ((2, 2), (3, 3)):
        carried_sum = carried_sum + shifted(
            span_list[slot_index].astype(jnp.bfloat16), ("seqa", "seqb"), distance
        ).astype(jnp.float32)
    return carried_sum


def neighbour_returns(totals, length, block_size, half_size):
    level_zero, level_one, level_two = (totals[0], totals[1], totals[2])
    breadth = level_zero.shape[1]
    own_zero = level_zero[block_size : 5 * block_size]
    own_one = level_one[2 * half_size : 6 * half_size]
    own_two = level_two[2 * half_size : 4 * half_size]
    extra_rows = jnp.zeros((length, breadth), jnp.float32)
    from_above = shifted(
        (level_zero[:block_size], level_one[: 2 * half_size], level_two[: 2 * half_size]),
        ("seqa", "seqb"),
        -1,
    )
    from_below = shifted(
        (level_zero[5 * block_size :], level_one[6 * half_size :], level_two[4 * half_size :]),
        ("seqa", "seqb"),
        1,
    )
    own_zero = own_zero.at[-block_size:].add(from_above[0]).at[:block_size].add(from_below[0])
    own_one = own_one.at[-2 * half_size :].add(from_above[1]).at[: 2 * half_size].add(from_below[1])
    own_two = own_two + from_above[2] + from_below[2]
    return (own_zero, own_one, own_two, extra_rows)


def attend(queries, grad_out, extended, usable, bias_rows, block_size, half_size):
    length, features = queries.shape
    block_count = length // block_size
    head_count = features // HEAD_DIM
    paired = 2
    stripe = paired * HEAD_DIM
    factor = HEAD_DIM ** (-0.5)

    def head_step(step_index, carried):
        mixed_all, query_all, totals = carried
        column = step_index * stripe
        key_ext = [lax.dynamic_slice_in_dim(array, column, stripe, 1) for array in extended]
        value_ext = [
            lax.dynamic_slice_in_dim(array, features + column, stripe, 1) for array in extended
        ]
        key_rows = jnp.stack(
            [
                assemble(key_ext, block_number, block_size, half_size)
                for block_number in range(block_count)
            ]
        )
        value_rows = jnp.stack(
            [
                assemble(value_ext, block_number, block_size, half_size)
                for block_number in range(block_count)
            ]
        )
        key_rows = key_rows.reshape(block_count, -1, paired, HEAD_DIM)
        value_rows = value_rows.reshape(block_count, -1, paired, HEAD_DIM)
        query_part = lax.dynamic_slice_in_dim(queries, column, stripe, 1).reshape(
            block_count, block_size, paired, HEAD_DIM
        )
        grad_part = lax.dynamic_slice_in_dim(grad_out, column, stripe, 1).reshape(
            block_count, block_size, paired, HEAD_DIM
        )
        scores = (
            jnp.einsum("bqhd,bkhd->bhqk", query_part, key_rows, preferred_element_type=jnp.float32)
            * factor
            + bias_rows
        )
        scores = jnp.where(usable[:, None, None, :], scores, -jnp.inf)
        highest = jnp.max(scores, axis=3, keepdims=True)
        weights = jnp.exp(scores - highest)
        probability = weights / jnp.sum(weights, axis=3, keepdims=True)
        probs_low = probability.astype(jnp.bfloat16)
        mixed_rows = jnp.einsum(
            "bhqk,bkhd->bqhd", probs_low, value_rows, preferred_element_type=jnp.float32
        ).astype(jnp.bfloat16)
        inner_sum = jnp.sum(
            grad_part.astype(jnp.float32) * mixed_rows.astype(jnp.float32), axis=3
        ).transpose(0, 2, 1)[..., None]
        dprobs = jnp.einsum(
            "bqhd,bkhd->bhqk", grad_part, value_rows, preferred_element_type=jnp.float32
        )
        dscores = (probability * (dprobs - inner_sum)).astype(jnp.bfloat16)
        query_grad = (
            jnp.einsum("bhqk,bkhd->bqhd", dscores, key_rows, preferred_element_type=jnp.float32)
            * factor
        )
        key_grad = (
            jnp.einsum("bhqk,bqhd->bkhd", dscores, query_part, preferred_element_type=jnp.float32)
            * factor
        )
        value_grad = jnp.einsum(
            "bhqk,bqhd->bkhd", probs_low, grad_part, preferred_element_type=jnp.float32
        )
        key_grad = key_grad.reshape(block_count, -1, stripe)
        value_grad = value_grad.reshape(block_count, -1, stripe)
        key_totals = [jnp.zeros((array.shape[0], stripe), jnp.float32) for array in extended]
        value_totals = [jnp.zeros((array.shape[0], stripe), jnp.float32) for array in extended]
        for block_number in range(block_count):
            key_totals = spread(
                key_totals, key_grad[block_number], block_number, block_size, half_size
            )
            value_totals = spread(
                value_totals, value_grad[block_number], block_number, block_size, half_size
            )
        updated = []
        for total_rows, key_total, value_total in zip(totals, key_totals, value_totals):
            total_rows = lax.dynamic_update_slice_in_dim(total_rows, key_total, column, 1)
            total_rows = lax.dynamic_update_slice_in_dim(
                total_rows, value_total, features + column, 1
            )
            updated.append(total_rows)
        mixed_all = lax.dynamic_update_slice_in_dim(
            mixed_all, mixed_rows.reshape(length, stripe), column, 1
        )
        query_all = lax.dynamic_update_slice_in_dim(
            query_all, query_grad.reshape(length, stripe).astype(jnp.bfloat16), column, 1
        )
        return (mixed_all, query_all, tuple(updated))

    initial = (
        jnp.zeros((length, features), jnp.bfloat16),
        jnp.zeros((length, features), jnp.bfloat16),
        tuple((jnp.zeros((array.shape[0], 2 * features), jnp.float32) for array in extended)),
    )
    return lax.fori_loop(0, head_count // paired, head_step, initial)


def local(queries, keys, values, grad_out):
    length, features = queries.shape
    block_size = BLOCK
    half_size = block_size // 2
    block_count = length // block_size
    device_index = lax.axis_index(("seqa", "seqb"))
    devices = lax.axis_size(("seqa", "seqb"))
    pieces = jnp.concatenate([keys, values], axis=1)
    fine_one = coarsen(pieces, 2)
    fine_two = coarsen(pieces, 4)
    coarsest = coarsen(pieces, 8)
    lower_side, upper_side = neighbour_levels(pieces, fine_one, fine_two, block_size, half_size)
    far_rows = far_spans(coarsest)
    odd_device = device_index % 2 == 1
    extended = [
        jnp.concatenate([lower_side[0], pieces, upper_side[0]], 0),
        jnp.concatenate([lower_side[1], fine_one, upper_side[1]], 0),
        jnp.concatenate([lower_side[2], fine_two, upper_side[2]], 0),
        jnp.where(odd_device, far_rows[: 3 * half_size], far_rows[half_size:]),
    ]
    beside_all = device_index + jnp.array([-3, -2, 2, 3], jnp.int32)
    far_valid = (beside_all >= 0) & (beside_all < devices)
    validity = [
        inside(device_index * block_count - 1, block_count + 2, block_count * devices),
        inside(device_index * block_count - 2, block_count + 4, block_count * devices),
        inside(
            device_index * (block_count // 2) - 2, block_count // 2 + 4, block_count // 2 * devices
        ),
        jnp.where(odd_device, far_valid[:3], far_valid[1:]),
    ]
    usable = jnp.stack(
        [
            row_mask(validity, block_number, block_size, half_size)
            for block_number in range(block_count)
        ]
    )
    bias_rows = row_bias(block_size, half_size)
    mixed_all, query_all, totals = attend(
        queries, grad_out, extended, usable, bias_rows, block_size, half_size
    )
    far_grads = totals[3]
    empty_span = jnp.zeros((half_size, far_grads.shape[1]), jnp.float32)
    far_sent = jnp.where(
        odd_device,
        jnp.concatenate([far_grads, empty_span], 0),
        jnp.concatenate([empty_span, far_grads], 0),
    )
    own_three = far_returns(far_sent, half_size)
    own_zero, own_one, own_two, extra_rows = neighbour_returns(
        totals, length, block_size, half_size
    )
    summed = (
        own_zero
        + jnp.repeat(own_one / 2, 2, axis=0)
        + jnp.repeat(own_two / 4, 4, axis=0)
        + jnp.repeat(own_three / 8, 8, axis=0)
        + extra_rows
    )
    return (
        mixed_all,
        query_all,
        summed[:, :features].astype(jnp.bfloat16),
        summed[:, features:].astype(jnp.bfloat16),
    )


def solution(mesh):
    placed = (
        P(("seqa", "seqb"), None),
        P(("seqa", "seqb"), None),
        P(("seqa", "seqb"), None),
        P(("seqa", "seqb"), None),
    )
    return jax.shard_map(
        local,
        mesh=mesh,
        in_specs=placed,
        out_specs=(
            P(("seqa", "seqb"), None),
            P(("seqa", "seqb"), None),
            P(("seqa", "seqb"), None),
            P(("seqa", "seqb"), None),
        ),
        check_vma=False,
    )
```

profile of v0, /device:TPU:36, one launch (start us, length us, event | category | flops | bytes accessed | tf_op | source)
XLA Modules:
  0.0 1115.6 jit_solution(12269489717425767563)
XLA Ops:
  29.0 8.3 convert_reduce_fusion.1
  58.9 12.6 %convert_reduce_fusion.2 = f32[512,2048]{1,0:T(8,128)S(1)} fusion(bf16[512,2,1024]{2,1,0:T(2,128)(2,1)} %concatenate.603, bf16[512,2,1024]{2,1,0:T(2,128)(2,1)S(1)} %copy-done.8), kind=kLoop, calls=%fused_computation.260 | loop fusion | flops 9437184 | bytes 8388608 | tf_op jit(solution)/shard_map/reduce_sum | solution.py:23
  112.1 7.9 collective-permute-start.1
  126.3 37.4 %collective-permute-done.4 = bf16[256,2048]{1,0:T(8,128)(2,1)} collective-permute-done((bf16[256,2048]{1,0:T(8,128)(2,1)S(1)}, bf16[256,2048]{1,0:T(8,128)(2,1)}, u32[]{:S(2)}, u32[]{:S(2)}) %collective-permute-start.4) | collective-permute-done | bytes 1048608 | tf_op jit(solution)/shard_map/ppermute | solution.py:18
  171.5 14.7 %collective-permute-done.2 = bf16[256,2048]{1,0:T(8,128)(2,1)} collective-permute-done((bf16[256,2048]{1,0:T(8,128)(2,1)}, bf16[256,2048]{1,0:T(8,128)(2,1)}, u32[]{:S(2)}, u32[]{:S(2)}) %collective-permute-start.2) | collective-permute-done | bytes 1048608 | tf_op jit(solution)/shard_map/ppermute | solution.py:18
  189.9 6.4 copy.47
  196.3 7.4 collective-permute-done
  203.8 10.0 pad_maximum_fusion.9
  231.8 556.4 %while.126 = (s32[]{:T(128)}, bf16[1024,1024]{1,0:T(8,128)(2,1)}, bf16[1024,1024]{1,0:T(8,128)(2,1)}, f32[1536,2048]{0,1:T(8,128)}, f32[1024,2048]{0,1:T(8,128)}...) while((s32[]{:T(128)}, bf16[1024,1024]{1,0:T(8,128)(2,1)}, ...), condition=%wide.region_7.8_spmd, body=%wide.region_3.7_spmd.sunk | while | flops 3078488064 | bytes 295821152 | solution.py:243
  245.3 9.4 fusion.234
  254.7 8.3 fusion.235
  270.3 6.4 multiply_convert_fusion.5
  276.7 6.3 fusion.236
  314.8 9.4 fusion.234
  324.2 8.3 fusion.235
  339.8 6.4 multiply_convert_fusion.5
  346.2 6.3 fusion.236
  384.3 9.4 fusion.234
  393.8 8.3 fusion.235
  409.4 6.4 multiply_convert_fusion.5
  415.8 6.3 fusion.236
  454.0 9.4 fusion.234
  463.4 8.3 fusion.235
  479.0 6.4 multiply_convert_fusion.5
  523.4 9.4 fusion.234
  532.8 8.3 fusion.235
  548.4 6.4 multiply_convert_fusion.5
  592.9 9.4 fusion.234
  602.3 8.3 fusion.235
  617.9 6.4 multiply_convert_fusion.5
  662.3 9.4 fusion.234
  671.8 8.3 fusion.235
  687.4 6.4 multiply_convert_fusion.5
  731.8 9.4 fusion.234
  741.2 8.3 fusion.235
  756.8 6.4 multiply_convert_fusion.5
  793.3 6.7 copy.60
  812.6 8.8 collective-permute-start.16
  825.3 9.2 copy.56
  839.2 39.9 %collective-permute-start.12 = (f32[256,2048]{1,0:T(8,128)}, f32[256,2048]{1,0:T(8,128)}, u32[]{:S(2)}, u32[]{:S(2)}) collective-permute-start(f32[256,2048]{1,0:T(8,128)} %get-tuple-element.2808), channel_id=1, source_target_pairs={{1,0},{2,1},{3,2},{4,3},{5,4},{6,5},{7,6},{8,7},{9,8},{10,9},{11,1... | collective-permute-start | bytes 6291464 | tf_op jit(solution)/shard_map/ppermute | solution.py:18
  879.1 12.7 %copy.52 = f32[1536,2048]{1,0:T(8,128)} copy(f32[1536,2048]{0,1:T(8,128)} %get-tuple-element.2587) | data formatting | bytes 25165824 | tf_op jit(solution)/shard_map/while | solution.py:243
  922.9 43.8 %collective-permute-done.15 = f32[256,2048]{1,0:T(8,128)} collective-permute-done((f32[256,2048]{1,0:T(8,128)}, f32[256,2048]{1,0:T(8,128)}, u32[]{:S(2)}, u32[]{:S(2)}) %collective-permute-start.15) | collective-permute-done | bytes 2097184 | tf_op jit(solution)/shard_map/ppermute | solution.py:18
  970.1 12.0 %collective-permute-done.12 = f32[256,2048]{1,0:T(8,128)} collective-permute-done((f32[256,2048]{1,0:T(8,128)}, f32[256,2048]{1,0:T(8,128)}, u32[]{:S(2)}, u32[]{:S(2)}) %collective-permute-start.12) | collective-permute-done | bytes 2097184 | tf_op jit(solution)/shard_map/ppermute | solution.py:18
  991.7 10.3 reshape.5082
  1001.9 54.6 %collective-permute-done.13 = f32[256,2048]{1,0:T(8,128)} collective-permute-done((f32[256,2048]{1,0:T(8,128)}, f32[256,2048]{1,0:T(8,128)}, u32[]{:S(2)}, u32[]{:S(2)}) %collective-permute-start.13) | collective-permute-done | bytes 2097184 | tf_op jit(solution)/shard_map/ppermute | solution.py:18
  1068.8 10.9 reshape.5081
  1083.8 17.6 %collective-permute-done.11 = f32[256,2048]{1,0:T(8,128)} collective-permute-done((f32[256,2048]{1,0:T(8,128)}, f32[256,2048]{1,0:T(8,128)}, u32[]{:S(2)}, u32[]{:S(2)}) %collective-permute-start.11) | collective-permute-done | bytes 2097184 | tf_op jit(solution)/shard_map/ppermute | solution.py:18
  1105.3 7.4 fusion.96
  (1450 shorter events, 555.3 us)
Async XLA Ops:
  0.6 22.1 %copy-start.4 = (bf16[1024,1024]{1,0:T(8,128)(2,1)S(1)}, bf16[1024,1024]{1,0:T(8,128)(2,1)}, u32[]{:S(2)}) copy-start(bf16[1024,1024]{1,0:T(8,128)(2,1)} %param.208) | copy-start | bytes 6291460
  6.7 80.1 %collective-permute-start.9 = (bf16[128,2048]{1,0:T(8,128)(2,1)}, bf16[128,2048]{1,0:T(8,128)(2,1)}, u32[]{:S(2)}, u32[]{:S(2)}) collective-permute-start(bf16[128,2048]{1,0:T(8,128)(2,1)} %multiply_convert_fusion.3), channel_id=1, source_target_pairs={{3,0},{4,1},{5,2},{6,3},{7,4},{8,5},{9,6},{10,7},{11,8},{12,9},{13... | collective-permute-start | bytes 1572872 | tf_op jit(solution)/shard_map/ppermute | solution.py:18
  12.4 88.2 %collective-permute-start.8 = (bf16[128,2048]{1,0:T(8,128)(2,1)}, bf16[128,2048]{1,0:T(8,128)(2,1)}, u32[]{:S(2)}, u32[]{:S(2)}) collective-permute-start(bf16[128,2048]{1,0:T(8,128)(2,1)} %multiply_convert_fusion.3), channel_id=1, source_target_pairs={{2,0},{3,1},{4,2},{5,3},{6,4},{7,5},{8,6},{9,7},{10,8},{11,9},{12,... | collective-permute-start | bytes 1572872 | tf_op jit(solution)/shard_map/ppermute | solution.py:18
  15.6 86.9 %collective-permute-start.7 = (bf16[128,2048]{1,0:T(8,128)(2,1)}, bf16[128,2048]{1,0:T(8,128)(2,1)}, u32[]{:S(2)}, u32[]{:S(2)}) collective-permute-start(bf16[128,2048]{1,0:T(8,128)(2,1)} %multiply_convert_fusion.3), channel_id=1, source_target_pairs={{0,2},{1,3},{2,4},{3,5},{4,6},{5,7},{6,8},{7,9},{8,10},{9,11},{10,... | collective-permute-start | bytes 1572872 | tf_op jit(solution)/shard_map/ppermute | solution.py:18
  18.2 92.0 %collective-permute-start.6 = (bf16[128,2048]{1,0:T(8,128)(2,1)}, bf16[128,2048]{1,0:T(8,128)(2,1)}, u32[]{:S(2)}, u32[]{:S(2)}) collective-permute-start(bf16[128,2048]{1,0:T(8,128)(2,1)} %multiply_convert_fusion.3), channel_id=1, source_target_pairs={{0,3},{1,4},{2,5},{3,6},{4,7},{5,8},{6,9},{7,10},{8,11},{9,12},{10... | collective-permute-start | bytes 1572872 | tf_op jit(solution)/shard_map/ppermute | solution.py:18
  37.5 74.6 %collective-permute-start.5 = (bf16[256,2048]{1,0:T(8,128)(2,1)S(1)}, bf16[256,2048]{1,0:T(8,128)(2,1)}, u32[]{:S(2)}, u32[]{:S(2)}) collective-permute-start(bf16[256,2048]{1,0:T(8,128)(2,1)S(1)} %multiply_convert_fusion.2), channel_id=1, source_target_pairs={{1,0},{2,1},{3,2},{4,3},{5,4},{6,5},{7,6},{8,7},{9,8},{10,9},{11,1... | collective-permute-start | bytes 3145736 | tf_op jit(solution)/shard_map/ppermute | solution.py:18
  71.5 15.2 %copy-start.15 = (s32[4]{0:T(128)S(1)}, s32[4]{0:T(128)}, u32[]{:S(2)}) copy-start(s32[4]{0:T(128)} %constant.3911.clone) | copy-start | bytes 52
  71.5 35.9 %copy-start.6 = (bf16[1024,1024]{0,1:T(8,128)(2,1)S(1)}, bf16[1024,1024]{0,1:T(8,128)(2,1)}, u32[]{:S(2)}) copy-start(bf16[1024,1024]{0,1:T(8,128)(2,1)} %copy.45) | copy-start | bytes 6291460
  86.7 76.9 %collective-permute-start.4 = (bf16[256,2048]{1,0:T(8,128)(2,1)S(1)}, bf16[256,2048]{1,0:T(8,128)(2,1)}, u32[]{:S(2)}, u32[]{:S(2)}) collective-permute-start(bf16[256,2048]{1,0:T(8,128)(2,1)S(1)} %multiply_convert_fusion.2), channel_id=1, source_target_pairs={{0,1},{1,2},{2,3},{3,4},{4,5},{5,6},{6,7},{7,8},{8,9},{9,10},{10,1... | collective-permute-start | bytes 3145736 | tf_op jit(solution)/shard_map/ppermute | solution.py:18
  100.6 85.5 %collective-permute-start.2 = (bf16[256,2048]{1,0:T(8,128)(2,1)}, bf16[256,2048]{1,0:T(8,128)(2,1)}, u32[]{:S(2)}, u32[]{:S(2)}) collective-permute-start(bf16[256,2048]{1,0:T(8,128)(2,1)} %get-tuple-element.2819), channel_id=1, source_target_pairs={{0,1},{1,2},{2,3},{3,4},{4,5},{5,6},{6,7},{7,8},{8,9},{9,10},{10,1... | collective-permute-start | bytes 3145736 | tf_op jit(solution)/shard_map/ppermute | solution.py:18
  102.5 83.6 %collective-permute-start.3 = (bf16[256,2048]{1,0:T(8,128)(2,1)}, bf16[256,2048]{1,0:T(8,128)(2,1)}, u32[]{:S(2)}, u32[]{:S(2)}) collective-permute-start(bf16[256,2048]{1,0:T(8,128)(2,1)} %get-tuple-element.2820), channel_id=1, source_target_pairs={{1,0},{2,1},{3,2},{4,3},{5,4},{6,5},{7,6},{8,7},{9,8},{10,9},{11,1... | collective-permute-start | bytes 3145736 | tf_op jit(solution)/shard_map/ppermute | solution.py:18
  110.2 93.6 %collective-permute-start = (bf16[256,2048]{0,1:T(8,128)(2,1)}, bf16[256,2048]{0,1:T(8,128)(2,1)}, u32[]{:S(2)}, u32[]{:S(2)}) collective-permute-start(bf16[256,2048]{0,1:T(8,128)(2,1)} %get-tuple-element.2813), channel_id=1, source_target_pairs={{0,1},{1,2},{2,3},{3,4},{4,5},{5,6},{6,7},{7,8},{8,9},{9,10},{10,1... | collective-permute-start | bytes 3145736 | tf_op jit(solution)/shard_map/ppermute | solution.py:18
  112.1 91.7 %collective-permute-start.1 = (bf16[256,2048]{0,1:T(8,128)(2,1)}, bf16[256,2048]{0,1:T(8,128)(2,1)}, u32[]{:S(2)}, u32[]{:S(2)}) collective-permute-start(bf16[256,2048]{0,1:T(8,128)(2,1)} %get-tuple-element.2814), channel_id=1, source_target_pairs={{1,0},{2,1},{3,2},{4,3},{5,4},{6,5},{7,6},{8,7},{9,8},{10,9},{11,1... | collective-permute-start | bytes 3145736 | tf_op jit(solution)/shard_map/ppermute | solution.py:18
  254.7 15.6 %slice-start = ((s8[15728640]{0:T(1024)(128)(4,1)}), s8[4194304]{0:T(1024)(128)(4,1)S(1)}, s32[]{:S(2)}) async-start(s8[15728640]{0:T(1024)(128)(4,1)} %bitcast.381), calls=%async_computation | async-start | bytes 8388608 | tf_op jit(solution)/shard_map/while
  254.7 15.6 %slice-start.1 = ((s8[15728640]{0:T(1024)(128)(4,1)}), s8[4194304]{0:T(1024)(128)(4,1)S(1)}, s32[]{:S(2)}) async-start(s8[15728640]{0:T(1024)(128)(4,1)} %bitcast.381), calls=%async_computation.1 | async-start | bytes 8388608 | tf_op jit(solution)/shard_map/while
  313.6 10.5 copy-start.9
  313.6 10.5 copy-start.10
  324.2 15.6 %slice-start = ((s8[15728640]{0:T(1024)(128)(4,1)}), s8[4194304]{0:T(1024)(128)(4,1)S(1)}, s32[]{:S(2)}) async-start(s8[15728640]{0:T(1024)(128)(4,1)} %bitcast.381), calls=%async_computation | async-start | bytes 8388608 | tf_op jit(solution)/shard_map/while
  324.2 15.6 %slice-start.1 = ((s8[15728640]{0:T(1024)(128)(4,1)}), s8[4194304]{0:T(1024)(128)(4,1)S(1)}, s32[]{:S(2)}) async-start(s8[15728640]{0:T(1024)(128)(4,1)} %bitcast.381), calls=%async_computation.1 | async-start | bytes 8388608 | tf_op jit(solution)/shard_map/while
  393.7 15.6 %slice-start = ((s8[15728640]{0:T(1024)(128)(4,1)}), s8[4194304]{0:T(1024)(128)(4,1)S(1)}, s32[]{:S(2)}) async-start(s8[15728640]{0:T(1024)(128)(4,1)} %bitcast.381), calls=%async_computation | async-start | bytes 8388608 | tf_op jit(solution)/shard_map/while
  393.7 15.6 %slice-start.1 = ((s8[15728640]{0:T(1024)(128)(4,1)}), s8[4194304]{0:T(1024)(128)(4,1)S(1)}, s32[]{:S(2)}) async-start(s8[15728640]{0:T(1024)(128)(4,1)} %bitcast.381), calls=%async_computation.1 | async-start | bytes 8388608 | tf_op jit(solution)/shard_map/while
  452.8 10.5 copy-start.9
  452.8 10.5 copy-start.10
  463.4 15.6 %slice-start = ((s8[15728640]{0:T(1024)(128)(4,1)}), s8[4194304]{0:T(1024)(128)(4,1)S(1)}, s32[]{:S(2)}) async-start(s8[15728640]{0:T(1024)(128)(4,1)} %bitcast.381), calls=%async_computation | async-start | bytes 8388608 | tf_op jit(solution)/shard_map/while
  463.4 15.6 %slice-start.1 = ((s8[15728640]{0:T(1024)(128)(4,1)}), s8[4194304]{0:T(1024)(128)(4,1)S(1)}, s32[]{:S(2)}) async-start(s8[15728640]{0:T(1024)(128)(4,1)} %bitcast.381), calls=%async_computation.1 | async-start | bytes 8388608 | tf_op jit(solution)/shard_map/while
  522.2 10.5 copy-start.9
  522.3 10.5 copy-start.10
  532.8 15.6 %slice-start = ((s8[15728640]{0:T(1024)(128)(4,1)}), s8[4194304]{0:T(1024)(128)(4,1)S(1)}, s32[]{:S(2)}) async-start(s8[15728640]{0:T(1024)(128)(4,1)} %bitcast.381), calls=%async_computation | async-start | bytes 8388608 | tf_op jit(solution)/shard_map/while
  532.8 15.6 %slice-start.1 = ((s8[15728640]{0:T(1024)(128)(4,1)}), s8[4194304]{0:T(1024)(128)(4,1)S(1)}, s32[]{:S(2)}) async-start(s8[15728640]{0:T(1024)(128)(4,1)} %bitcast.381), calls=%async_computation.1 | async-start | bytes 8388608 | tf_op jit(solution)/shard_map/while
  591.7 10.5 copy-start.9
  591.8 10.5 copy-start.10
  602.3 15.6 %slice-start = ((s8[15728640]{0:T(1024)(128)(4,1)}), s8[4194304]{0:T(1024)(128)(4,1)S(1)}, s32[]{:S(2)}) async-start(s8[15728640]{0:T(1024)(128)(4,1)} %bitcast.381), calls=%async_computation | async-start | bytes 8388608 | tf_op jit(solution)/shard_map/while
  602.3 15.6 %slice-start.1 = ((s8[15728640]{0:T(1024)(128)(4,1)}), s8[4194304]{0:T(1024)(128)(4,1)S(1)}, s32[]{:S(2)}) async-start(s8[15728640]{0:T(1024)(128)(4,1)} %bitcast.381), calls=%async_computation.1 | async-start | bytes 8388608 | tf_op jit(solution)/shard_map/while
  671.7 15.6 %slice-start = ((s8[15728640]{0:T(1024)(128)(4,1)}), s8[4194304]{0:T(1024)(128)(4,1)S(1)}, s32[]{:S(2)}) async-start(s8[15728640]{0:T(1024)(128)(4,1)} %bitcast.381), calls=%async_computation | async-start | bytes 8388608 | tf_op jit(solution)/shard_map/while
  671.7 15.6 %slice-start.1 = ((s8[15728640]{0:T(1024)(128)(4,1)}), s8[4194304]{0:T(1024)(128)(4,1)S(1)}, s32[]{:S(2)}) async-start(s8[15728640]{0:T(1024)(128)(4,1)} %bitcast.381), calls=%async_computation.1 | async-start | bytes 8388608 | tf_op jit(solution)/shard_map/while
  741.2 15.6 %slice-start = ((s8[15728640]{0:T(1024)(128)(4,1)}), s8[4194304]{0:T(1024)(128)(4,1)S(1)}, s32[]{:S(2)}) async-start(s8[15728640]{0:T(1024)(128)(4,1)} %bitcast.381), calls=%async_computation | async-start | bytes 8388608 | tf_op jit(solution)/shard_map/while
  741.2 15.6 %slice-start.1 = ((s8[15728640]{0:T(1024)(128)(4,1)}), s8[4194304]{0:T(1024)(128)(4,1)S(1)}, s32[]{:S(2)}) async-start(s8[15728640]{0:T(1024)(128)(4,1)} %bitcast.381), calls=%async_computation.1 | async-start | bytes 8388608 | tf_op jit(solution)/shard_map/while
  804.7 116.3 %collective-permute-start.14 = (f32[256,2048]{1,0:T(8,128)}, f32[256,2048]{1,0:T(8,128)}, u32[]{:S(2)}, u32[]{:S(2)}) collective-permute-start(f32[256,2048]{1,0:T(8,128)} %get-tuple-element.2809), channel_id=1, source_target_pairs={{1,0},{2,1},{3,2},{4,3},{5,4},{6,5},{7,6},{8,7},{9,8},{10,9},{11,1... | collective-permute-start | bytes 6291464 | tf_op jit(solution)/shard_map/ppermute | solution.py:18
  806.6 160.1 %collective-permute-start.15 = (f32[256,2048]{1,0:T(8,128)}, f32[256,2048]{1,0:T(8,128)}, u32[]{:S(2)}, u32[]{:S(2)}) collective-permute-start(f32[256,2048]{1,0:T(8,128)} %get-tuple-element.2810), channel_id=1, source_target_pairs={{0,1},{1,2},{2,3},{3,4},{4,5},{5,6},{6,7},{7,8},{8,9},{9,10},{10,1... | collective-permute-start | bytes 6291464 | tf_op jit(solution)/shard_map/ppermute | solution.py:18
  812.6 26.6 %collective-permute-start.16 = (bf16[128,2048]{1,0:T(8,128)(2,1)}, bf16[128,2048]{1,0:T(8,128)(2,1)S(1)}, u32[]{:S(2)}, u32[]{:S(2)}) collective-permute-start(bf16[128,2048]{1,0:T(8,128)(2,1)} %get-tuple-element.2815), channel_id=1, source_target_pairs={{2,0},{3,1},{4,2},{5,3},{6,4},{7,5},{8,6},{9,7},{10,8},{11,9},{12,... | collective-permute-start | bytes 1572872 | tf_op jit(solution)/shard_map/ppermute | solution.py:18
  821.4 70.4 %collective-permute-start.19 = (bf16[128,2048]{1,0:T(8,128)(2,1)}, bf16[128,2048]{1,0:T(8,128)(2,1)S(1)}, u32[]{:S(2)}, u32[]{:S(2)}) collective-permute-start(bf16[128,2048]{1,0:T(8,128)(2,1)} %get-tuple-element.2816), channel_id=1, source_target_pairs={{0,3},{1,4},{2,5},{3,6},{4,7},{5,8},{6,9},{7,10},{8,11},{9,12},{10... | collective-permute-start | bytes 1572872 | tf_op jit(solution)/shard_map/ppermute | solution.py:18
  823.3 73.1 %collective-permute-start.18 = (bf16[128,2048]{1,0:T(8,128)(2,1)S(1)}, bf16[128,2048]{1,0:T(8,128)(2,1)S(1)}, u32[]{:S(2)}, u32[]{:S(2)}) collective-permute-start(bf16[128,2048]{1,0:T(8,128)(2,1)S(1)} %get-tuple-element.2817), channel_id=1, source_target_pairs={{0,2},{1,3},{2,4},{3,5},{4,6},{5,7},{6,8},{7,9},{8,10},{9,11},{10,... | collective-permute-start | bytes 1572872 | tf_op jit(solution)/shard_map/ppermute | solution.py:18
  839.2 142.8 %collective-permute-start.12 = (f32[256,2048]{1,0:T(8,128)}, f32[256,2048]{1,0:T(8,128)}, u32[]{:S(2)}, u32[]{:S(2)}) collective-permute-start(f32[256,2048]{1,0:T(8,128)} %get-tuple-element.2808), channel_id=1, source_target_pairs={{1,0},{2,1},{3,2},{4,3},{5,4},{6,5},{7,6},{8,7},{9,8},{10,9},{11,1... | collective-permute-start | bytes 6291464 | tf_op jit(solution)/shard_map/ppermute | solution.py:18
  891.8 23.7 %collective-permute-start.17 = (bf16[128,2048]{1,0:T(8,128)(2,1)S(1)}, bf16[128,2048]{1,0:T(8,128)(2,1)S(1)}, u32[]{:S(2)}, u32[]{:S(2)}) collective-permute-start(bf16[128,2048]{1,0:T(8,128)(2,1)S(1)} %get-tuple-element.2818), channel_id=1, source_target_pairs={{3,0},{4,1},{5,2},{6,3},{7,4},{8,5},{9,6},{10,7},{11,8},{12,9},{13... | collective-permute-start | bytes 1572872 | tf_op jit(solution)/shard_map/ppermute | solution.py:18
  896.5 160.1 %collective-permute-start.13 = (f32[256,2048]{1,0:T(8,128)}, f32[256,2048]{1,0:T(8,128)}, u32[]{:S(2)}, u32[]{:S(2)}) collective-permute-start(f32[256,2048]{1,0:T(8,128)} %get-tuple-element.2807), channel_id=1, source_target_pairs={{0,1},{1,2},{2,3},{3,4},{4,5},{5,6},{6,7},{7,8},{8,9},{9,10},{10,1... | collective-permute-start | bytes 6291464 | tf_op jit(solution)/shard_map/ppermute | solution.py:18
  915.5 185.9 %collective-permute-start.11 = (f32[256,2048]{1,0:T(8,128)}, f32[256,2048]{1,0:T(8,128)}, u32[]{:S(2)}, u32[]{:S(2)}) collective-permute-start(f32[256,2048]{1,0:T(8,128)} %get-tuple-element.2805), channel_id=1, source_target_pairs={{0,1},{1,2},{2,3},{3,4},{4,5},{5,6},{6,7},{7,8},{8,9},{9,10},{10,1... | collective-permute-start | bytes 6291464 | tf_op jit(solution)/shard_map/ppermute | solution.py:18
  921.0 158.8 %collective-permute-start.10 = (f32[256,2048]{1,0:T(8,128)}, f32[256,2048]{1,0:T(8,128)}, u32[]{:S(2)}, u32[]{:S(2)}) collective-permute-start(f32[256,2048]{1,0:T(8,128)} %get-tuple-element.2806), channel_id=1, source_target_pairs={{1,0},{2,1},{3,2},{4,3},{5,4},{6,5},{7,6},{8,7},{9,8},{10,9},{11,1... | collective-permute-start | bytes 6291464 | tf_op jit(solution)/shard_map/ppermute | solution.py:18
  1079.7 25.6 %copy-start.5 = (f32[1024,2048]{1,0:T(8,128)S(1)}, f32[1024,2048]{1,0:T(8,128)}, u32[]{:S(2)}) copy-start(f32[1024,2048]{1,0:T(8,128)} %reshape.5081) | copy-start | bytes 25165828
  (84 other events, 348.2 us)
where the time goes:
time: 1140 us; the launch traced here: 1120 us
  local copies, waits for them, and re-layouts  379 us (33%)
  matrix products  261 us (23%)
  waiting for transfers between devices  188 us (16%)
  other arithmetic  162 us (14%)
  starting transfers between devices  115 us (10%)
    ppermute x20, waiting for transfers between devices, shifted(): return lax.ppermute(array, axis, pairs)  188 us
    ppermute x20, starting transfers between devices, shifted(): return lax.ppermute(array, axis, pairs)  115 us
    while x264, local copies, waits for them, and re-layouts  84.2 us
    sub x8, matrix products, head_step(): weights = jnp.exp(scores - highest)  75.1 us
    convert_element_type x8, other arithmetic, head_step(): probs_low = probability.astype(jnp.bfloat16)  66.3 us
    dot_general x8, matrix products, head_step(): jnp.einsum('bqhd,bkhd->bhqk', grad_part, value_rows, preferred_element_ty...  51.3 us
    dot_general x8, matrix products, head_step(): jnp.einsum('bhqk,bkhd->bqhd', dscores, key_rows, preferred_element_type=j...  50.5 us
    while x7, local copies, waits for them, and re-layouts, attend(): return lax.fori_loop(0, head_count // paired, head_step, initial)  44.9 us
  transfers between devices with their start and end apart: 20, of which 8 were waited for; matrix products, arithmetic and copies ran while one was open for 17% of the time, Pallas kernels for 0%

commit v1 on v0

v1 whole, which is shorter than its diff:
```python
import math

import jax
import jax.numpy as jnp
from jax import lax
from jax.experimental import pallas as pl
from jax.experimental.pallas import tpu as pltpu
from jax.sharding import PartitionSpec as P

HEAD_DIM = 64
BLOCK = 256
HALF = 128
PAIR = 128
AXES = ("seqa", "seqb")
GROUPS = (2, 2, 2, 2)
LOG2E = math.log2(math.e)
BF16 = jnp.bfloat16
F32 = jnp.float32
NT = (((1,), (1,)), ((), ()))
NN = (((1,), (0,)), ((), ()))

BASE = (0, 1536, 2560, 3072)
ROWS = 3456

TILES = (
    (0, 0, 256, 1024, 0, 1),
    (0, 256, 256, 512, 0, 2),
    (0, 512, 256, 0, 0, 3),
    (0, 768, 256, 0, 1, 3),
    (0, 1024, 256, 0, 2, 2),
    (0, 1280, 256, 0, 3, 1),
    (1, 0, 128, 512, 1, 1),
    (1, 128, 256, 0, 0, 2),
    (1, 384, 128, 0, 0, 1),
    (1, 512, 128, 512, 3, 1),
    (1, 640, 256, 0, 2, 2),
    (1, 896, 128, 0, 2, 1),
    (2, 0, 128, 0, 0, 2),
    (2, 128, 256, 0, 0, 4),
    (2, 384, 128, 1024, 2, 2),
    (3, 0, 384, 0, 0, 4),
)


def pieces(b, h):
    at = h * 256
    low = (b // 2) * 512 + (1 - b % 2) * 128
    return (
        (0, b * 256, 256, 1024 + at),
        (0, b * 256 + 256, 256, 512 + at),
        (0, b * 256 + 512, 256, at),
        (1, low, 384, (b % 2) * 512 + at),
        (2, (b // 2) * 128, 384, b * 512 + at),
        (3, 0, 384, b * 512 + at),
    )


def dot(a, b, dims=NN):
    return lax.dot_general(a, b, dims, preferred_element_type=F32)


def mean_rows(ref, start, count, stride):
    total = ref[pl.ds(start, count, stride=stride), :]
    for i in range(1, stride):
        total = total + ref[pl.ds(start + i, count, stride=stride), :]
    return total * (1.0 / stride)


def spread_rows(ref, start, rows, stride):
    for i in range(stride):
        at = pl.ds(start + i, rows.shape[0], stride=stride)
        ref[at, :] = ref[at, :] + rows


def attend_kernel(
    valid, q, k, v, do, lk, lv, uk, uv, fk, fv,
    o, dq, gk, gv, glk, glv, guk, guv, gfk, gfv,
    kext, vext, kt, vt, e0, e1, e2, e3, x0, x1, x2, x3,
    qz, doz, qs, dos, inn, rls, ftmp, gtmp, flag,
):
    es = (e0, e1, e2, e3)
    xs = (x0, x1, x2, x3)
    lane = lax.broadcasted_iota(jnp.int32, (256, PAIR), 1)
    first = lane < HEAD_DIM

    for own, low, up, far, ext in ((k, lk, uk, fk, kext), (v, lv, uv, fv, vext)):
        ext[0:256] = low[0:256]
        ext[256:1280] = own[...]
        ext[1280:1536] = up[0:256]
        ftmp[0:1024] = own[...].astype(F32)
        spans = mean_rows(ftmp, 0, 512, 2).astype(BF16)
        b1 = BASE[1]
        ext[b1 + 256 : b1 + 384] = spans[384:512]
        ext[b1 + 384 : b1 + 512] = spans[256:384]
        ext[b1 + 512 : b1 + 640] = spans[128:256]
        ext[b1 + 640 : b1 + 768] = spans[0:128]
        ext[b1 + 128 : b1 + 256] = low[256:384]
        ext[b1 + 768 : b1 + 896] = up[256:384]
        b2 = BASE[2]
        ftmp[0:384] = low[0:384].astype(F32)
        ext[b1 : b1 + 128] = mean_rows(ftmp, 0, 128, 2).astype(BF16)
        ext[b2 + 384 : b2 + 448] = mean_rows(ftmp, 256, 64, 2).astype(BF16)
        ext[b2 + 448 : b2 + 512] = mean_rows(ftmp, 0, 64, 4).astype(BF16)
        ftmp[0:384] = up[0:384].astype(F32)
        ext[b1 + 896 : b1 + 1024] = mean_rows(ftmp, 0, 128, 2).astype(BF16)
        ext[b2 : b2 + 64] = mean_rows(ftmp, 0, 64, 4).astype(BF16)
        ext[b2 + 64 : b2 + 128] = mean_rows(ftmp, 256, 64, 2).astype(BF16)
        ext[b2 + 128 : b2 + 256] = low[384:512]
        ext[b2 + 256 : b2 + 384] = up[384:512]
        ext[BASE[3] : ROWS] = far[...]

    low_ok, up_ok = valid[0], valid[1]
    for level, row, rows, ok in (
        (0, 0, 256, low_ok), (0, 256, 1024, 1.0), (0, 1280, 256, up_ok),
        (1, 0, 256, low_ok), (1, 256, 512, 1.0), (1, 768, 256, up_ok),
        (2, 0, 128, up_ok), (2, 128, 128, low_ok), (2, 256, 128, up_ok), (2, 384, 128, low_ok),
        (3, 0, 128, valid[2]), (3, 128, 128, valid[3]), (3, 256, 128, valid[4]),
    ):
        at = slice(BASE[level] + row, BASE[level] + row + rows)
        scale = float(2**level)
        kt[:, at] = (kext[at] * scale).astype(BF16).T
        vals = (vext[at] * scale).astype(BF16).T
        top = lax.broadcasted_iota(jnp.int32, (16, rows), 0) == 0
        ones = jnp.where(top, ok * scale, 0.0).astype(BF16)
        for h in range(2):
            vt[h, 0:64, at] = vals[h * 64 : h * 64 + 64]
            vt[h, 64:80, at] = ones

    for b in range(4):
        at = slice(b * 256, b * 256 + 256)
        for h in range(2):
            to = slice((b * 2 + h) * 256, (b * 2 + h) * 256 + 256)
            mine = first if h == 0 else ~first
            qz[to] = jnp.where(mine, q[at].astype(F32) * 0.125, 0.0).astype(BF16)
            doz[to] = jnp.where(mine, do[at].astype(F32), 0.0).astype(BF16)

    for level, row, rows, col, b, nb in TILES:
        keys = kext[BASE[level] + row : BASE[level] + row + rows]
        for i in range(nb * 2):
            s = dot(keys, qz[(b * 2 + i) * 256 : (b * 2 + i) * 256 + 256], NT)
            es[level][row : row + rows, col + i * 256 : col + i * 256 + 256] = jnp.exp2(
                s * LOG2E
            ).astype(BF16)

    def finish_forward():
        least = jnp.full((1, 256), jnp.inf, F32)
        most = jnp.zeros((1, 256), F32)
        for b in range(4):
            at = slice(b * 256, b * 256 + 256)
            outs, recips = [], []
            for h in range(2):
                acc = jnp.zeros((80, 256), F32)
                for level, row, rows, col in pieces(b, h):
                    acc = acc + dot(
                        vt[h, :, BASE[level] + row : BASE[level] + row + rows],
                        es[level][row : row + rows, col : col + 256],
                    )
                total = acc[64:65]
                least = jnp.minimum(least, total)
                most = jnp.maximum(most, total)
                recip = 1.0 / total
                outs.append(acc[0:64] * recip)
                recips.append(recip)
                to = slice((b * 2 + h) * 256, (b * 2 + h) * 256 + 256)
                rls[0:1, to] = recip
            mixed = jnp.concatenate(outs, 0)
            o[at] = mixed.T.astype(BF16)
            prod = mixed.astype(BF16).astype(F32) * do[at].astype(F32).T
            wide = jnp.concatenate([jnp.broadcast_to(r, (64, 256)) for r in recips], 0).T
            for h in range(2):
                to = slice((b * 2 + h) * 256, (b * 2 + h) * 256 + 256)
                inn[0:1, to] = jnp.sum(prod[h * 64 : h * 64 + 64], axis=0, keepdims=True)
                mine = first if h == 0 else ~first
                dos[to] = jnp.where(mine, do[at].astype(F32) * wide, 0.0).astype(BF16)
                qs[to] = jnp.where(mine, q[at].astype(F32) * (wide * 0.125), 0.0).astype(BF16)
        fine = (jnp.min(least) > 2.0**-60) & (jnp.max(most) < 2.0**60)
        flag[0] = jnp.where(fine, 0, 1)

    finish_forward()

    @pl.when(flag[0] == 1)
    def _():
        oks = {
            0: (low_ok, 1.0, 1.0, 1.0, 1.0, up_ok),
            1: (low_ok, low_ok, 1.0, 1.0, 1.0, 1.0, up_ok, up_ok),
            2: (up_ok, low_ok, up_ok, low_ok),
            3: (valid[2], valid[3], valid[4]),
        }
        for b in range(4):
            for h in range(2):
                query = qz[(b * 2 + h) * 256 : (b * 2 + h) * 256 + 256]

                def scores(level, row, rows):
                    return dot(
                        kext[BASE[level] + row : BASE[level] + row + rows], query, NT
                    ) * LOG2E

                parts = []
                for level, row, rows, col in pieces(b, h):
                    step = 256 if level == 0 else 128
                    for r in range(row, row + rows, step):
                        parts.append((level, r, step, col, oks[level][r // step]))
                highest = jnp.full((1, 256), -jnp.inf, F32)
                for level, row, rows, col, ok in parts:
                    top = jnp.max(scores(level, row, rows), axis=0, keepdims=True)
                    highest = jnp.maximum(highest, jnp.where(ok > 0.5, top, -jnp.inf))
                for level, row, rows, col, ok in parts:
                    s = jnp.where(ok > 0.5, scores(level, row, rows) - highest, -200.0)
                    es[level][row : row + rows, col : col + 256] = jnp.exp2(s).astype(BF16)
        finish_forward()

    for level, row, rows, col, b, nb in TILES:
        vals = vext[BASE[level] + row : BASE[level] + row + rows]
        for i in range(nb * 2):
            to = slice((b * 2 + i) * 256, (b * 2 + i) * 256 + 256)
            at = (slice(row, row + rows), slice(col + i * 256, col + i * 256 + 256))
            dp = dot(vals, doz[to], NT) - inn[0:1, to]
            xs[level][at] = es[level][at] * dp.astype(BF16)

    for b in range(4):
        outs = []
        for h in range(2):
            acc = jnp.zeros((64, 256), F32)
            for level, row, rows, col in pieces(b, h):
                acc = acc + dot(
                    kt[h * 64 : h * 64 + 64, BASE[level] + row : BASE[level] + row + rows],
                    xs[level][row : row + rows, col : col + 256],
                )
            to = slice((b * 2 + h) * 256, (b * 2 + h) * 256 + 256)
            outs.append(acc * (rls[0:1, to] * 0.125))
        dq[b * 256 : b * 256 + 256] = jnp.concatenate(outs, 0).T.astype(BF16)

    for ws, right, own, low, up, far in (
        (xs, qs, gk, glk, guk, gfk), (es, dos, gv, glv, guv, gfv)
    ):
        got = {}
        for level, row, rows, col, b, nb in TILES:
            got[level, row] = dot(
                ws[level][row : row + rows, col : col + nb * 512],
                right[b * 512 : (b + nb) * 512],
            )
            if level == 0 and 0 < row < 1280:
                own[row - 256 : row] = got[level, row]
            elif level == 0:
                gtmp[0 if row == 0 else 384 : 256 if row == 0 else 640] = got[level, row]
            elif level == 1:
                g = got[level, row]
                if row == 0:
                    spread_rows(gtmp, 0, g, 2)
                elif row == 128:
                    gtmp[256:384] = g[0:128]
                    spread_rows(own, 768, g[128:256], 2)
                elif row == 384:
                    spread_rows(own, 512, g, 2)
                elif row == 512:
                    spread_rows(own, 256, g, 2)
                elif row == 640:
                    spread_rows(own, 0, g[0:128], 2)
                    gtmp[640:768] = g[128:256]
                else:
                    spread_rows(gtmp, 384, g, 2)
            elif level == 2:
                g = got[level, row]
                if row == 0:
                    spread_rows(gtmp, 384, g[0:64], 4)
                    spread_rows(gtmp, 640, g[64:128], 2)
                elif row == 128:
                    low[384:512] = g[0:128].astype(BF16)
                    up[384:512] = g[128:256].astype(BF16)
                else:
                    spread_rows(gtmp, 256, g[0:64], 2)
                    spread_rows(gtmp, 0, g[64:128], 4)
            else:
                far[...] = got[level, row].astype(BF16)
        low[0:384] = gtmp[0:384].astype(BF16)
        up[0:384] = gtmp[384:768].astype(BF16)


def moved(array, pairs):
    return lax.ppermute(array, AXES, pairs)


def shape(*dims, dtype=BF16):
    return jax.ShapeDtypeStruct(dims, dtype)


def vmem(limit):
    return pltpu.CompilerParams(vmem_limit_bytes=limit * 2**20)


def send(keys, values, start, pairs):
    col = start
    block = pl.BlockSpec((1024, PAIR), lambda j: (0, col + j))

    def body(k, v, up, down, far, tmp):
        for own, side in ((k, 0), (v, 1)):
            tmp[...] = own[...].astype(F32)
            up[side, 0:256] = own[768:1024]
            up[side, 256:384] = mean_rows(tmp, 512, 128, 2).astype(BF16)
            up[side, 384:512] = mean_rows(tmp, 0, 128, 4).astype(BF16)
            down[side, 0:256] = own[0:256]
            down[side, 256:384] = mean_rows(tmp, 256, 128, 2).astype(BF16)
            down[side, 384:512] = mean_rows(tmp, 512, 128, 4).astype(BF16)
            far[side] = mean_rows(tmp, 0, 128, 8).astype(BF16)

    side = lambda rows: pl.BlockSpec((2, rows, PAIR), lambda j: (0, 0, j))
    width = pairs * PAIR
    return pl.pallas_call(
        body,
        grid=(pairs,),
        in_specs=[block, block],
        out_specs=[side(512), side(512), side(128)],
        out_shape=[shape(2, 512, width), shape(2, 512, width), shape(2, 128, width)],
        scratch_shapes=[pltpu.VMEM((1024, PAIR), F32)],
        compiler_params=vmem(32),
        name="rows_to_send",
    )(keys, values)


def attend(valid, queries, keys, values, grad_out, low, up, far, start, pairs):
    whole = pl.BlockSpec((1024, PAIR), lambda j: (0, start + j))
    mine = pl.BlockSpec((1024, PAIR), lambda j: (0, j))

    def side(rows, which):
        return pl.BlockSpec((None, rows, PAIR), lambda j: (which, 0, j))

    width = pairs * PAIR

    def body(*refs):
        ins = refs[:11]
        o, dq, gk, gv, gl, gu, gf = refs[11:18]
        attend_kernel(
            *ins, o, dq, gk, gv,
            gl.at[0], gl.at[1], gu.at[0], gu.at[1], gf.at[0], gf.at[1], *refs[18:],
        )

    both = lambda rows: pl.BlockSpec((2, rows, PAIR), lambda j: (0, 0, j))
    return pl.pallas_call(
        body,
        grid=(pairs,),
        in_specs=[pl.BlockSpec(memory_space=pltpu.SMEM), whole, whole, whole, whole]
        + [side(rows, which) for rows in (512, 512, 384) for which in (0, 1)],
        out_specs=[mine, mine, mine, mine, both(512), both(512), both(384)],
        out_shape=[
            shape(1024, width), shape(1024, width),
            shape(1024, width, dtype=F32), shape(1024, width, dtype=F32),
            shape(2, 512, width), shape(2, 512, width), shape(2, 384, width),
        ],
        scratch_shapes=[
            pltpu.VMEM((ROWS, PAIR), BF16), pltpu.VMEM((ROWS, PAIR), BF16),
            pltpu.VMEM((PAIR, ROWS), BF16), pltpu.VMEM((2, 80, ROWS), BF16),
        ]
        + [
            pltpu.VMEM(dims, BF16)
            for dims in ((1536, 1536), (1024, 1024), (512, 2048), (384, 2048)) * 2
        ]
        + [pltpu.VMEM((2048, PAIR), BF16)] * 4
        + [
            pltpu.VMEM((8, 2048), F32), pltpu.VMEM((8, 2048), F32),
            pltpu.VMEM((1024, PAIR), F32), pltpu.VMEM((768, PAIR), F32),
            pltpu.SMEM((1,), jnp.int32),
        ],
        compiler_params=vmem(56),
        cost_estimate=pl.CostEstimate(
            flops=pairs * 14 * 10**9, bytes_accessed=pairs * 4 * 10**6, transcendentals=0
        ),
        name="attend_pairs",
    )(valid, queries, keys, values, grad_out, low, low, up, up, far, far)


def finish(own_k, own_v, above, below, far, pairs):
    mine = pl.BlockSpec((1024, PAIR), lambda j: (0, j))
    both = lambda rows: pl.BlockSpec((2, rows, PAIR), lambda j: (0, 0, j))

    def body(gk, gv, above, below, f0, f1, f2, dk, dv, tmp):
        for side, own, out in ((0, gk, dk), (1, gv, dv)):
            tmp[...] = own[...]
            tmp[768:1024] = tmp[768:1024] + above[side, 0:256].astype(F32)
            spread_rows(tmp, 512, above[side, 256:384].astype(F32), 2)
            spread_rows(tmp, 0, above[side, 384:512].astype(F32), 4)
            tmp[0:256] = tmp[0:256] + below[side, 0:256].astype(F32)
            spread_rows(tmp, 256, below[side, 256:384].astype(F32), 2)
            spread_rows(tmp, 512, below[side, 384:512].astype(F32), 4)
            total = f0[side].astype(F32) + f1[side].astype(F32) + f2[side].astype(F32)
            spread_rows(tmp, 0, total, 8)
            out[...] = tmp[...].astype(BF16)

    width = pairs * PAIR
    return pl.pallas_call(
        body,
        grid=(pairs,),
        in_specs=[mine, mine, both(512), both(512), both(128), both(128), both(128)],
        out_specs=[mine, mine],
        out_shape=[shape(1024, width), shape(1024, width)],
        scratch_shapes=[pltpu.VMEM((1024, PAIR), F32)],
        compiler_params=vmem(32),
        name="sum_grads",
    )(own_k, own_v, above, below, *far)


def local(queries, keys, values, grad_out):
    index = lax.axis_index(AXES)
    count = lax.axis_size(AXES)

    def by(step):
        return [(i, i + step) for i in range(count) if 0 <= i + step < count]

    three = [
        (i, i + (3 if i % 2 == 0 else -3))
        for i in range(count)
        if 0 <= i + (3 if i % 2 == 0 else -3) < count
    ]
    third = jnp.where(index % 2 == 0, index + 3, index - 3)
    valid = jnp.stack(
        [
            index > 0,
            index < count - 1,
            index >= 2,
            index < count - 2,
            (third >= 0) & (third < count),
        ]
    ).astype(F32)

    halos = []
    start = 0
    for pairs in GROUPS:
        up, down, far = send(keys, values, start, pairs)
        low = moved(up, by(1))
        high = moved(down, by(-1))
        spans = jnp.concatenate(
            [moved(far, by(2)), moved(far, by(-2)), moved(far, three)], axis=1
        )
        halos.append((start, pairs, low, high, spans))
        start += pairs

    results = []
    for start, pairs, low, high, spans in halos:
        o, dq, gk, gv, gl, gu, gf = attend(
            valid, queries, keys, values, grad_out, low, high, spans, start, pairs
        )
        above = moved(gl, by(-1))
        below = moved(gu, by(1))
        far = (
            moved(gf[:, 0:128], by(-2)),
            moved(gf[:, 128:256], by(2)),
            moved(gf[:, 256:384], [(b, a) for a, b in three]),
        )
        dk, dv = finish(gk, gv, above, below, far, pairs)
        results.append((o, dq, dk, dv))
    return tuple(jnp.concatenate(parts, axis=1) if len(parts) > 1 else parts[0]
                 for parts in zip(*results))


def solution(mesh):
    placed = P(AXES, None)
    return jax.shard_map(
        local,
        mesh=mesh,
        in_specs=(placed,) * 4,
        out_specs=(placed,) * 4,
        check_vma=False,
    )
```

time: 1140 us -> 393 us (0.34); the launches traced: 1120 us -> 386 us
  local copies, waits for them, and re-layouts: 379 us -> 10.4 us
  matrix products: 261 us -> 0 us
  Pallas kernels: 0 us -> 196 us
  waiting for transfers between devices: 188 us -> 0.11 us
  other arithmetic: 162 us -> 11.5 us
  starting transfers between devices: 115 us -> 166 us
    pallas_call x0 -> x12, Pallas kernels: none -> 196 us  [the longest x4 183 us: attend(): pl.pallas_call(body, grid=(pairs,), in_specs=[pl.BlockSpec(memory_space=p...]
    ppermute x20 -> x40, waiting for transfers between devices: 188 us -> 0.11 us  [moved(): return lax.ppermute(array, AXES, pairs)]
    dot_general x40 -> x0, matrix products: 185 us -> none  [the longest x8 51.3 us: head_step(): jnp.einsum('bqhd,bkhd->bhqk', grad_part, value_rows, preferred_element_ty...]
    while x271 -> x0, local copies, waits for them, and re-layouts: 129 us -> none
    sub x8 -> x0, matrix products: 75.1 us -> none  [head_step(): weights = jnp.exp(scores - highest)]
    dynamic_update_slice x104 -> x0, local copies, waits for them, and re-layouts: 68.8 us -> none  [the longest x32 26 us: head_step(): lax.dynamic_update_slice_in_dim(total_rows, value_total, features + colum...]
    convert_element_type x11 -> x1, other arithmetic: 67.8 us -> 0.49 us  [local(): valid = jnp.stack([index > 0, index < count - 1, index >= 2, index < coun...]
    ppermute x20 -> x40, starting transfers between devices: 115 us -> 166 us  [moved(): return lax.ppermute(array, AXES, pairs)]
  transfers between devices with their start and end apart: 20 -> 40, of which waited for: 8 -> 0; matrix products, arithmetic and copies ran while one was open for 17% -> 3% of each run, Pallas kernels for 0% -> 50%
where the time goes in v1:
time: 393 us; the launch traced here: 386 us
  Pallas kernels  196 us (50%)
  starting transfers between devices  166 us (42%)
  other arithmetic  11.5 us (3%)
  local copies, waits for them, and re-layouts  10.4 us (3%)
    pallas_call x4, Pallas kernels, attend(): pl.pallas_call(body, grid=(pairs,), in_specs=[pl.BlockSpec(memory_space=p...  183 us
    ppermute x40, starting transfers between devices, moved(): return lax.ppermute(array, AXES, pairs)  166 us
    unnamed x70, local copies, waits for them, and re-layouts  8.07 us
  transfers between devices with their start and end apart: 40, of which 0 were waited for; matrix products, arithmetic and copies ran while one was open for 3% of the time, Pallas kernels for 50%

profile of v1, /device:TPU:36, one launch (start us, length us, event | category | flops | bytes accessed | tf_op | source)
XLA Modules:
  0.0 385.5 jit_solution(15275206841429977167)
XLA Ops:
  5.5 3.5 collective-permute-start.2
  9.0 6.6 %collective-permute-start.3 = (bf16[2,128,256]{2,1,0:T(8,128)(2,1)S(1)}, bf16[2,128,256]{2,1,0:T(8,128)(2,1)}, u32[]{:S(2)}, u32[]{:S(2)}) collective-permute-start(bf16[2,128,256]{2,1,0:T(8,128)(2,1)S(1)} %get-tuple-element.54), channel_id=1, source_target_pairs={{2,0},{3,1},{4,2},{5,3},{6,4},{7,5},{8,6},{9,7},{10,8},{11,9},{12,... | collective-permute-start | bytes 393224 | tf_op jit(solution)/shard_map/ppermute | solution.py:280
  15.6 1.9 collective-permute-start.4
  17.5 1.9 collective-permute-start
  19.5 4.1 %collective-permute-start.1 = (bf16[2,512,256]{2,1,0:T(8,128)(2,1)}, bf16[2,512,256]{2,1,0:T(8,128)(2,1)}, u32[]{:S(2)}, u32[]{:S(2)}) collective-permute-start(bf16[2,512,256]{2,1,0:T(8,128)(2,1)} %get-tuple-element.53), channel_id=1, source_target_pairs={{1,0},{2,1},{3,2},{4,3},{5,4},{6,5},{7,6},{8,7},{9,8},{10,9},{11,1... | collective-permute-start | bytes 1572872 | tf_op jit(solution)/shard_map/ppermute | solution.py:280
  26.3 3.5 collective-permute-start.7
  29.8 6.6 %collective-permute-start.8 = (bf16[2,128,256]{2,1,0:T(8,128)(2,1)S(1)}, bf16[2,128,256]{2,1,0:T(8,128)(2,1)}, u32[]{:S(2)}, u32[]{:S(2)}) collective-permute-start(bf16[2,128,256]{2,1,0:T(8,128)(2,1)S(1)} %get-tuple-element.58), channel_id=1, source_target_pairs={{2,0},{3,1},{4,2},{5,3},{6,4},{7,5},{8,6},{9,7},{10,8},{11,9},{12,... | collective-permute-start | bytes 393224 | tf_op jit(solution)/shard_map/ppermute | solution.py:280
  36.4 3.9 %collective-permute-start.9 = (bf16[2,128,256]{2,1,0:T(8,128)(2,1)S(1)}, bf16[2,128,256]{2,1,0:T(8,128)(2,1)}, u32[]{:S(2)}, u32[]{:S(2)}) collective-permute-start(bf16[2,128,256]{2,1,0:T(8,128)(2,1)S(1)} %get-tuple-element.58), channel_id=1, source_target_pairs={{0,3},{2,5},{3,0},{4,7},{5,2},{6,9},{7,4},{8,11},{9,6},{10,13},{11... | collective-permute-start | bytes 393224 | tf_op jit(solution)/shard_map/ppermute | solution.py:280
  46.5 5.4 %collective-permute-start.12 = (bf16[2,128,256]{2,1,0:T(8,128)(2,1)S(1)}, bf16[2,128,256]{2,1,0:T(8,128)(2,1)S(1)}, u32[]{:S(2)}, u32[]{:S(2)}) collective-permute-start(bf16[2,128,256]{2,1,0:T(8,128)(2,1)S(1)} %get-tuple-element.62), channel_id=1, source_target_pairs={{0,2},{1,3},{2,4},{3,5},{4,6},{5,7},{6,8},{7,9},{8,10},{9,11},{10,... | collective-permute-start | bytes 393224 | tf_op jit(solution)/shard_map/ppermute | solution.py:280
  51.9 4.6 %collective-permute-start.13 = (bf16[2,128,256]{2,1,0:T(8,128)(2,1)S(1)}, bf16[2,128,256]{2,1,0:T(8,128)(2,1)S(1)}, u32[]{:S(2)}, u32[]{:S(2)}) collective-permute-start(bf16[2,128,256]{2,1,0:T(8,128)(2,1)S(1)} %get-tuple-element.62), channel_id=1, source_target_pairs={{2,0},{3,1},{4,2},{5,3},{6,4},{7,5},{8,6},{9,7},{10,8},{11,9},{12,... | collective-permute-start | bytes 393224 | tf_op jit(solution)/shard_map/ppermute | solution.py:280
  56.6 1.9 collective-permute-start.14
  62.2 5.4 %collective-permute-start.17 = (bf16[2,128,256]{2,1,0:T(8,128)(2,1)S(1)}, bf16[2,128,256]{2,1,0:T(8,128)(2,1)S(1)}, u32[]{:S(2)}, u32[]{:S(2)}) collective-permute-start(bf16[2,128,256]{2,1,0:T(8,128)(2,1)S(1)} %get-tuple-element.66), channel_id=1, source_target_pairs={{0,2},{1,3},{2,4},{3,5},{4,6},{5,7},{6,8},{7,9},{8,10},{9,11},{10,... | collective-permute-start | bytes 393224 | tf_op jit(solution)/shard_map/ppermute | solution.py:280
  67.6 4.6 %collective-permute-start.18 = (bf16[2,128,256]{2,1,0:T(8,128)(2,1)S(1)}, bf16[2,128,256]{2,1,0:T(8,128)(2,1)S(1)}, u32[]{:S(2)}, u32[]{:S(2)}) collective-permute-start(bf16[2,128,256]{2,1,0:T(8,128)(2,1)S(1)} %get-tuple-element.66), channel_id=1, source_target_pairs={{2,0},{3,1},{4,2},{5,3},{6,4},{7,5},{8,6},{9,7},{10,8},{11,9},{12,... | collective-permute-start | bytes 393224 | tf_op jit(solution)/shard_map/ppermute | solution.py:280
  72.3 1.9 collective-permute-start.19
  75.0 2.1 collective-permute-start.5
  77.1 3.9 %collective-permute-start.6 = (bf16[2,512,256]{2,1,0:T(8,128)(2,1)S(1)}, bf16[2,512,256]{2,1,0:T(8,128)(2,1)S(1)}, u32[]{:S(2)}, u32[]{:S(2)}) collective-permute-start(bf16[2,512,256]{2,1,0:T(8,128)(2,1)S(1)} %copy-done.13), channel_id=1, source_target_pairs={{1,0},{2,1},{3,2},{4,3},{5,4},{6,5},{7,6},{8,7},{9,8},{10,9},{11,1... | collective-permute-start | bytes 1572872 | tf_op jit(solution)/shard_map/ppermute | solution.py:280
  81.1 39.4 %attend_pairs.4 = (bf16[1024,256]{1,0:T(8,128)(2,1)}, bf16[1024,256]{1,0:T(8,128)(2,1)}, f32[1024,256]{1,0:T(8,128)}, f32[1024,256]{1,0:T(8,128)}, bf16[2,512,25...) custom-call(f32[5]{0:T(128)} %convert_element_type.3.refs_0_, ...), custom_call_target="tpu_custom_call" | custom-call | flops 28000000000 | bytes 8000000 | tf_op jit(solution)/shard_map/attend_pairs/pallas_call | solution.py:338
  120.5 4.8 %collective-permute-start.10 = (bf16[2,512,256]{2,1,0:T(8,128)(2,1)S(1)}, bf16[2,512,256]{2,1,0:T(8,128)(2,1)S(1)}, u32[]{:S(2)}, u32[]{:S(2)}) collective-permute-start(bf16[2,512,256]{2,1,0:T(8,128)(2,1)S(1)} %copy-done.19), channel_id=1, source_target_pairs={{0,1},{1,2},{2,3},{3,4},{4,5},{5,6},{6,7},{7,8},{8,9},{9,10},{10,1... | collective-permute-start | bytes 1572872 | tf_op jit(solution)/shard_map/ppermute | solution.py:280
  125.3 4.9 %collective-permute-start.11 = (bf16[2,512,256]{2,1,0:T(8,128)(2,1)S(1)}, bf16[2,512,256]{2,1,0:T(8,128)(2,1)S(1)}, u32[]{:S(2)}, u32[]{:S(2)}) collective-permute-start(bf16[2,512,256]{2,1,0:T(8,128)(2,1)S(1)} %copy-done.17), channel_id=1, source_target_pairs={{1,0},{2,1},{3,2},{4,3},{5,4},{6,5},{7,6},{8,7},{9,8},{10,9},{11,1... | collective-permute-start | bytes 1572872 | tf_op jit(solution)/shard_map/ppermute | solution.py:280
  130.3 39.6 %attend_pairs.5 = (bf16[1024,256]{1,0:T(8,128)(2,1)}, bf16[1024,256]{1,0:T(8,128)(2,1)}, f32[1024,256]{1,0:T(8,128)}, f32[1024,256]{1,0:T(8,128)}, bf16[2,512,25...) custom-call(f32[5]{0:T(128)} %convert_element_type.3.refs_0_, ...), custom_call_target="tpu_custom_call" | custom-call | flops 28000000000 | bytes 8000000 | tf_op jit(solution)/shard_map/attend_pairs/pallas_call | solution.py:338
  169.9 1.9 collective-permute-start.15
  171.9 8.0 %collective-permute-start.16 = (bf16[2,512,256]{2,1,0:T(8,128)(2,1)S(1)}, bf16[2,512,256]{2,1,0:T(8,128)(2,1)S(1)}, u32[]{:S(2)}, u32[]{:S(2)}) collective-permute-start(bf16[2,512,256]{2,1,0:T(8,128)(2,1)S(1)} %get-tuple-element.65), channel_id=1, source_target_pairs={{1,0},{2,1},{3,2},{4,3},{5,4},{6,5},{7,6},{8,7},{9,8},{10,9},{11,1... | collective-permute-start | bytes 1572872 | tf_op jit(solution)/shard_map/ppermute | solution.py:280
  179.9 52.5 %attend_pairs.6 = (bf16[1024,256]{1,0:T(8,128)(2,1)}, bf16[1024,256]{1,0:T(8,128)(2,1)}, f32[1024,256]{1,0:T(8,128)}, f32[1024,256]{1,0:T(8,128)}, bf16[2,512,25...) custom-call(f32[5]{0:T(128)} %convert_element_type.3.refs_0_, ...), custom_call_target="tpu_custom_call" | custom-call | flops 28000000000 | bytes 8000000 | tf_op jit(solution)/shard_map/attend_pairs/pallas_call | solution.py:338
  232.5 6.7 %collective-permute-start.22 = (bf16[2,128,256]{2,1,0:T(8,128)(2,1)S(1)}, bf16[2,128,256]{2,1,0:T(8,128)(2,1)S(1)}, u32[]{:S(2)}, u32[]{:S(2)}) collective-permute-start(bf16[2,128,256]{2,1,0:T(8,128)(2,1)S(1)} %get-tuple-element.102), channel_id=1, source_target_pairs={{2,0},{3,1},{4,2},{5,3},{6,4},{7,5},{8,6},{9,7},{10,8},{11,9},{12,... | collective-permute-start | bytes 393224 | tf_op jit(solution)/shard_map/ppermute | solution.py:280
  239.2 3.1 collective-permute-start.20
  242.3 3.9 %collective-permute-start.23 = (bf16[2,128,256]{2,1,0:T(8,128)(2,1)S(1)}, bf16[2,128,256]{2,1,0:T(8,128)(2,1)S(1)}, u32[]{:S(2)}, u32[]{:S(2)}) collective-permute-start(bf16[2,128,256]{2,1,0:T(8,128)(2,1)S(1)} %get-tuple-element.101), channel_id=1, source_target_pairs={{0,2},{1,3},{2,4},{3,5},{4,6},{5,7},{6,8},{7,9},{8,10},{9,11},{10,... | collective-permute-start | bytes 393224 | tf_op jit(solution)/shard_map/ppermute | solution.py:280
  246.3 4.1 %collective-permute-start.24 = (bf16[2,128,256]{2,1,0:T(8,128)(2,1)S(1)}, bf16[2,128,256]{2,1,0:T(8,128)(2,1)S(1)}, u32[]{:S(2)}, u32[]{:S(2)}) collective-permute-start(bf16[2,128,256]{2,1,0:T(8,128)(2,1)S(1)} %get-tuple-element.100), channel_id=1, source_target_pairs={{3,0},{5,2},{0,3},{7,4},{2,5},{9,6},{4,7},{11,8},{6,9},{13,10},{8,... | collective-permute-start | bytes 393224 | tf_op jit(solution)/shard_map/ppermute | solution.py:280
  250.4 4.0 %collective-permute-start.27 = (bf16[2,128,256]{2,1,0:T(8,128)(2,1)S(1)}, bf16[2,128,256]{2,1,0:T(8,128)(2,1)S(1)}, u32[]{:S(2)}, u32[]{:S(2)}) collective-permute-start(bf16[2,128,256]{2,1,0:T(8,128)(2,1)S(1)} %get-tuple-element.105), channel_id=1, source_target_pairs={{2,0},{3,1},{4,2},{5,3},{6,4},{7,5},{8,6},{9,7},{10,8},{11,9},{12,... | collective-permute-start | bytes 393224 | tf_op jit(solution)/shard_map/ppermute | solution.py:280
  254.4 1.9 collective-permute-start.28
  257.4 8.7 %collective-permute-start.29 = (bf16[2,128,256]{2,1,0:T(8,128)(2,1)S(1)}, bf16[2,128,256]{2,1,0:T(8,128)(2,1)S(1)}, u32[]{:S(2)}, u32[]{:S(2)}) collective-permute-start(bf16[2,128,256]{2,1,0:T(8,128)(2,1)S(1)} %get-tuple-element.103), channel_id=1, source_target_pairs={{3,0},{5,2},{0,3},{7,4},{2,5},{9,6},{4,7},{11,8},{6,9},{13,10},{8,... | collective-permute-start | bytes 393224 | tf_op jit(solution)/shard_map/ppermute | solution.py:280
  266.1 1.9 collective-permute-start.32
  268.0 3.9 %collective-permute-start.33 = (bf16[2,128,256]{2,1,0:T(8,128)(2,1)S(1)}, bf16[2,128,256]{2,1,0:T(8,128)(2,1)S(1)}, u32[]{:S(2)}, u32[]{:S(2)}) collective-permute-start(bf16[2,128,256]{2,1,0:T(8,128)(2,1)S(1)} %get-tuple-element.107), channel_id=1, source_target_pairs={{0,2},{1,3},{2,4},{3,5},{4,6},{5,7},{6,8},{7,9},{8,10},{9,11},{10,... | collective-permute-start | bytes 393224 | tf_op jit(solution)/shard_map/ppermute | solution.py:280
  272.0 6.2 %collective-permute-start.34 = (bf16[2,128,256]{2,1,0:T(8,128)(2,1)S(1)}, bf16[2,128,256]{2,1,0:T(8,128)(2,1)S(1)}, u32[]{:S(2)}, u32[]{:S(2)}) collective-permute-start(bf16[2,128,256]{2,1,0:T(8,128)(2,1)S(1)} %get-tuple-element.106), channel_id=1, source_target_pairs={{3,0},{5,2},{0,3},{7,4},{2,5},{9,6},{4,7},{11,8},{6,9},{13,10},{8,... | collective-permute-start | bytes 393224 | tf_op jit(solution)/shard_map/ppermute | solution.py:280
  278.9 1.9 collective-permute-start.21
  280.9 3.9 %collective-permute-start.25 = (bf16[2,512,256]{2,1,0:T(8,128)(2,1)}, bf16[2,512,256]{2,1,0:T(8,128)(2,1)S(1)}, u32[]{:S(2)}, u32[]{:S(2)}) collective-permute-start(bf16[2,512,256]{2,1,0:T(8,128)(2,1)} %get-tuple-element.80), channel_id=1, source_target_pairs={{1,0},{2,1},{3,2},{4,3},{5,4},{6,5},{7,6},{8,7},{9,8},{10,9},{11,1... | collective-permute-start | bytes 1572872 | tf_op jit(solution)/shard_map/ppermute | solution.py:280
  284.8 2.8 collective-permute-start.26
  287.6 3.0 collective-permute-start.30
  290.8 4.0 %collective-permute-start.31 = (bf16[2,512,256]{2,1,0:T(8,128)(2,1)}, bf16[2,512,256]{2,1,0:T(8,128)(2,1)S(1)}, u32[]{:S(2)}, u32[]{:S(2)}) collective-permute-start(bf16[2,512,256]{2,1,0:T(8,128)(2,1)} %get-tuple-element.87), channel_id=1, source_target_pairs={{0,1},{1,2},{2,3},{3,4},{4,5},{5,6},{6,7},{7,8},{8,9},{9,10},{10,1... | collective-permute-start | bytes 1572872 | tf_op jit(solution)/shard_map/ppermute | solution.py:280
  294.7 51.5 %attend_pairs.7 = (bf16[1024,256]{1,0:T(8,128)(2,1)}, bf16[1024,256]{1,0:T(8,128)(2,1)}, f32[1024,256]{1,0:T(8,128)}, f32[1024,256]{1,0:T(8,128)}, bf16[2,512,25...) custom-call(f32[5]{0:T(128)} %convert_element_type.3.refs_0_, ...), custom_call_target="tpu_custom_call" | custom-call | flops 28000000000 | bytes 8000000 | tf_op jit(solution)/shard_map/attend_pairs/pallas_call | solution.py:338
  346.3 5.2 %collective-permute-start.35 = (bf16[2,512,256]{2,1,0:T(8,128)(2,1)}, bf16[2,512,256]{2,1,0:T(8,128)(2,1)S(1)}, u32[]{:S(2)}, u32[]{:S(2)}) collective-permute-start(bf16[2,512,256]{2,1,0:T(8,128)(2,1)} %get-tuple-element.92), channel_id=1, source_target_pairs={{1,0},{2,1},{3,2},{4,3},{5,4},{6,5},{7,6},{8,7},{9,8},{10,9},{11,1... | collective-permute-start | bytes 1572872 | tf_op jit(solution)/shard_map/ppermute | solution.py:280
  351.5 1.9 collective-permute-start.36
  354.5 12.6 %collective-permute-start.37 = (bf16[2,128,256]{2,1,0:T(8,128)(2,1)S(1)}, bf16[2,128,256]{2,1,0:T(8,128)(2,1)S(1)}, u32[]{:S(2)}, u32[]{:S(2)}) collective-permute-start(bf16[2,128,256]{2,1,0:T(8,128)(2,1)S(1)} %get-tuple-element.111), channel_id=1, source_target_pairs={{2,0},{3,1},{4,2},{5,3},{6,4},{7,5},{8,6},{9,7},{10,8},{11,9},{12,... | collective-permute-start | bytes 393224 | tf_op jit(solution)/shard_map/ppermute | solution.py:280
  367.2 1.9 collective-permute-start.38
  369.1 2.5 collective-permute-start.39
  371.7 3.5 pad_maximum_fusion
  377.1 1.9 sum_grads.5
  379.1 1.9 sum_grads.6
  383.0 2.3 pad_maximum_fusion.2
  (126 shorter events, 25.2 us)
Async XLA Ops:
  5.5 20.8 %collective-permute-start.2 = (bf16[2,128,256]{2,1,0:T(8,128)(2,1)S(1)}, bf16[2,128,256]{2,1,0:T(8,128)(2,1)}, u32[]{:S(2)}, u32[]{:S(2)}) collective-permute-start(bf16[2,128,256]{2,1,0:T(8,128)(2,1)S(1)} %get-tuple-element.54), channel_id=1, source_target_pairs={{0,2},{1,3},{2,4},{3,5},{4,6},{5,7},{6,8},{7,9},{8,10},{9,11},{10,... | collective-permute-start | bytes 393224 | tf_op jit(solution)/shard_map/ppermute | solution.py:280
  9.0 20.8 %collective-permute-start.3 = (bf16[2,128,256]{2,1,0:T(8,128)(2,1)S(1)}, bf16[2,128,256]{2,1,0:T(8,128)(2,1)}, u32[]{:S(2)}, u32[]{:S(2)}) collective-permute-start(bf16[2,128,256]{2,1,0:T(8,128)(2,1)S(1)} %get-tuple-element.54), channel_id=1, source_target_pairs={{2,0},{3,1},{4,2},{5,3},{6,4},{7,5},{8,6},{9,7},{10,8},{11,9},{12,... | collective-permute-start | bytes 393224 | tf_op jit(solution)/shard_map/ppermute | solution.py:280
  15.6 20.8 %collective-permute-start.4 = (bf16[2,128,256]{2,1,0:T(8,128)(2,1)S(1)}, bf16[2,128,256]{2,1,0:T(8,128)(2,1)}, u32[]{:S(2)}, u32[]{:S(2)}) collective-permute-start(bf16[2,128,256]{2,1,0:T(8,128)(2,1)S(1)} %get-tuple-element.54), channel_id=1, source_target_pairs={{0,3},{2,5},{3,0},{4,7},{5,2},{6,9},{7,4},{8,11},{9,6},{10,13},{11... | collective-permute-start | bytes 393224 | tf_op jit(solution)/shard_map/ppermute | solution.py:280
  17.5 57.5 %collective-permute-start = (bf16[2,512,256]{2,1,0:T(8,128)(2,1)}, bf16[2,512,256]{2,1,0:T(8,128)(2,1)}, u32[]{:S(2)}, u32[]{:S(2)}) collective-permute-start(bf16[2,512,256]{2,1,0:T(8,128)(2,1)} %get-tuple-element.52), channel_id=1, source_target_pairs={{0,1},{1,2},{2,3},{3,4},{4,5},{5,6},{6,7},{7,8},{8,9},{9,10},{10,1... | collective-permute-start | bytes 1572872 | tf_op jit(solution)/shard_map/ppermute | solution.py:280
  19.5 57.6 %collective-permute-start.1 = (bf16[2,512,256]{2,1,0:T(8,128)(2,1)}, bf16[2,512,256]{2,1,0:T(8,128)(2,1)}, u32[]{:S(2)}, u32[]{:S(2)}) collective-permute-start(bf16[2,512,256]{2,1,0:T(8,128)(2,1)} %get-tuple-element.53), channel_id=1, source_target_pairs={{1,0},{2,1},{3,2},{4,3},{5,4},{6,5},{7,6},{8,7},{9,8},{10,9},{11,1... | collective-permute-start | bytes 1572872 | tf_op jit(solution)/shard_map/ppermute | solution.py:280
  26.3 20.2 %collective-permute-start.7 = (bf16[2,128,256]{2,1,0:T(8,128)(2,1)S(1)}, bf16[2,128,256]{2,1,0:T(8,128)(2,1)}, u32[]{:S(2)}, u32[]{:S(2)}) collective-permute-start(bf16[2,128,256]{2,1,0:T(8,128)(2,1)S(1)} %get-tuple-element.58), channel_id=1, source_target_pairs={{0,2},{1,3},{2,4},{3,5},{4,6},{5,7},{6,8},{7,9},{8,10},{9,11},{10,... | collective-permute-start | bytes 393224 | tf_op jit(solution)/shard_map/ppermute | solution.py:280
  29.8 22.1 %collective-permute-start.8 = (bf16[2,128,256]{2,1,0:T(8,128)(2,1)S(1)}, bf16[2,128,256]{2,1,0:T(8,128)(2,1)}, u32[]{:S(2)}, u32[]{:S(2)}) collective-permute-start(bf16[2,128,256]{2,1,0:T(8,128)(2,1)S(1)} %get-tuple-element.58), channel_id=1, source_target_pairs={{2,0},{3,1},{4,2},{5,3},{6,4},{7,5},{8,6},{9,7},{10,8},{11,9},{12,... | collective-permute-start | bytes 393224 | tf_op jit(solution)/shard_map/ppermute | solution.py:280
  36.4 20.2 %collective-permute-start.9 = (bf16[2,128,256]{2,1,0:T(8,128)(2,1)S(1)}, bf16[2,128,256]{2,1,0:T(8,128)(2,1)}, u32[]{:S(2)}, u32[]{:S(2)}) collective-permute-start(bf16[2,128,256]{2,1,0:T(8,128)(2,1)S(1)} %get-tuple-element.58), channel_id=1, source_target_pairs={{0,3},{2,5},{3,0},{4,7},{5,2},{6,9},{7,4},{8,11},{9,6},{10,13},{11... | collective-permute-start | bytes 393224 | tf_op jit(solution)/shard_map/ppermute | solution.py:280
  46.5 15.7 %collective-permute-start.12 = (bf16[2,128,256]{2,1,0:T(8,128)(2,1)S(1)}, bf16[2,128,256]{2,1,0:T(8,128)(2,1)S(1)}, u32[]{:S(2)}, u32[]{:S(2)}) collective-permute-start(bf16[2,128,256]{2,1,0:T(8,128)(2,1)S(1)} %get-tuple-element.62), channel_id=1, source_target_pairs={{0,2},{1,3},{2,4},{3,5},{4,6},{5,7},{6,8},{7,9},{8,10},{9,11},{10,... | collective-permute-start | bytes 393224 | tf_op jit(solution)/shard_map/ppermute | solution.py:280
  51.9 15.7 %collective-permute-start.13 = (bf16[2,128,256]{2,1,0:T(8,128)(2,1)S(1)}, bf16[2,128,256]{2,1,0:T(8,128)(2,1)S(1)}, u32[]{:S(2)}, u32[]{:S(2)}) collective-permute-start(bf16[2,128,256]{2,1,0:T(8,128)(2,1)S(1)} %get-tuple-element.62), channel_id=1, source_target_pairs={{2,0},{3,1},{4,2},{5,3},{6,4},{7,5},{8,6},{9,7},{10,8},{11,9},{12,... | collective-permute-start | bytes 393224 | tf_op jit(solution)/shard_map/ppermute | solution.py:280
  56.6 15.7 %collective-permute-start.14 = (bf16[2,128,256]{2,1,0:T(8,128)(2,1)S(1)}, bf16[2,128,256]{2,1,0:T(8,128)(2,1)S(1)}, u32[]{:S(2)}, u32[]{:S(2)}) collective-permute-start(bf16[2,128,256]{2,1,0:T(8,128)(2,1)S(1)} %get-tuple-element.62), channel_id=1, source_target_pairs={{0,3},{2,5},{3,0},{4,7},{5,2},{6,9},{7,4},{8,11},{9,6},{10,13},{11... | collective-permute-start | bytes 393224 | tf_op jit(solution)/shard_map/ppermute | solution.py:280
  62.2 170.3 %collective-permute-start.17 = (bf16[2,128,256]{2,1,0:T(8,128)(2,1)S(1)}, bf16[2,128,256]{2,1,0:T(8,128)(2,1)S(1)}, u32[]{:S(2)}, u32[]{:S(2)}) collective-permute-start(bf16[2,128,256]{2,1,0:T(8,128)(2,1)S(1)} %get-tuple-element.66), channel_id=1, source_target_pairs={{0,2},{1,3},{2,4},{3,5},{4,6},{5,7},{6,8},{7,9},{8,10},{9,11},{10,... | collective-permute-start | bytes 393224 | tf_op jit(solution)/shard_map/ppermute | solution.py:280
  67.6 171.6 %collective-permute-start.18 = (bf16[2,128,256]{2,1,0:T(8,128)(2,1)S(1)}, bf16[2,128,256]{2,1,0:T(8,128)(2,1)S(1)}, u32[]{:S(2)}, u32[]{:S(2)}) collective-permute-start(bf16[2,128,256]{2,1,0:T(8,128)(2,1)S(1)} %get-tuple-element.66), channel_id=1, source_target_pairs={{2,0},{3,1},{4,2},{5,3},{6,4},{7,5},{8,6},{9,7},{10,8},{11,9},{12,... | collective-permute-start | bytes 393224 | tf_op jit(solution)/shard_map/ppermute | solution.py:280
  72.3 170.1 %collective-permute-start.19 = (bf16[2,128,256]{2,1,0:T(8,128)(2,1)S(1)}, bf16[2,128,256]{2,1,0:T(8,128)(2,1)S(1)}, u32[]{:S(2)}, u32[]{:S(2)}) collective-permute-start(bf16[2,128,256]{2,1,0:T(8,128)(2,1)S(1)} %get-tuple-element.66), channel_id=1, source_target_pairs={{0,3},{2,5},{3,0},{4,7},{5,2},{6,9},{7,4},{8,11},{9,6},{10,13},{11... | collective-permute-start | bytes 393224 | tf_op jit(solution)/shard_map/ppermute | solution.py:280
  75.0 45.5 %collective-permute-start.5 = (bf16[2,512,256]{2,1,0:T(8,128)(2,1)S(1)}, bf16[2,512,256]{2,1,0:T(8,128)(2,1)S(1)}, u32[]{:S(2)}, u32[]{:S(2)}) collective-permute-start(bf16[2,512,256]{2,1,0:T(8,128)(2,1)S(1)} %copy-done.15), channel_id=1, source_target_pairs={{0,1},{1,2},{2,3},{3,4},{4,5},{5,6},{6,7},{7,8},{8,9},{9,10},{10,1... | collective-permute-start | bytes 1572872 | tf_op jit(solution)/shard_map/ppermute | solution.py:280
  77.1 48.2 %collective-permute-start.6 = (bf16[2,512,256]{2,1,0:T(8,128)(2,1)S(1)}, bf16[2,512,256]{2,1,0:T(8,128)(2,1)S(1)}, u32[]{:S(2)}, u32[]{:S(2)}) collective-permute-start(bf16[2,512,256]{2,1,0:T(8,128)(2,1)S(1)} %copy-done.13), channel_id=1, source_target_pairs={{1,0},{2,1},{3,2},{4,3},{5,4},{6,5},{7,6},{8,7},{9,8},{10,9},{11,1... | collective-permute-start | bytes 1572872 | tf_op jit(solution)/shard_map/ppermute | solution.py:280
  120.5 49.4 %collective-permute-start.10 = (bf16[2,512,256]{2,1,0:T(8,128)(2,1)S(1)}, bf16[2,512,256]{2,1,0:T(8,128)(2,1)S(1)}, u32[]{:S(2)}, u32[]{:S(2)}) collective-permute-start(bf16[2,512,256]{2,1,0:T(8,128)(2,1)S(1)} %copy-done.19), channel_id=1, source_target_pairs={{0,1},{1,2},{2,3},{3,4},{4,5},{5,6},{6,7},{7,8},{8,9},{9,10},{10,1... | collective-permute-start | bytes 1572872 | tf_op jit(solution)/shard_map/ppermute | solution.py:280
  125.3 46.5 %collective-permute-start.11 = (bf16[2,512,256]{2,1,0:T(8,128)(2,1)S(1)}, bf16[2,512,256]{2,1,0:T(8,128)(2,1)S(1)}, u32[]{:S(2)}, u32[]{:S(2)}) collective-permute-start(bf16[2,512,256]{2,1,0:T(8,128)(2,1)S(1)} %copy-done.17), channel_id=1, source_target_pairs={{1,0},{2,1},{3,2},{4,3},{5,4},{6,5},{7,6},{8,7},{9,8},{10,9},{11,1... | collective-permute-start | bytes 1572872 | tf_op jit(solution)/shard_map/ppermute | solution.py:280
  169.9 76.3 %collective-permute-start.15 = (bf16[2,512,256]{2,1,0:T(8,128)(2,1)S(1)}, bf16[2,512,256]{2,1,0:T(8,128)(2,1)S(1)}, u32[]{:S(2)}, u32[]{:S(2)}) collective-permute-start(bf16[2,512,256]{2,1,0:T(8,128)(2,1)S(1)} %get-tuple-element.64), channel_id=1, source_target_pairs={{0,1},{1,2},{2,3},{3,4},{4,5},{5,6},{6,7},{7,8},{8,9},{9,10},{10,1... | collective-permute-start | bytes 1572872 | tf_op jit(solution)/shard_map/ppermute | solution.py:280
  171.9 67.3 %copy-start.28 = (bf16[2,512,256]{2,1,0:T(8,128)(2,1)S(1)}, bf16[2,512,256]{2,1,0:T(8,128)(2,1)}, u32[]{:S(2)}) copy-start(bf16[2,512,256]{2,1,0:T(8,128)(2,1)} %get-tuple-element.74) | copy-start | bytes 1572868
  171.9 70.4 %copy-start.27 = (bf16[2,384,256]{2,1,0:T(8,128)(2,1)S(1)}, bf16[2,384,256]{2,1,0:T(8,128)(2,1)}, u32[]{:S(2)}) copy-start(bf16[2,384,256]{2,1,0:T(8,128)(2,1)} %get-tuple-element.82) | copy-start | bytes 1179652
  171.9 78.5 %collective-permute-start.16 = (bf16[2,512,256]{2,1,0:T(8,128)(2,1)S(1)}, bf16[2,512,256]{2,1,0:T(8,128)(2,1)S(1)}, u32[]{:S(2)}, u32[]{:S(2)}) collective-permute-start(bf16[2,512,256]{2,1,0:T(8,128)(2,1)S(1)} %get-tuple-element.65), channel_id=1, source_target_pairs={{1,0},{2,1},{3,2},{4,3},{5,4},{6,5},{7,6},{8,7},{9,8},{10,9},{11,1... | collective-permute-start | bytes 1572872 | tf_op jit(solution)/shard_map/ppermute | solution.py:280
  232.5 21.9 %collective-permute-start.22 = (bf16[2,128,256]{2,1,0:T(8,128)(2,1)S(1)}, bf16[2,128,256]{2,1,0:T(8,128)(2,1)S(1)}, u32[]{:S(2)}, u32[]{:S(2)}) collective-permute-start(bf16[2,128,256]{2,1,0:T(8,128)(2,1)S(1)} %get-tuple-element.102), channel_id=1, source_target_pairs={{2,0},{3,1},{4,2},{5,3},{6,4},{7,5},{8,6},{9,7},{10,8},{11,9},{12,... | collective-permute-start | bytes 393224 | tf_op jit(solution)/shard_map/ppermute | solution.py:280
  239.2 51.5 %collective-permute-start.20 = (bf16[2,512,256]{2,1,0:T(8,128)(2,1)S(1)}, bf16[2,512,256]{2,1,0:T(8,128)(2,1)S(1)}, u32[]{:S(2)}, u32[]{:S(2)}) collective-permute-start(bf16[2,512,256]{2,1,0:T(8,128)(2,1)S(1)} %copy-done.28), channel_id=1, source_target_pairs={{1,0},{2,1},{3,2},{4,3},{5,4},{6,5},{7,6},{8,7},{9,8},{10,9},{11,1... | collective-permute-start | bytes 1572872 | tf_op jit(solution)/shard_map/ppermute | solution.py:280
  242.3 15.1 %collective-permute-start.23 = (bf16[2,128,256]{2,1,0:T(8,128)(2,1)S(1)}, bf16[2,128,256]{2,1,0:T(8,128)(2,1)S(1)}, u32[]{:S(2)}, u32[]{:S(2)}) collective-permute-start(bf16[2,128,256]{2,1,0:T(8,128)(2,1)S(1)} %get-tuple-element.101), channel_id=1, source_target_pairs={{0,2},{1,3},{2,4},{3,5},{4,6},{5,7},{6,8},{7,9},{8,10},{9,11},{10,... | collective-permute-start | bytes 393224 | tf_op jit(solution)/shard_map/ppermute | solution.py:280
  246.3 19.8 %collective-permute-start.24 = (bf16[2,128,256]{2,1,0:T(8,128)(2,1)S(1)}, bf16[2,128,256]{2,1,0:T(8,128)(2,1)S(1)}, u32[]{:S(2)}, u32[]{:S(2)}) collective-permute-start(bf16[2,128,256]{2,1,0:T(8,128)(2,1)S(1)} %get-tuple-element.100), channel_id=1, source_target_pairs={{3,0},{5,2},{0,3},{7,4},{2,5},{9,6},{4,7},{11,8},{6,9},{13,10},{8,... | collective-permute-start | bytes 393224 | tf_op jit(solution)/shard_map/ppermute | solution.py:280
  250.4 17.6 %collective-permute-start.27 = (bf16[2,128,256]{2,1,0:T(8,128)(2,1)S(1)}, bf16[2,128,256]{2,1,0:T(8,128)(2,1)S(1)}, u32[]{:S(2)}, u32[]{:S(2)}) collective-permute-start(bf16[2,128,256]{2,1,0:T(8,128)(2,1)S(1)} %get-tuple-element.105), channel_id=1, source_target_pairs={{2,0},{3,1},{4,2},{5,3},{6,4},{7,5},{8,6},{9,7},{10,8},{11,9},{12,... | collective-permute-start | bytes 393224 | tf_op jit(solution)/shard_map/ppermute | solution.py:280
  254.4 17.5 %collective-permute-start.28 = (bf16[2,128,256]{2,1,0:T(8,128)(2,1)S(1)}, bf16[2,128,256]{2,1,0:T(8,128)(2,1)S(1)}, u32[]{:S(2)}, u32[]{:S(2)}) collective-permute-start(bf16[2,128,256]{2,1,0:T(8,128)(2,1)S(1)} %get-tuple-element.104), channel_id=1, source_target_pairs={{0,2},{1,3},{2,4},{3,5},{4,6},{5,7},{6,8},{7,9},{8,10},{9,11},{10,... | collective-permute-start | bytes 393224 | tf_op jit(solution)/shard_map/ppermute | solution.py:280
  257.4 21.5 %collective-permute-start.29 = (bf16[2,128,256]{2,1,0:T(8,128)(2,1)S(1)}, bf16[2,128,256]{2,1,0:T(8,128)(2,1)S(1)}, u32[]{:S(2)}, u32[]{:S(2)}) collective-permute-start(bf16[2,128,256]{2,1,0:T(8,128)(2,1)S(1)} %get-tuple-element.103), channel_id=1, source_target_pairs={{3,0},{5,2},{0,3},{7,4},{2,5},{9,6},{4,7},{11,8},{6,9},{13,10},{8,... | collective-permute-start | bytes 393224 | tf_op jit(solution)/shard_map/ppermute | solution.py:280
  266.1 14.8 %collective-permute-start.32 = (bf16[2,128,256]{2,1,0:T(8,128)(2,1)S(1)}, bf16[2,128,256]{2,1,0:T(8,128)(2,1)S(1)}, u32[]{:S(2)}, u32[]{:S(2)}) collective-permute-start(bf16[2,128,256]{2,1,0:T(8,128)(2,1)S(1)} %get-tuple-element.108), channel_id=1, source_target_pairs={{2,0},{3,1},{4,2},{5,3},{6,4},{7,5},{8,6},{9,7},{10,8},{11,9},{12,... | collective-permute-start | bytes 393224 | tf_op jit(solution)/shard_map/ppermute | solution.py:280
  268.0 16.8 %collective-permute-start.33 = (bf16[2,128,256]{2,1,0:T(8,128)(2,1)S(1)}, bf16[2,128,256]{2,1,0:T(8,128)(2,1)S(1)}, u32[]{:S(2)}, u32[]{:S(2)}) collective-permute-start(bf16[2,128,256]{2,1,0:T(8,128)(2,1)S(1)} %get-tuple-element.107), channel_id=1, source_target_pairs={{0,2},{1,3},{2,4},{3,5},{4,6},{5,7},{6,8},{7,9},{8,10},{9,11},{10,... | collective-permute-start | bytes 393224 | tf_op jit(solution)/shard_map/ppermute | solution.py:280
  272.0 15.7 %collective-permute-start.34 = (bf16[2,128,256]{2,1,0:T(8,128)(2,1)S(1)}, bf16[2,128,256]{2,1,0:T(8,128)(2,1)S(1)}, u32[]{:S(2)}, u32[]{:S(2)}) collective-permute-start(bf16[2,128,256]{2,1,0:T(8,128)(2,1)S(1)} %get-tuple-element.106), channel_id=1, source_target_pairs={{3,0},{5,2},{0,3},{7,4},{2,5},{9,6},{4,7},{11,8},{6,9},{13,10},{8,... | collective-permute-start | bytes 393224 | tf_op jit(solution)/shard_map/ppermute | solution.py:280
  278.9 67.3 %collective-permute-start.21 = (bf16[2,512,256]{2,1,0:T(8,128)(2,1)}, bf16[2,512,256]{2,1,0:T(8,128)(2,1)S(1)}, u32[]{:S(2)}, u32[]{:S(2)}) collective-permute-start(bf16[2,512,256]{2,1,0:T(8,128)(2,1)} %get-tuple-element.75), channel_id=1, source_target_pairs={{0,1},{1,2},{2,3},{3,4},{4,5},{5,6},{6,7},{7,8},{8,9},{9,10},{10,1... | collective-permute-start | bytes 1572872 | tf_op jit(solution)/shard_map/ppermute | solution.py:280
  280.9 70.7 %collective-permute-start.25 = (bf16[2,512,256]{2,1,0:T(8,128)(2,1)}, bf16[2,512,256]{2,1,0:T(8,128)(2,1)S(1)}, u32[]{:S(2)}, u32[]{:S(2)}) collective-permute-start(bf16[2,512,256]{2,1,0:T(8,128)(2,1)} %get-tuple-element.80), channel_id=1, source_target_pairs={{1,0},{2,1},{3,2},{4,3},{5,4},{6,5},{7,6},{8,7},{9,8},{10,9},{11,1... | collective-permute-start | bytes 1572872 | tf_op jit(solution)/shard_map/ppermute | solution.py:280
  284.8 69.7 %collective-permute-start.26 = (bf16[2,512,256]{2,1,0:T(8,128)(2,1)}, bf16[2,512,256]{2,1,0:T(8,128)(2,1)S(1)}, u32[]{:S(2)}, u32[]{:S(2)}) collective-permute-start(bf16[2,512,256]{2,1,0:T(8,128)(2,1)} %get-tuple-element.81), channel_id=1, source_target_pairs={{0,1},{1,2},{2,3},{3,4},{4,5},{5,6},{6,7},{7,8},{8,9},{9,10},{10,1... | collective-permute-start | bytes 1572872 | tf_op jit(solution)/shard_map/ppermute | solution.py:280
  287.6 79.5 %collective-permute-start.30 = (bf16[2,512,256]{2,1,0:T(8,128)(2,1)}, bf16[2,512,256]{2,1,0:T(8,128)(2,1)S(1)}, u32[]{:S(2)}, u32[]{:S(2)}) collective-permute-start(bf16[2,512,256]{2,1,0:T(8,128)(2,1)} %get-tuple-element.86), channel_id=1, source_target_pairs={{1,0},{2,1},{3,2},{4,3},{5,4},{6,5},{7,6},{8,7},{9,8},{10,9},{11,1... | collective-permute-start | bytes 1572872 | tf_op jit(solution)/shard_map/ppermute | solution.py:280
  290.7 80.9 %copy-start.20 = (bf16[1024,256]{1,0:T(8,128)(2,1)S(1)}, bf16[1024,256]{1,0:T(8,128)(2,1)}, u32[]{:S(2)}) copy-start(bf16[1024,256]{1,0:T(8,128)(2,1)} %get-tuple-element.55) | copy-start | bytes 1572868
  290.7 80.9 %copy-start.21 = (bf16[1024,256]{1,0:T(8,128)(2,1)S(1)}, bf16[1024,256]{1,0:T(8,128)(2,1)}, u32[]{:S(2)}) copy-start(bf16[1024,256]{1,0:T(8,128)(2,1)} %get-tuple-element.68) | copy-start | bytes 1572868
  290.7 80.9 %copy-start.22 = (bf16[1024,256]{1,0:T(8,128)(2,1)S(1)}, bf16[1024,256]{1,0:T(8,128)(2,1)}, u32[]{:S(2)}) copy-start(bf16[1024,256]{1,0:T(8,128)(2,1)} %get-tuple-element.59) | copy-start | bytes 1572868
  290.7 80.9 %copy-start.23 = (bf16[1024,256]{1,0:T(8,128)(2,1)S(1)}, bf16[1024,256]{1,0:T(8,128)(2,1)}, u32[]{:S(2)}) copy-start(bf16[1024,256]{1,0:T(8,128)(2,1)} %get-tuple-element.69) | copy-start | bytes 1572868
  290.7 80.9 %copy-start.24 = (bf16[1024,256]{1,0:T(8,128)(2,1)S(1)}, bf16[1024,256]{1,0:T(8,128)(2,1)}, u32[]{:S(2)}) copy-start(bf16[1024,256]{1,0:T(8,128)(2,1)} %get-tuple-element.63) | copy-start | bytes 1572868
  290.7 80.9 %copy-start.25 = (bf16[1024,256]{1,0:T(8,128)(2,1)S(1)}, bf16[1024,256]{1,0:T(8,128)(2,1)}, u32[]{:S(2)}) copy-start(bf16[1024,256]{1,0:T(8,128)(2,1)} %get-tuple-element.70) | copy-start | bytes 1572868
  290.8 78.4 %collective-permute-start.31 = (bf16[2,512,256]{2,1,0:T(8,128)(2,1)}, bf16[2,512,256]{2,1,0:T(8,128)(2,1)S(1)}, u32[]{:S(2)}, u32[]{:S(2)}) collective-permute-start(bf16[2,512,256]{2,1,0:T(8,128)(2,1)} %get-tuple-element.87), channel_id=1, source_target_pairs={{0,1},{1,2},{2,3},{3,4},{4,5},{5,6},{6,7},{7,8},{8,9},{9,10},{10,1... | collective-permute-start | bytes 1572872 | tf_op jit(solution)/shard_map/ppermute | solution.py:280
  346.3 34.7 %collective-permute-start.35 = (bf16[2,512,256]{2,1,0:T(8,128)(2,1)}, bf16[2,512,256]{2,1,0:T(8,128)(2,1)S(1)}, u32[]{:S(2)}, u32[]{:S(2)}) collective-permute-start(bf16[2,512,256]{2,1,0:T(8,128)(2,1)} %get-tuple-element.92), channel_id=1, source_target_pairs={{1,0},{2,1},{3,2},{4,3},{5,4},{6,5},{7,6},{8,7},{9,8},{10,9},{11,1... | collective-permute-start | bytes 1572872 | tf_op jit(solution)/shard_map/ppermute | solution.py:280
  351.5 29.5 %collective-permute-start.36 = (bf16[2,512,256]{2,1,0:T(8,128)(2,1)}, bf16[2,512,256]{2,1,0:T(8,128)(2,1)S(1)}, u32[]{:S(2)}, u32[]{:S(2)}) collective-permute-start(bf16[2,512,256]{2,1,0:T(8,128)(2,1)} %get-tuple-element.93), channel_id=1, source_target_pairs={{0,1},{1,2},{2,3},{3,4},{4,5},{5,6},{6,7},{7,8},{8,9},{9,10},{10,1... | collective-permute-start | bytes 1572872 | tf_op jit(solution)/shard_map/ppermute | solution.py:280
  354.5 26.5 %collective-permute-start.37 = (bf16[2,128,256]{2,1,0:T(8,128)(2,1)S(1)}, bf16[2,128,256]{2,1,0:T(8,128)(2,1)S(1)}, u32[]{:S(2)}, u32[]{:S(2)}) collective-permute-start(bf16[2,128,256]{2,1,0:T(8,128)(2,1)S(1)} %get-tuple-element.111), channel_id=1, source_target_pairs={{2,0},{3,1},{4,2},{5,3},{6,4},{7,5},{8,6},{9,7},{10,8},{11,9},{12,... | collective-permute-start | bytes 393224 | tf_op jit(solution)/shard_map/ppermute | solution.py:280
  367.2 13.8 %collective-permute-start.38 = (bf16[2,128,256]{2,1,0:T(8,128)(2,1)S(1)}, bf16[2,128,256]{2,1,0:T(8,128)(2,1)S(1)}, u32[]{:S(2)}, u32[]{:S(2)}) collective-permute-start(bf16[2,128,256]{2,1,0:T(8,128)(2,1)S(1)} %get-tuple-element.110), channel_id=1, source_target_pairs={{0,2},{1,3},{2,4},{3,5},{4,6},{5,7},{6,8},{7,9},{8,10},{9,11},{10,... | collective-permute-start | bytes 393224 | tf_op jit(solution)/shard_map/ppermute | solution.py:280
  369.1 11.9 %collective-permute-start.39 = (bf16[2,128,256]{2,1,0:T(8,128)(2,1)S(1)}, bf16[2,128,256]{2,1,0:T(8,128)(2,1)S(1)}, u32[]{:S(2)}, u32[]{:S(2)}) collective-permute-start(bf16[2,128,256]{2,1,0:T(8,128)(2,1)S(1)} %get-tuple-element.109), channel_id=1, source_target_pairs={{3,0},{5,2},{0,3},{7,4},{2,5},{9,6},{4,7},{11,8},{6,9},{13,10},{8,... | collective-permute-start | bytes 393224 | tf_op jit(solution)/shard_map/ppermute | solution.py:280
  (27 other events, 366.0 us)

commit v2 on v1

--- a/solution.py
+++ b/solution.py
@@ -13,6 +13,14 @@
 PAIR = 128
 AXES = ("seqa", "seqb")
 GROUPS = (2, 2, 2, 2)
+ORDER = (
+    ("pair", 0), ("cross", 0), ("pair", 1), ("cross", 1), ("pair", 2),
+    ("attend", 0), ("cross", 2), ("pair", 3),
+    ("attend", 1), ("cross", 3), ("back", 0),
+    ("attend", 2), ("back", 1),
+    ("attend", 3), ("back", 2), ("sum", 0), ("back", 3), ("sum", 1), ("sum", 2), ("sum", 3),
+)
+LIMIT = 60
 LOG2E = math.log2(math.e)
 BF16 = jnp.bfloat16
 F32 = jnp.float32
@@ -59,11 +67,28 @@
     return lax.dot_general(a, b, dims, preferred_element_type=F32)
 
 
-def mean_rows(ref, start, count, stride):
-    total = ref[pl.ds(start, count, stride=stride), :]
-    for i in range(1, stride):
-        total = total + ref[pl.ds(start + i, count, stride=stride), :]
-    return total * (1.0 / stride)
+def mean_rows(rows, stride):
+    step = min(256, rows.shape[0])
+    out = lax.broadcasted_iota(jnp.int32, (step // stride, step), 0)
+    at = lax.broadcasted_iota(jnp.int32, (step // stride, step), 1)
+    take = jnp.where(at // stride == out, 1.0 / stride, 0.0).astype(BF16)
+    parts = [dot(take, rows[i : i + step]) for i in range(0, rows.shape[0], step)]
+    parts = [part.astype(BF16) for part in parts]
+    return parts[0] if len(parts) == 1 else jnp.concatenate(parts, 0)
+
+
+def repeat_rows(rows, stride):
+    step = min(256 // stride, rows.shape[0])
+    out = lax.broadcasted_iota(jnp.int32, (step * stride, step), 0)
+    at = lax.broadcasted_iota(jnp.int32, (step * stride, step), 1)
+    put = jnp.where(out // stride == at, 1.0, 0.0).astype(BF16)
+    parts = [dot(put, rows[i : i + step]) for i in range(0, rows.shape[0], step)]
+    return parts[0] if len(parts) == 1 else jnp.concatenate(parts, 0)
+
+
+def add_rows(ref, start, rows, stride):
+    at = slice(start, start + rows.shape[0] * stride)
+    ref[at] = ref[at] + (repeat_rows(rows, stride) if stride > 1 else rows.astype(F32))
 
 
 def spread_rows(ref, start, rows, stride):
@@ -73,22 +98,41 @@
 
 
 def attend_kernel(
-    valid, q, k, v, do, lk, lv, uk, uv, fk, fv,
-    o, dq, gk, gv, glk, glv, guk, guv, gfk, gfv,
+    role, valid, q, k, v, do, hk, hv, bk, bv, ak, av,
+    o, dq, gk, gv, rh, rup, rdown, token,
     kext, vext, kt, vt, e0, e1, e2, e3, x0, x1, x2, x3,
-    qz, doz, qs, dos, inn, rls, ftmp, gtmp, flag,
+    qz, doz, qs, dos, inn, rls, gtmp, cross, small, side, flag,
 ):
     es = (e0, e1, e2, e3)
     xs = (x0, x1, x2, x3)
     lane = lax.broadcasted_iota(jnp.int32, (256, PAIR), 1)
     first = lane < HEAD_DIM
-
-    for own, low, up, far, ext in ((k, lk, uk, fk, kext), (v, lv, uv, fv, vext)):
+    even = role[0] == 0
+    odd = jnp.logical_not(even)
+    pass_on(role, token)
+
+    for which, (h, b, a) in enumerate(((hk, bk, ak), (hv, bv, av))):
+
+        @pl.when(even)
+        def _():
+            cross[which] = b[...]
+            small[which] = a[0:256]
+            side[0, which] = b[0:512]
+            side[1, which] = h[...]
+
+        @pl.when(odd)
+        def _():
+            cross[which] = a[...]
+            small[which] = b[0:256]
+            side[0, which] = h[...]
+            side[1, which] = a[0:512]
+
+    for which, own, ext in ((0, k, kext), (1, v, vext)):
+        low, up = side.at[0, which], side.at[1, which]
         ext[0:256] = low[0:256]
         ext[256:1280] = own[...]
         ext[1280:1536] = up[0:256]
-        ftmp[0:1024] = own[...].astype(F32)
-        spans = mean_rows(ftmp, 0, 512, 2).astype(BF16)
+        spans = mean_rows(own[...], 2)
         b1 = BASE[1]
         ext[b1 + 256 : b1 + 384] = spans[384:512]
         ext[b1 + 384 : b1 + 512] = spans[256:384]
@@ -97,17 +141,16 @@
         ext[b1 + 128 : b1 + 256] = low[256:384]
         ext[b1 + 768 : b1 + 896] = up[256:384]
         b2 = BASE[2]
-        ftmp[0:384] = low[0:384].astype(F32)
-        ext[b1 : b1 + 128] = mean_rows(ftmp, 0, 128, 2).astype(BF16)
-        ext[b2 + 384 : b2 + 448] = mean_rows(ftmp, 256, 64, 2).astype(BF16)
-        ext[b2 + 448 : b2 + 512] = mean_rows(ftmp, 0, 64, 4).astype(BF16)
-        ftmp[0:384] = up[0:384].astype(F32)
-        ext[b1 + 896 : b1 + 1024] = mean_rows(ftmp, 0, 128, 2).astype(BF16)
-        ext[b2 : b2 + 64] = mean_rows(ftmp, 0, 64, 4).astype(BF16)
-        ext[b2 + 64 : b2 + 128] = mean_rows(ftmp, 256, 64, 2).astype(BF16)
+        ext[b1 : b1 + 128] = mean_rows(low[0:256], 2)
+        ext[b2 + 384 : b2 + 448] = mean_rows(low[256:384], 2)
+        ext[b2 + 448 : b2 + 512] = mean_rows(low[0:256], 4)
+        ext[b1 + 896 : b1 + 1024] = mean_rows(up[0:256], 2)
+        ext[b2 : b2 + 64] = mean_rows(up[0:256], 4)
+        ext[b2 + 64 : b2 + 128] = mean_rows(up[256:384], 2)
         ext[b2 + 128 : b2 + 256] = low[384:512]
         ext[b2 + 256 : b2 + 384] = up[384:512]
-        ext[BASE[3] : ROWS] = far[...]
+        ext[BASE[3] : BASE[3] + 128] = cross[which, 512:640]
+        ext[BASE[3] + 128 : ROWS] = small[which]
 
     low_ok, up_ok = valid[0], valid[1]
     for level, row, rows, ok in (
@@ -230,9 +273,8 @@
             outs.append(acc * (rls[0:1, to] * 0.125))
         dq[b * 256 : b * 256 + 256] = jnp.concatenate(outs, 0).T.astype(BF16)
 
-    for ws, right, own, low, up, far in (
-        (xs, qs, gk, glk, guk, gfk), (es, dos, gv, glv, guv, gfv)
-    ):
+    for which, ws, right, own in ((0, xs, qs, gk), (1, es, dos, gv)):
+        low, up = side.at[0, which], side.at[1, which]
         got = {}
         for level, row, rows, col, b, nb in TILES:
             got[level, row] = dot(
@@ -271,10 +313,53 @@
                     spread_rows(gtmp, 256, g[0:64], 2)
                     spread_rows(gtmp, 0, g[64:128], 4)
             else:
-                far[...] = got[level, row].astype(BF16)
+                cross[which, 512:640] = got[level, row][0:128].astype(BF16)
+                small[which] = got[level, row][128:384].astype(BF16)
         low[0:384] = gtmp[0:384].astype(BF16)
         up[0:384] = gtmp[384:768].astype(BF16)
 
+        @pl.when(even)
+        def _():
+            rh[which] = up[...]
+            rdown[which, 0:512] = low[...]
+            rdown[which, 512:640] = cross[which, 512:640]
+            rup[which, 0:256] = small[which]
+
+        @pl.when(odd)
+        def _():
+            rh[which] = low[...]
+            rup[which, 0:512] = up[...]
+            rup[which, 512:640] = cross[which, 512:640]
+            rdown[which, 0:256] = small[which]
+
+
+def pass_on(role, token):
+    token[0] = role[0]
+    token[1] = role[1]
+
+
+def add_down(ref, rows, own):
+    add_rows(ref, 0, rows[0:256], 1)
+    if own:
+        add_rows(ref, 256, rows[256:384], 2)
+        add_rows(ref, 512, rows[384:512], 4)
+    else:
+        add_rows(ref, 512, rows[256:384], 1)
+        add_rows(ref, 640, rows[384:448], 2)
+        add_rows(ref, 256, rows[448:512], 4)
+
+
+def add_up(ref, rows, own):
+    if own:
+        add_rows(ref, 768, rows[0:256], 1)
+        add_rows(ref, 512, rows[256:384], 2)
+        add_rows(ref, 0, rows[384:512], 4)
+    else:
+        add_rows(ref, 256, rows[0:256], 1)
+        add_rows(ref, 640, rows[256:384], 1)
+        add_rows(ref, 0, rows[384:448], 4)
+        add_rows(ref, 512, rows[448:512], 2)
+
 
 def moved(array, pairs):
     return lax.ppermute(array, AXES, pairs)
@@ -288,64 +373,141 @@
     return pltpu.CompilerParams(vmem_limit_bytes=limit * 2**20)
 
 
-def send(keys, values, start, pairs):
-    col = start
-    block = pl.BlockSpec((1024, PAIR), lambda j: (0, col + j))
-
-    def body(k, v, up, down, far, tmp):
-        for own, side in ((k, 0), (v, 1)):
-            tmp[...] = own[...].astype(F32)
-            up[side, 0:256] = own[768:1024]
-            up[side, 256:384] = mean_rows(tmp, 512, 128, 2).astype(BF16)
-            up[side, 384:512] = mean_rows(tmp, 0, 128, 4).astype(BF16)
-            down[side, 0:256] = own[0:256]
-            down[side, 256:384] = mean_rows(tmp, 256, 128, 2).astype(BF16)
-            down[side, 384:512] = mean_rows(tmp, 512, 128, 4).astype(BF16)
-            far[side] = mean_rows(tmp, 0, 128, 8).astype(BF16)
-
-    side = lambda rows: pl.BlockSpec((2, rows, PAIR), lambda j: (0, 0, j))
+SMEM = pl.BlockSpec(memory_space=pltpu.SMEM)
+
+
+def both(rows):
+    return pl.BlockSpec((2, rows, PAIR), lambda j: (0, 0, j))
+
+
+def columns(start):
+    return pl.BlockSpec((1024, PAIR), lambda j: (0, start + j))
+
+
+TOKEN = shape(2, dtype=jnp.int32)
+
+
+def pair_rows(role, keys, values, start, pairs):
+    def body(role, k, v, out, token):
+        pass_on(role, token)
+        for which, own in ((0, k), (1, v)):
+            out[which, 0:256] = own[0:256]
+            out[which, 256:512] = own[768:1024]
+            out[which, 512:768] = mean_rows(own[256:768], 2)
+
+    return pl.pallas_call(
+        body,
+        grid=(pairs,),
+        in_specs=[SMEM] + [columns(start)] * 2,
+        out_specs=[both(768), SMEM],
+        out_shape=[shape(2, 768, pairs * PAIR), TOKEN],
+        compiler_params=vmem(LIMIT),
+        name="pair_rows",
+    )(role, keys, values)
+
+
+def cross_rows(role, keys, values, partner, start, pairs):
+    def body(role, k, v, p, near, up_out, down_out, token, spans):
+        even, wrap = role[0] == 0, role[1]
+        odd = jnp.logical_not(even)
+        pass_on(role, token)
+
+        for which, own in ((0, k), (1, v)):
+            spans[0:128] = mean_rows(own[...], 8)
+            spans[128:160] = mean_rows(p[which, 0:256], 8)
+            spans[160:192] = mean_rows(p[which, 512:640], 4)
+            spans[192:224] = mean_rows(p[which, 640:768], 4)
+            spans[224:256] = mean_rows(p[which, 256:512], 8)
+
+            def theirs_down(out):
+                out[which, 0:256] = p[which, 0:256]
+                out[which, 256:384] = p[which, 512:640]
+                out[which, 384:448] = mean_rows(p[which, 640:768], 2)
+                out[which, 448:512] = mean_rows(p[which, 256:512], 4)
+
+            def theirs_up(out):
+                out[which, 0:256] = p[which, 256:512]
+                out[which, 256:384] = p[which, 640:768]
+                out[which, 384:448] = mean_rows(p[which, 0:256], 4)
+                out[which, 448:512] = mean_rows(p[which, 512:640], 2)
+
+            @pl.when(even)
+            def _():
+                theirs_down(near)
+                theirs_up(up_out)
+                up_out[which, 512:640] = spans[0:128]
+                down_out[which, 0:256] = spans[...]
+
+            @pl.when(odd)
+            def _():
+                theirs_up(near)
+                theirs_down(down_out)
+                down_out[which, 512:640] = spans[0:128]
+                up_out[which, 0:256] = spans[...]
+
+            @pl.when((wrap == 1) & even)
+            def _():
+                down_out[which, 0:256] = own[0:256]
+                down_out[which, 256:384] = mean_rows(own[256:512], 2)
+                down_out[which, 384:512] = mean_rows(own[512:1024], 4)
+                down_out[which, 512:640] = spans[128:256]
+
+            @pl.when((wrap == 1) & odd)
+            def _():
+                up_out[which, 0:256] = own[768:1024]
+                up_out[which, 256:384] = mean_rows(own[512:768], 2)
+                up_out[which, 384:512] = mean_rows(own[0:512], 4)
+                up_out[which, 512:640] = spans[128:256]
+
+            @pl.when((wrap == 2) & even)
+            def _():
+                up_out[which, 0:128] = spans[128:256]
+                up_out[which, 128:256] = spans[0:128]
+
+            @pl.when((wrap == 2) & odd)
+            def _():
+                down_out[which, 0:128] = spans[128:256]
+                down_out[which, 128:256] = spans[0:128]
+
     width = pairs * PAIR
     return pl.pallas_call(
         body,
         grid=(pairs,),
-        in_specs=[block, block],
-        out_specs=[side(512), side(512), side(128)],
-        out_shape=[shape(2, 512, width), shape(2, 512, width), shape(2, 128, width)],
-        scratch_shapes=[pltpu.VMEM((1024, PAIR), F32)],
-        compiler_params=vmem(32),
-        name="rows_to_send",
-    )(keys, values)
-
-
-def attend(valid, queries, keys, values, grad_out, low, up, far, start, pairs):
-    whole = pl.BlockSpec((1024, PAIR), lambda j: (0, start + j))
-    mine = pl.BlockSpec((1024, PAIR), lambda j: (0, j))
+        in_specs=[SMEM, columns(start), columns(start), both(768)],
+        out_specs=[both(512), both(640), both(640), SMEM],
+        out_shape=[shape(2, rows, width) for rows in (512, 640, 640)] + [TOKEN],
+        scratch_shapes=[pltpu.VMEM((256, PAIR), BF16)],
+        compiler_params=vmem(LIMIT),
+        name="cross_rows",
+    )(role, keys, values, partner)
+
+
+def attend(role, valid, queries, keys, values, grad_out, came, before, start, pairs):
+    width = pairs * PAIR
 
     def side(rows, which):
         return pl.BlockSpec((None, rows, PAIR), lambda j: (which, 0, j))
 
-    width = pairs * PAIR
+    extra = 0 if before is None else 2
 
     def body(*refs):
-        ins = refs[:11]
-        o, dq, gk, gv, gl, gu, gf = refs[11:18]
-        attend_kernel(
-            *ins, o, dq, gk, gv,
-            gl.at[0], gl.at[1], gu.at[0], gu.at[1], gf.at[0], gf.at[1], *refs[18:],
-        )
-
-    both = lambda rows: pl.BlockSpec((2, rows, PAIR), lambda j: (0, 0, j))
+        attend_kernel(*refs[:12], *refs[12 + extra :])
+
+    heights = (512, 640, 640)
+    whole = shape(1024, queries.shape[1])
     return pl.pallas_call(
         body,
         grid=(pairs,),
-        in_specs=[pl.BlockSpec(memory_space=pltpu.SMEM), whole, whole, whole, whole]
-        + [side(rows, which) for rows in (512, 512, 384) for which in (0, 1)],
-        out_specs=[mine, mine, mine, mine, both(512), both(512), both(384)],
-        out_shape=[
-            shape(1024, width), shape(1024, width),
-            shape(1024, width, dtype=F32), shape(1024, width, dtype=F32),
-            shape(2, 512, width), shape(2, 512, width), shape(2, 384, width),
-        ],
+        in_specs=[SMEM, SMEM] + [columns(start)] * 4
+        + [side(rows, which) for rows in heights for which in (0, 1)]
+        + [pl.BlockSpec(memory_space=pl.ANY)] * extra,
+        out_specs=[columns(start)] * 2 + [columns(0)] * 2 + [both(rows) for rows in heights]
+        + [SMEM],
+        out_shape=[whole, whole]
+        + [shape(1024, width, dtype=F32)] * 2
+        + [shape(2, rows, width) for rows in heights]
+        + [TOKEN],
+        input_output_aliases={12: 0, 13: 1} if extra else {},
         scratch_shapes=[
             pltpu.VMEM((ROWS, PAIR), BF16), pltpu.VMEM((ROWS, PAIR), BF16),
             pltpu.VMEM((PAIR, ROWS), BF16), pltpu.VMEM((2, 80, ROWS), BF16),
@@ -357,98 +519,198 @@
         + [pltpu.VMEM((2048, PAIR), BF16)] * 4
         + [
             pltpu.VMEM((8, 2048), F32), pltpu.VMEM((8, 2048), F32),
-            pltpu.VMEM((1024, PAIR), F32), pltpu.VMEM((768, PAIR), F32),
+            pltpu.VMEM((768, PAIR), F32),
+            pltpu.VMEM((2, 640, PAIR), BF16), pltpu.VMEM((2, 256, PAIR), BF16),
+            pltpu.VMEM((2, 2, 512, PAIR), BF16),
             pltpu.SMEM((1,), jnp.int32),
         ],
-        compiler_params=vmem(56),
+        compiler_params=vmem(LIMIT),
         cost_estimate=pl.CostEstimate(
             flops=pairs * 14 * 10**9, bytes_accessed=pairs * 4 * 10**6, transcendentals=0
         ),
         name="attend_pairs",
-    )(valid, queries, keys, values, grad_out, low, low, up, up, far, far)
-
-
-def finish(own_k, own_v, above, below, far, pairs):
-    mine = pl.BlockSpec((1024, PAIR), lambda j: (0, j))
-    both = lambda rows: pl.BlockSpec((2, rows, PAIR), lambda j: (0, 0, j))
-
-    def body(gk, gv, above, below, f0, f1, f2, dk, dv, tmp):
-        for side, own, out in ((0, gk, dk), (1, gv, dv)):
-            tmp[...] = own[...]
-            tmp[768:1024] = tmp[768:1024] + above[side, 0:256].astype(F32)
-            spread_rows(tmp, 512, above[side, 256:384].astype(F32), 2)
-            spread_rows(tmp, 0, above[side, 384:512].astype(F32), 4)
-            tmp[0:256] = tmp[0:256] + below[side, 0:256].astype(F32)
-            spread_rows(tmp, 256, below[side, 256:384].astype(F32), 2)
-            spread_rows(tmp, 512, below[side, 384:512].astype(F32), 4)
-            total = f0[side].astype(F32) + f1[side].astype(F32) + f2[side].astype(F32)
-            spread_rows(tmp, 0, total, 8)
-            out[...] = tmp[...].astype(BF16)
-
-    width = pairs * PAIR
+    )(
+        role, valid, queries, keys, values, grad_out,
+        *[part for pair in came for part in (pair, pair)], *(before or ()),
+    )
+
+
+def pair_grads(role, near, above, below, pairs):
+    def body(role, near, above, below, out, token, tmp):
+        even, wrap = role[0] == 0, role[1]
+        odd = jnp.logical_not(even)
+        pass_on(role, token)
+
+        def add_span(rows):
+            add_rows(tmp, 0, rows[0:32], 8)
+            add_rows(tmp, 512, rows[32:64], 4)
+            add_rows(tmp, 640, rows[64:96], 4)
+            add_rows(tmp, 256, rows[96:128], 8)
+
+        for which in (0, 1):
+            tmp[...] = jnp.zeros_like(tmp)
+
+            @pl.when(even)
+            def _():
+                add_down(tmp, near[which], False)
+
+                @pl.when(wrap != 2)
+                def _():
+                    add_up(tmp, above[which, 0:512], False)
+
+                @pl.when(wrap == 2)
+                def _():
+                    add_span(above[which, 0:128])
+
+                @pl.when(wrap == 1)
+                def _():
+                    add_span(below[which, 512:640])
+
+                @pl.when(wrap != 1)
+                def _():
+                    add_span(below[which, 128:256])
+
+            @pl.when(odd)
+            def _():
+                add_up(tmp, near[which], False)
+
+                @pl.when(wrap != 2)
+                def _():
+                    add_down(tmp, below[which, 0:512], False)
+
+                @pl.when(wrap == 2)
+                def _():
+                    add_span(below[which, 0:128])
+
+                @pl.when(wrap == 1)
+                def _():
+                    add_span(above[which, 512:640])
+
+                @pl.when(wrap != 1)
+                def _():
+                    add_span(above[which, 128:256])
+
+            out[which] = tmp[...].astype(BF16)
+
     return pl.pallas_call(
         body,
         grid=(pairs,),
-        in_specs=[mine, mine, both(512), both(512), both(128), both(128), both(128)],
-        out_specs=[mine, mine],
-        out_shape=[shape(1024, width), shape(1024, width)],
+        in_specs=[SMEM, both(512), both(640), both(640)],
+        out_specs=[both(768), SMEM],
+        out_shape=[shape(2, 768, pairs * PAIR), TOKEN],
+        scratch_shapes=[pltpu.VMEM((768, PAIR), F32)],
+        compiler_params=vmem(LIMIT),
+        name="pair_grads",
+    )(role, near, above, below)
+
+
+def finish(role, own_k, own_v, above, below, partner, before, start, pairs):
+    extra = 0 if before is None else 2
+
+    def body(*refs):
+        role, gk, gv, above, below, got = refs[:6]
+        dk, dv, token, tmp = refs[6 + extra :]
+        even, wrap = role[0] == 0, role[1]
+        odd = jnp.logical_not(even)
+        pass_on(role, token)
+        for which, own, out in ((0, gk, dk), (1, gv, dv)):
+            tmp[...] = own[...]
+            add_rows(tmp, 0, got[which, 0:256], 1)
+            add_rows(tmp, 768, got[which, 256:512], 1)
+            add_rows(tmp, 256, got[which, 512:768], 2)
+
+            for here, large, small, add in ((even, above, below, add_down), (odd, below, above, add_up)):
+
+                @pl.when(here & (wrap != 2))
+                def _():
+                    add_rows(tmp, 0, large[which, 512:640], 8)
+
+                @pl.when(here & (wrap == 2))
+                def _():
+                    add_rows(tmp, 0, large[which, 128:256], 8)
+
+                @pl.when(here & (wrap != 1))
+                def _():
+                    add_rows(tmp, 0, small[which, 0:128], 8)
+
+                @pl.when(here & (wrap == 1))
+                def _():
+                    add(tmp, small[which, 0:512], True)
+
+            out[...] = tmp[...].astype(BF16)
+
+    whole = shape(1024, 1024)
+    return pl.pallas_call(
+        body,
+        grid=(pairs,),
+        in_specs=[SMEM] + [columns(0)] * 2 + [both(640), both(640), both(768)]
+        + [pl.BlockSpec(memory_space=pl.ANY)] * extra,
+        out_specs=[columns(start)] * 2 + [SMEM],
+        out_shape=[whole, whole, TOKEN],
+        input_output_aliases={6: 0, 7: 1} if extra else {},
         scratch_shapes=[pltpu.VMEM((1024, PAIR), F32)],
-        compiler_params=vmem(32),
+        compiler_params=vmem(LIMIT),
         name="sum_grads",
-    )(own_k, own_v, above, below, *far)
+    )(role, own_k, own_v, above, below, partner, *(before or ()))
+
+
+def routes(outer, inner):
+    count = outer * inner
+    up = {i: i + 2 for i in range(count - 2)}
+    for a in range(1, outer - 1, 2):
+        last = a * inner + inner - 2
+        up[last], up[last + 1] = last + 3, last + 2
+    return [(i, i ^ 1) for i in range(count)], sorted(up.items())
 
 
 def local(queries, keys, values, grad_out):
-    index = lax.axis_index(AXES)
-    count = lax.axis_size(AXES)
-
-    def by(step):
-        return [(i, i + step) for i in range(count) if 0 <= i + step < count]
-
-    three = [
-        (i, i + (3 if i % 2 == 0 else -3))
-        for i in range(count)
-        if 0 <= i + (3 if i % 2 == 0 else -3) < count
-    ]
-    third = jnp.where(index % 2 == 0, index + 3, index - 3)
+    a, b = lax.axis_index(AXES[0]), lax.axis_index(AXES[1])
+    outer, inner = lax.axis_size(AXES[0]), lax.axis_size(AXES[1])
+    index = a * inner + b
+    count = outer * inner
+    partners, up = routes(outer, inner)
+    down = [(j, i) for i, j in up]
+    above = (a % 2 == 1) & (a < outer - 1) & (b >= inner - 2)
+    below = (a % 2 == 0) & (a > 0) & (b < 2)
+    ends = (b == 0) | (b == inner - 1)
+    odd = index % 2
+    wrap = jnp.where(above | below, jnp.where(ends, 1, 2), 0)
+    token = jnp.stack([odd, wrap]).astype(jnp.int32)
+    sign = 1 - 2 * odd
+
+    def there(step):
+        at = index + step * sign
+        return (at >= 0) & (at < count)
+
     valid = jnp.stack(
-        [
-            index > 0,
-            index < count - 1,
-            index >= 2,
-            index < count - 2,
-            (third >= 0) & (third < count),
-        ]
+        [index > 0, index < count - 1, there(-2), there(2), there(3)]
     ).astype(F32)
 
-    halos = []
-    start = 0
-    for pairs in GROUPS:
-        up, down, far = send(keys, values, start, pairs)
-        low = moved(up, by(1))
-        high = moved(down, by(-1))
-        spans = jnp.concatenate(
-            [moved(far, by(2)), moved(far, by(-2)), moved(far, three)], axis=1
-        )
-        halos.append((start, pairs, low, high, spans))
-        start += pairs
-
-    results = []
-    for start, pairs, low, high, spans in halos:
-        o, dq, gk, gv, gl, gu, gf = attend(
-            valid, queries, keys, values, grad_out, low, high, spans, start, pairs
-        )
-        above = moved(gl, by(-1))
-        below = moved(gu, by(1))
-        far = (
-            moved(gf[:, 0:128], by(-2)),
-            moved(gf[:, 128:256], by(2)),
-            moved(gf[:, 256:384], [(b, a) for a, b in three]),
-        )
-        dk, dv = finish(gk, gv, above, below, far, pairs)
-        results.append((o, dq, dk, dv))
-    return tuple(jnp.concatenate(parts, axis=1) if len(parts) > 1 else parts[0]
-                 for parts in zip(*results))
+    starts = [sum(GROUPS[:i]) for i in range(len(GROUPS))]
+    partner, came, grown, near, answers, returned = {}, {}, {}, {}, {}, {}
+    mixed = grads = None
+    for step, i in ORDER:
+        start, pairs = starts[i], GROUPS[i]
+        if step == "pair":
+            rows, token = pair_rows(token, keys, values, start, pairs)
+            partner[i] = moved(rows, partners)
+        elif step == "cross":
+            side, upward, downward, token = cross_rows(
+                token, keys, values, partner[i], start, pairs
+            )
+            came[i] = (side, moved(upward, up), moved(downward, down))
+        elif step == "attend":
+            *mixed, gk, gv, near[i], upward, downward, token = attend(
+                token, valid, queries, keys, values, grad_out, came[i], mixed, start, pairs
+            )
+            grown[i] = (gk, gv)
+            answers[i] = (moved(downward, down), moved(upward, up))
+        elif step == "back":
+            rows, token = pair_grads(token, near[i], *answers[i], pairs)
+            returned[i] = moved(rows, partners)
+        else:
+            *grads, token = finish(token, *grown[i], *answers[i], returned[i], grads, start, pairs)
+    return (*mixed, *grads)
 
 
 def solution(mesh):

time: 393 us -> 380 us (0.967)
  the two profiles are of different devices: /device:TPU:36 before, /device:TPU:18 now
where the time goes in v2:
time: 380 us; the launch traced here: 376 us
  Pallas kernels  247 us (65%)
  starting transfers between devices  64.9 us (17%)
  waiting for transfers between devices  51.9 us (14%)
  local copies, waits for them, and re-layouts  9.14 us (2%)
    pallas_call x4, Pallas kernels, attend(): pl.pallas_call(body, grid=(pairs,), in_specs=[SMEM, SMEM] + [columns(star...  186 us
    ppermute x24, starting transfers between devices, moved(): return lax.ppermute(array, AXES, pairs)  64.9 us
    ppermute x24, waiting for transfers between devices, moved(): return lax.ppermute(array, AXES, pairs)  51.9 us
    pallas_call x4, Pallas kernels, finish(): pl.pallas_call(body, grid=(pairs,), in_specs=[SMEM] + [columns(0)] * 2 +...  19.4 us
    pallas_call x4, Pallas kernels, pair_grads(): pl.pallas_call(body, grid=(pairs,), in_specs=[SMEM, both(512), both(640),...  17.2 us
    pallas_call x4, Pallas kernels, cross_rows(): pl.pallas_call(body, grid=(pairs,), in_specs=[SMEM, columns(start), colum...  15.5 us
    pallas_call x4, Pallas kernels, pair_rows(): pl.pallas_call(body, grid=(pairs,), in_specs=[SMEM] + [columns(start)] *...  9.28 us
    unnamed x42, local copies, waits for them, and re-layouts  9.04 us
  transfers between devices with their start and end apart: 24, of which 5 were waited for; matrix products, arithmetic and copies ran while one was open for 0% of the time, Pallas kernels for 62%

profile of v2, /device:TPU:18, one launch (start us, length us, event | category | flops | bytes accessed | tf_op | source)
XLA Modules:
  0.0 375.6 jit_solution(13037104754037437430)
XLA Ops:
  1.3 2.3 pair_rows.4
  3.5 1.9 collective-permute-start
  5.5 17.7 %collective-permute-done.p = bf16[2,768,256]{2,1,0:T(8,128)(2,1)S(1)} collective-permute-done((bf16[2,768,256]{2,1,0:T(8,128)(2,1)}, bf16[2,768,256]{2,1,0:T(8,128)(2,1)S(1)}, u32[]{:S(2)}, u32[]{:S(2)}) %collective-permute-start) | collective-permute-done | bytes 786464 | tf_op jit(solution)/shard_map/ppermute | solution.py:365
  24.1 3.8 %cross_rows.4 = (bf16[2,512,256]{2,1,0:T(8,128)(2,1)}, bf16[2,640,256]{2,1,0:T(8,128)(2,1)}, bf16[2,640,256]{2,1,0:T(8,128)(2,1)}, s32[2]{0:T(128)}) custom-call(s32[2]{0:T(128)} %get-tuple-element.79.role, bf16[1024,1024]{1,0:T(8,128)(2,1)} %refs_3_.7, bf16[1024,1024]{1,0:T(8,128)(2,1)} %refs_4_.7, bf16[2,768,256]{2,1,0:T(8,128)(2,1)} %copy-done.14), custom_call_target="tpu_custom_call" | custom-call | tf_op jit(solution)/shard_map/cross_rows/pallas_call | solution.py:473
  27.9 2.4 pair_rows.5
  30.3 1.7 collective-permute-start.1
  32.0 3.2 collective-permute-start.2
  35.2 2.7 collective-permute-start.3
  38.6 10.5 %collective-permute-done.1.p = bf16[2,768,256]{2,1,0:T(8,128)(2,1)S(1)} collective-permute-done((bf16[2,768,256]{2,1,0:T(8,128)(2,1)}, bf16[2,768,256]{2,1,0:T(8,128)(2,1)S(1)}, u32[]{:S(2)}, u32[]{:S(2)}) %collective-permute-start.1) | collective-permute-done | bytes 786464 | tf_op jit(solution)/shard_map/ppermute | solution.py:365
  50.0 3.9 %cross_rows.5 = (bf16[2,512,256]{2,1,0:T(8,128)(2,1)}, bf16[2,640,256]{2,1,0:T(8,128)(2,1)}, bf16[2,640,256]{2,1,0:T(8,128)(2,1)}, s32[2]{0:T(128)}) custom-call(s32[2]{0:T(128)} %get-tuple-element.82.role, bf16[1024,1024]{1,0:T(8,128)(2,1)} %refs_3_.7, bf16[1024,1024]{1,0:T(8,128)(2,1)} %refs_4_.7, bf16[2,768,256]{2,1,0:T(8,128)(2,1)} %copy-done.9), custom_call_target="tpu_custom_call" | custom-call | tf_op jit(solution)/shard_map/cross_rows/pallas_call | solution.py:473
  53.9 3.7 collective-permute-start.5
  57.5 2.2 collective-permute-start.6
  59.7 2.3 pair_rows.6
  62.0 1.5 collective-permute-start.4
  64.7 40.2 %attend_pairs.4 = (bf16[1024,1024]{1,0:T(8,128)(2,1)}, bf16[1024,1024]{1,0:T(8,128)(2,1)}, f32[1024,256]{1,0:T(8,128)}, f32[1024,256]{1,0:T(8,128)}, bf16[2,512,...) custom-call(s32[2]{0:T(128)} %get-tuple-element.85.refs_0_, ...), custom_call_target="tpu_custom_call" | custom-call | flops 28000000000 | bytes 8000000 | tf_op jit(solution)/shard_map/attend_pairs/pallas_call | solution.py:498
  104.8 2.4 collective-permute-start.8
  107.2 3.5 collective-permute-start.9
  111.6 3.9 %cross_rows.6 = (bf16[2,512,256]{2,1,0:T(8,128)(2,1)}, bf16[2,640,256]{2,1,0:T(8,128)(2,1)}, bf16[2,640,256]{2,1,0:T(8,128)(2,1)}, s32[2]{0:T(128)}) custom-call(s32[2]{0:T(128)} %get-tuple-element.89.role, bf16[1024,1024]{1,0:T(8,128)(2,1)} %refs_3_.7, bf16[1024,1024]{1,0:T(8,128)(2,1)} %refs_4_.7, bf16[2,768,256]{2,1,0:T(8,128)(2,1)} %copy-done.12), custom_call_target="tpu_custom_call" | custom-call | tf_op jit(solution)/shard_map/cross_rows/pallas_call | solution.py:473
  115.5 4.8 %collective-permute-start.10 = (bf16[2,640,256]{2,1,0:T(8,128)(2,1)}, bf16[2,640,256]{2,1,0:T(8,128)(2,1)S(1)}, u32[]{:S(2)}, u32[]{:S(2)}) collective-permute-start(bf16[2,640,256]{2,1,0:T(8,128)(2,1)} %get-tuple-element.106), channel_id=1, source_target_pairs={{0,2},{1,3},{2,4},{3,5},{4,6},{5,7},{6,8},{7,9},{8,10},{9,11},{10,... | collective-permute-start | bytes 1966088 | tf_op jit(solution)/shard_map/ppermute | solution.py:365
  120.3 2.3 pair_rows.7
  122.6 1.9 collective-permute-start.11
  124.5 1.2 collective-permute-start.7
  125.7 52.8 %attend_pairs.5 = (bf16[1024,1024]{1,0:T(8,128)(2,1)}, bf16[1024,1024]{1,0:T(8,128)(2,1)}, f32[1024,256]{1,0:T(8,128)}, f32[1024,256]{1,0:T(8,128)}, bf16[2,512,...) custom-call(s32[2]{0:T(128)} %get-tuple-element.92.refs_0_, ...), custom_call_target="tpu_custom_call", output_to_operand_aliasing={{0}: (12, {}), {1}: (13, {})} | custom-call | flops 28000000000 | bytes 8000000 | tf_op jit(solution)/shard_map/attend_pairs/pallas_call | solution.py:498
  178.6 3.9 %collective-permute-start.12 = (bf16[2,640,256]{2,1,0:T(8,128)(2,1)}, bf16[2,640,256]{2,1,0:T(8,128)(2,1)S(1)}, u32[]{:S(2)}, u32[]{:S(2)}) collective-permute-start(bf16[2,640,256]{2,1,0:T(8,128)(2,1)} %get-tuple-element.112), channel_id=1, source_target_pairs={{2,0},{3,1},{4,2},{5,3},{6,4},{7,5},{8,6},{9,7},{10,8},{11,9},{12,... | collective-permute-start | bytes 1966088 | tf_op jit(solution)/shard_map/ppermute | solution.py:365
  182.5 3.9 %cross_rows.7 = (bf16[2,512,256]{2,1,0:T(8,128)(2,1)}, bf16[2,640,256]{2,1,0:T(8,128)(2,1)}, bf16[2,640,256]{2,1,0:T(8,128)(2,1)}, s32[2]{0:T(128)}) custom-call(s32[2]{0:T(128)} %get-tuple-element.98.role, bf16[1024,1024]{1,0:T(8,128)(2,1)} %refs_3_.7, bf16[1024,1024]{1,0:T(8,128)(2,1)} %refs_4_.7, bf16[2,768,256]{2,1,0:T(8,128)(2,1)} %copy-done.13), custom_call_target="tpu_custom_call" | custom-call | tf_op jit(solution)/shard_map/cross_rows/pallas_call | solution.py:473
  186.5 1.9 collective-permute-start.13
  188.4 4.0 %collective-permute-start.14 = (bf16[2,640,256]{2,1,0:T(8,128)(2,1)}, bf16[2,640,256]{2,1,0:T(8,128)(2,1)S(1)}, u32[]{:S(2)}, u32[]{:S(2)}) collective-permute-start(bf16[2,640,256]{2,1,0:T(8,128)(2,1)} %get-tuple-element.116), channel_id=1, source_target_pairs={{0,2},{1,3},{2,4},{3,5},{4,6},{5,7},{6,8},{7,9},{8,10},{9,11},{10,... | collective-permute-start | bytes 1966088 | tf_op jit(solution)/shard_map/ppermute | solution.py:365
  192.5 4.3 %pair_grads.4 = (bf16[2,768,256]{2,1,0:T(8,128)(2,1)}, s32[2]{0:T(128)}) custom-call(s32[2]{0:T(128)} %get-tuple-element.100.role, bf16[2,512,256]{2,1,0:T(8,128)(2,1)} %get-tuple-element.101.near, bf16[2,640,256]{2,1,0:T(8,128)(2,1)} %copy-done.6, bf16[2,640,256]{2,1,0:T(8,128)(2,1)} %copy-done.7), custom_call_target="tpu_custom_call" | custom-call | tf_op jit(solution)/shard_map/pair_grads/pallas_call | solution.py:595
  196.8 4.6 %collective-permute-start.15 = (bf16[2,640,256]{2,1,0:T(8,128)(2,1)}, bf16[2,640,256]{2,1,0:T(8,128)(2,1)}, u32[]{:S(2)}, u32[]{:S(2)}) collective-permute-start(bf16[2,640,256]{2,1,0:T(8,128)(2,1)} %get-tuple-element.117), channel_id=1, source_target_pairs={{2,0},{3,1},{4,2},{5,3},{6,4},{7,5},{8,6},{9,7},{10,8},{11,9},{12,... | collective-permute-start | bytes 1966088 | tf_op jit(solution)/shard_map/ppermute | solution.py:365
  201.3 2.0 collective-permute-start.18
  203.3 40.2 %attend_pairs.6 = (bf16[1024,1024]{1,0:T(8,128)(2,1)}, bf16[1024,1024]{1,0:T(8,128)(2,1)}, f32[1024,256]{1,0:T(8,128)}, f32[1024,256]{1,0:T(8,128)}, bf16[2,512,...) custom-call(s32[2]{0:T(128)} %get-tuple-element.104.refs_0_, ...), custom_call_target="tpu_custom_call", output_to_operand_aliasing={{0}: (12, {}), {1}: (13, {})} | custom-call | flops 28000000000 | bytes 8000000 | tf_op jit(solution)/shard_map/attend_pairs/pallas_call | solution.py:498
  243.5 4.0 %collective-permute-start.16 = (bf16[2,640,256]{2,1,0:T(8,128)(2,1)}, bf16[2,640,256]{2,1,0:T(8,128)(2,1)S(1)}, u32[]{:S(2)}, u32[]{:S(2)}) collective-permute-start(bf16[2,640,256]{2,1,0:T(8,128)(2,1)} %get-tuple-element.124), channel_id=1, source_target_pairs={{2,0},{3,1},{4,2},{5,3},{6,4},{7,5},{8,6},{9,7},{10,8},{11,9},{12,... | collective-permute-start | bytes 1966088 | tf_op jit(solution)/shard_map/ppermute | solution.py:365
  247.5 1.9 collective-permute-start.17
  249.5 4.3 %pair_grads.5 = (bf16[2,768,256]{2,1,0:T(8,128)(2,1)}, s32[2]{0:T(128)}) custom-call(s32[2]{0:T(128)} %get-tuple-element.110.role, bf16[2,512,256]{2,1,0:T(8,128)(2,1)} %get-tuple-element.111.near, bf16[2,640,256]{2,1,0:T(8,128)(2,1)} %copy-done, bf16[2,640,256]{2,1,0:T(8,128)(2,1)} %copy-done.1), custom_call_target="tpu_custom_call" | custom-call | tf_op jit(solution)/shard_map/pair_grads/pallas_call | solution.py:595
  254.6 52.6 %attend_pairs.7 = (bf16[1024,1024]{1,0:T(8,128)(2,1)}, bf16[1024,1024]{1,0:T(8,128)(2,1)}, f32[1024,256]{1,0:T(8,128)}, f32[1024,256]{1,0:T(8,128)}, bf16[2,512,...) custom-call(s32[2]{0:T(128)} %get-tuple-element.114.refs_0_, ...), custom_call_target="tpu_custom_call", output_to_operand_aliasing={{0}: (12, {}), {1}: (13, {})} | custom-call | flops 28000000000 | bytes 8000000 | tf_op jit(solution)/shard_map/attend_pairs/pallas_call | solution.py:498
  307.3 6.7 %collective-permute-start.19 = (bf16[2,640,256]{2,1,0:T(8,128)(2,1)}, bf16[2,640,256]{2,1,0:T(8,128)(2,1)S(1)}, u32[]{:S(2)}, u32[]{:S(2)}) collective-permute-start(bf16[2,640,256]{2,1,0:T(8,128)(2,1)} %get-tuple-element.132), channel_id=1, source_target_pairs={{2,0},{3,1},{4,2},{5,3},{6,4},{7,5},{8,6},{9,7},{10,8},{11,9},{12,... | collective-permute-start | bytes 1966088 | tf_op jit(solution)/shard_map/ppermute | solution.py:365
  313.9 1.9 collective-permute-start.20
  315.9 1.3 collective-permute-start.21
  318.1 4.3 %pair_grads.6 = (bf16[2,768,256]{2,1,0:T(8,128)(2,1)}, s32[2]{0:T(128)}) custom-call(s32[2]{0:T(128)} %get-tuple-element.122.role, bf16[2,512,256]{2,1,0:T(8,128)(2,1)} %get-tuple-element.123.near, bf16[2,640,256]{2,1,0:T(8,128)(2,1)} %copy-done.2, bf16[2,640,256]{2,1,0:T(8,128)(2,1)} %copy-done.3), custom_call_target="tpu_custom_call" | custom-call | tf_op jit(solution)/shard_map/pair_grads/pallas_call | solution.py:595
  324.1 4.8 %sum_grads.4 = (bf16[1024,1024]{1,0:T(8,128)(2,1)}, bf16[1024,1024]{1,0:T(8,128)(2,1)}, s32[2]{0:T(128)}) custom-call(s32[2]{0:T(128)} %get-tuple-element.126.refs_0_, f32[1024,256]{1,0:T(8,128)} %get-tuple-element.127.refs_1_, f32[1024,256]{1,0:T(8,128)} %get-tuple-element.128.refs_2_, bf16[2,640,256]{2,1,0:T(8,128)(2,1)} %copy-done.6, ...), custom_call_target="tpu_custom_call" | custom-call | tf_op jit(solution)/shard_map/sum_grads/pallas_call | solution.py:643
  328.9 1.9 collective-permute-done.20.below.refs_4_
  331.7 4.3 %pair_grads.7 = (bf16[2,768,256]{2,1,0:T(8,128)(2,1)}, s32[2]{0:T(128)}) custom-call(s32[2]{0:T(128)} %get-tuple-element.130.role, bf16[2,512,256]{2,1,0:T(8,128)(2,1)} %get-tuple-element.131.near, bf16[2,640,256]{2,1,0:T(8,128)(2,1)} %copy-done.4, bf16[2,640,256]{2,1,0:T(8,128)(2,1)} %copy-done.5), custom_call_target="tpu_custom_call" | custom-call | tf_op jit(solution)/shard_map/pair_grads/pallas_call | solution.py:595
  336.0 1.3 collective-permute-start.23
  337.3 4.8 %sum_grads.5 = (bf16[1024,1024]{1,0:T(8,128)(2,1)}, bf16[1024,1024]{1,0:T(8,128)(2,1)}, s32[2]{0:T(128)}) custom-call(s32[2]{0:T(128)} %get-tuple-element.134.refs_0_, f32[1024,256]{1,0:T(8,128)} %get-tuple-element.135.refs_1_, f32[1024,256]{1,0:T(8,128)} %get-tuple-element.136.refs_2_, ...), custom_call_target="tpu_custom_call", output_to_operand_aliasing={{0}: (6, {}), {1}: (7, {})} | custom-call | tf_op jit(solution)/shard_map/sum_grads/pallas_call | solution.py:643
  342.2 11.2 %collective-permute-done.22.refs_5_ = bf16[2,768,256]{2,1,0:T(8,128)(2,1)S(1)} collective-permute-done((bf16[2,768,256]{2,1,0:T(8,128)(2,1)}, bf16[2,768,256]{2,1,0:T(8,128)(2,1)S(1)}, u32[]{:S(2)}, u32[]{:S(2)}) %collective-permute-start.22) | collective-permute-done | bytes 786464 | tf_op jit(solution)/shard_map/ppermute | solution.py:365
  354.3 4.8 %sum_grads.6 = (bf16[1024,1024]{1,0:T(8,128)(2,1)}, bf16[1024,1024]{1,0:T(8,128)(2,1)}, s32[2]{0:T(128)}) custom-call(s32[2]{0:T(128)} %get-tuple-element.140.refs_0_, f32[1024,256]{1,0:T(8,128)} %get-tuple-element.141.refs_1_, f32[1024,256]{1,0:T(8,128)} %get-tuple-element.142.refs_2_, ...), custom_call_target="tpu_custom_call", output_to_operand_aliasing={{0}: (6, {}), {1}: (7, {})} | custom-call | tf_op jit(solution)/shard_map/sum_grads/pallas_call | solution.py:643
  359.1 10.4 %collective-permute-done.23.refs_5_ = bf16[2,768,256]{2,1,0:T(8,128)(2,1)S(1)} collective-permute-done((bf16[2,768,256]{2,1,0:T(8,128)(2,1)}, bf16[2,768,256]{2,1,0:T(8,128)(2,1)S(1)}, u32[]{:S(2)}, u32[]{:S(2)}) %collective-permute-start.23) | collective-permute-done | bytes 786464 | tf_op jit(solution)/shard_map/ppermute | solution.py:365
  370.5 4.8 %sum_grads.7 = (bf16[1024,1024]{1,0:T(8,128)(2,1)}, bf16[1024,1024]{1,0:T(8,128)(2,1)}, s32[2]{0:T(128)}) custom-call(s32[2]{0:T(128)} %get-tuple-element.146.refs_0_, f32[1024,256]{1,0:T(8,128)} %get-tuple-element.147.refs_1_, f32[1024,256]{1,0:T(8,128)} %get-tuple-element.148.refs_2_, ...), custom_call_target="tpu_custom_call", output_to_operand_aliasing={{0}: (6, {}), {1}: (7, {})} | custom-call | tf_op jit(solution)/shard_map/sum_grads/pallas_call | solution.py:643
  (65 shorter events, 11.1 us)
Async XLA Ops:
  3.5 19.7 %collective-permute-start = (bf16[2,768,256]{2,1,0:T(8,128)(2,1)}, bf16[2,768,256]{2,1,0:T(8,128)(2,1)S(1)}, u32[]{:S(2)}, u32[]{:S(2)}) collective-permute-start(bf16[2,768,256]{2,1,0:T(8,128)(2,1)} %get-tuple-element.80), channel_id=1, source_target_pairs={{0,1},{1,0},{2,3},{3,2},{4,5},{5,4},{6,7},{7,6},{8,9},{9,8},{10,11... | collective-permute-start | bytes 2359304 | tf_op jit(solution)/shard_map/ppermute | solution.py:365
  23.2 0.9 copy-start.14
  27.9 4.1 %copy-start.18 = (bf16[2,640,256]{2,1,0:T(8,128)(2,1)S(1)}, bf16[2,640,256]{2,1,0:T(8,128)(2,1)}, u32[]{:S(2)}) copy-start(bf16[2,640,256]{2,1,0:T(8,128)(2,1)} %get-tuple-element.87) | copy-start | bytes 1966084
  27.9 7.3 %copy-start.15 = (bf16[2,640,256]{2,1,0:T(8,128)(2,1)S(1)}, bf16[2,640,256]{2,1,0:T(8,128)(2,1)}, u32[]{:S(2)}) copy-start(bf16[2,640,256]{2,1,0:T(8,128)(2,1)} %get-tuple-element.88) | copy-start | bytes 1966084
  30.3 18.8 %collective-permute-start.1 = (bf16[2,768,256]{2,1,0:T(8,128)(2,1)}, bf16[2,768,256]{2,1,0:T(8,128)(2,1)S(1)}, u32[]{:S(2)}, u32[]{:S(2)}) collective-permute-start(bf16[2,768,256]{2,1,0:T(8,128)(2,1)} %get-tuple-element.83), channel_id=1, source_target_pairs={{0,1},{1,0},{2,3},{3,2},{4,5},{5,4},{6,7},{7,6},{8,9},{9,8},{10,11... | collective-permute-start | bytes 2359304 | tf_op jit(solution)/shard_map/ppermute | solution.py:365
  32.0 31.5 %collective-permute-start.2 = (bf16[2,640,256]{2,1,0:T(8,128)(2,1)S(1)}, bf16[2,640,256]{2,1,0:T(8,128)(2,1)S(1)}, u32[]{:S(2)}, u32[]{:S(2)}) collective-permute-start(bf16[2,640,256]{2,1,0:T(8,128)(2,1)S(1)} %copy-done.18), channel_id=1, source_target_pairs={{0,2},{1,3},{2,4},{3,5},{4,6},{5,7},{6,8},{7,9},{8,10},{9,11},{10,... | collective-permute-start | bytes 1966088 | tf_op jit(solution)/shard_map/ppermute | solution.py:365
  35.2 28.3 %collective-permute-start.3 = (bf16[2,640,256]{2,1,0:T(8,128)(2,1)S(1)}, bf16[2,640,256]{2,1,0:T(8,128)(2,1)S(1)}, u32[]{:S(2)}, u32[]{:S(2)}) collective-permute-start(bf16[2,640,256]{2,1,0:T(8,128)(2,1)S(1)} %copy-done.15), channel_id=1, source_target_pairs={{2,0},{3,1},{4,2},{5,3},{6,4},{7,5},{8,6},{9,7},{10,8},{11,9},{12,... | collective-permute-start | bytes 1966088 | tf_op jit(solution)/shard_map/ppermute | solution.py:365
  49.1 0.9 copy-start.9
  53.9 68.7 %collective-permute-start.5 = (bf16[2,640,256]{2,1,0:T(8,128)(2,1)}, bf16[2,640,256]{2,1,0:T(8,128)(2,1)}, u32[]{:S(2)}, u32[]{:S(2)}) collective-permute-start(bf16[2,640,256]{2,1,0:T(8,128)(2,1)} %get-tuple-element.94), channel_id=1, source_target_pairs={{0,2},{1,3},{2,4},{3,5},{4,6},{5,7},{6,8},{7,9},{8,10},{9,11},{10,... | collective-permute-start | bytes 1966088 | tf_op jit(solution)/shard_map/ppermute | solution.py:365
  57.5 67.0 %collective-permute-start.6 = (bf16[2,640,256]{2,1,0:T(8,128)(2,1)}, bf16[2,640,256]{2,1,0:T(8,128)(2,1)}, u32[]{:S(2)}, u32[]{:S(2)}) collective-permute-start(bf16[2,640,256]{2,1,0:T(8,128)(2,1)} %get-tuple-element.95), channel_id=1, source_target_pairs={{2,0},{3,1},{4,2},{5,3},{6,4},{7,5},{8,6},{9,7},{10,8},{11,9},{12,... | collective-permute-start | bytes 1966088 | tf_op jit(solution)/shard_map/ppermute | solution.py:365
  62.0 48.7 %collective-permute-start.4 = (bf16[2,768,256]{2,1,0:T(8,128)(2,1)}, bf16[2,768,256]{2,1,0:T(8,128)(2,1)S(1)}, u32[]{:S(2)}, u32[]{:S(2)}) collective-permute-start(bf16[2,768,256]{2,1,0:T(8,128)(2,1)} %get-tuple-element.90), channel_id=1, source_target_pairs={{0,1},{1,0},{2,3},{3,2},{4,5},{5,4},{6,7},{7,6},{8,9},{9,8},{10,11... | collective-permute-start | bytes 2359304 | tf_op jit(solution)/shard_map/ppermute | solution.py:365
  63.5 0.9 copy-start.16
  63.6 1.1 copy-start.19
  104.8 81.6 %collective-permute-start.8 = (bf16[2,640,256]{2,1,0:T(8,128)(2,1)}, bf16[2,640,256]{2,1,0:T(8,128)(2,1)S(1)}, u32[]{:S(2)}, u32[]{:S(2)}) collective-permute-start(bf16[2,640,256]{2,1,0:T(8,128)(2,1)} %get-tuple-element.102), channel_id=1, source_target_pairs={{2,0},{3,1},{4,2},{5,3},{6,4},{7,5},{8,6},{9,7},{10,8},{11,9},{12,... | collective-permute-start | bytes 1966088 | tf_op jit(solution)/shard_map/ppermute | solution.py:365
  107.2 81.2 %collective-permute-start.9 = (bf16[2,640,256]{2,1,0:T(8,128)(2,1)}, bf16[2,640,256]{2,1,0:T(8,128)(2,1)S(1)}, u32[]{:S(2)}, u32[]{:S(2)}) collective-permute-start(bf16[2,640,256]{2,1,0:T(8,128)(2,1)} %get-tuple-element.103), channel_id=1, source_target_pairs={{0,2},{1,3},{2,4},{3,5},{4,6},{5,7},{6,8},{7,9},{8,10},{9,11},{10,... | collective-permute-start | bytes 1966088 | tf_op jit(solution)/shard_map/ppermute | solution.py:365
  110.7 0.9 copy-start.12
  115.5 81.3 %collective-permute-start.10 = (bf16[2,640,256]{2,1,0:T(8,128)(2,1)}, bf16[2,640,256]{2,1,0:T(8,128)(2,1)S(1)}, u32[]{:S(2)}, u32[]{:S(2)}) collective-permute-start(bf16[2,640,256]{2,1,0:T(8,128)(2,1)} %get-tuple-element.106), channel_id=1, source_target_pairs={{0,2},{1,3},{2,4},{3,5},{4,6},{5,7},{6,8},{7,9},{8,10},{9,11},{10,... | collective-permute-start | bytes 1966088 | tf_op jit(solution)/shard_map/ppermute | solution.py:365
  122.6 78.7 %collective-permute-start.11 = (bf16[2,640,256]{2,1,0:T(8,128)(2,1)}, bf16[2,640,256]{2,1,0:T(8,128)(2,1)}, u32[]{:S(2)}, u32[]{:S(2)}) collective-permute-start(bf16[2,640,256]{2,1,0:T(8,128)(2,1)} %get-tuple-element.107), channel_id=1, source_target_pairs={{2,0},{3,1},{4,2},{5,3},{6,4},{7,5},{8,6},{9,7},{10,8},{11,9},{12,... | collective-permute-start | bytes 1966088 | tf_op jit(solution)/shard_map/ppermute | solution.py:365
  124.5 54.1 %collective-permute-start.7 = (bf16[2,768,256]{2,1,0:T(8,128)(2,1)}, bf16[2,768,256]{2,1,0:T(8,128)(2,1)S(1)}, u32[]{:S(2)}, u32[]{:S(2)}) collective-permute-start(bf16[2,768,256]{2,1,0:T(8,128)(2,1)} %get-tuple-element.99), channel_id=1, source_target_pairs={{0,1},{1,0},{2,3},{3,2},{4,5},{5,4},{6,7},{7,6},{8,9},{9,8},{10,11... | collective-permute-start | bytes 2359304 | tf_op jit(solution)/shard_map/ppermute | solution.py:365
  178.6 3.9 %copy-start.13 = (bf16[2,768,256]{2,1,0:T(8,128)(2,1)}, bf16[2,768,256]{2,1,0:T(8,128)(2,1)S(1)}, u32[]{:S(2)}) copy-start(bf16[2,768,256]{2,1,0:T(8,128)(2,1)S(1)} %collective-permute-done.7.p) | copy-start | bytes 2359300
  178.6 64.9 %collective-permute-start.12 = (bf16[2,640,256]{2,1,0:T(8,128)(2,1)}, bf16[2,640,256]{2,1,0:T(8,128)(2,1)S(1)}, u32[]{:S(2)}, u32[]{:S(2)}) collective-permute-start(bf16[2,640,256]{2,1,0:T(8,128)(2,1)} %get-tuple-element.112), channel_id=1, source_target_pairs={{2,0},{3,1},{4,2},{5,3},{6,4},{7,5},{8,6},{9,7},{10,8},{11,9},{12,... | collective-permute-start | bytes 1966088 | tf_op jit(solution)/shard_map/ppermute | solution.py:365
  186.5 6.0 %copy-start.6 = (bf16[2,640,256]{2,1,0:T(8,128)(2,1)}, bf16[2,640,256]{2,1,0:T(8,128)(2,1)S(1)}, u32[]{:S(2)}) copy-start(bf16[2,640,256]{2,1,0:T(8,128)(2,1)S(1)} %collective-permute-done.8.above.refs_3_) | copy-start | bytes 1966084
  186.5 61.0 %collective-permute-start.13 = (bf16[2,640,256]{2,1,0:T(8,128)(2,1)}, bf16[2,640,256]{2,1,0:T(8,128)(2,1)S(1)}, u32[]{:S(2)}, u32[]{:S(2)}) collective-permute-start(bf16[2,640,256]{2,1,0:T(8,128)(2,1)} %get-tuple-element.113), channel_id=1, source_target_pairs={{0,2},{1,3},{2,4},{3,5},{4,6},{5,7},{6,8},{7,9},{8,10},{9,11},{10,... | collective-permute-start | bytes 1966088 | tf_op jit(solution)/shard_map/ppermute | solution.py:365
  188.4 4.0 %copy-start.7 = (bf16[2,640,256]{2,1,0:T(8,128)(2,1)}, bf16[2,640,256]{2,1,0:T(8,128)(2,1)S(1)}, u32[]{:S(2)}) copy-start(bf16[2,640,256]{2,1,0:T(8,128)(2,1)S(1)} %collective-permute-done.9.below.refs_4_) | copy-start | bytes 1966084
  188.4 65.4 %collective-permute-start.14 = (bf16[2,640,256]{2,1,0:T(8,128)(2,1)}, bf16[2,640,256]{2,1,0:T(8,128)(2,1)S(1)}, u32[]{:S(2)}, u32[]{:S(2)}) collective-permute-start(bf16[2,640,256]{2,1,0:T(8,128)(2,1)} %get-tuple-element.116), channel_id=1, source_target_pairs={{0,2},{1,3},{2,4},{3,5},{4,6},{5,7},{6,8},{7,9},{8,10},{9,11},{10,... | collective-permute-start | bytes 1966088 | tf_op jit(solution)/shard_map/ppermute | solution.py:365
  196.8 6.6 %copy-start.17 = (bf16[2,640,256]{2,1,0:T(8,128)(2,1)}, bf16[2,640,256]{2,1,0:T(8,128)(2,1)S(1)}, u32[]{:S(2)}) copy-start(bf16[2,640,256]{2,1,0:T(8,128)(2,1)S(1)} %collective-permute-done.10.refs_8_.refs_9_) | copy-start | bytes 1966084
  196.8 57.1 %collective-permute-start.15 = (bf16[2,640,256]{2,1,0:T(8,128)(2,1)}, bf16[2,640,256]{2,1,0:T(8,128)(2,1)}, u32[]{:S(2)}, u32[]{:S(2)}) collective-permute-start(bf16[2,640,256]{2,1,0:T(8,128)(2,1)} %get-tuple-element.117), channel_id=1, source_target_pairs={{2,0},{3,1},{4,2},{5,3},{6,4},{7,5},{8,6},{9,7},{10,8},{11,9},{12,... | collective-permute-start | bytes 1966088 | tf_op jit(solution)/shard_map/ppermute | solution.py:365
  201.3 121.8 %collective-permute-start.18 = (bf16[2,768,256]{2,1,0:T(8,128)(2,1)}, bf16[2,768,256]{2,1,0:T(8,128)(2,1)S(1)}, u32[]{:S(2)}, u32[]{:S(2)}) collective-permute-start(bf16[2,768,256]{2,1,0:T(8,128)(2,1)} %get-tuple-element.129), channel_id=1, source_target_pairs={{0,1},{1,0},{2,3},{3,2},{4,5},{5,4},{6,7},{7,6},{8,9},{9,8},{10,11... | collective-permute-start | bytes 2359304 | tf_op jit(solution)/shard_map/ppermute | solution.py:365
  243.5 6.0 %copy-start = (bf16[2,640,256]{2,1,0:T(8,128)(2,1)}, bf16[2,640,256]{2,1,0:T(8,128)(2,1)S(1)}, u32[]{:S(2)}) copy-start(bf16[2,640,256]{2,1,0:T(8,128)(2,1)S(1)} %collective-permute-done.12.above.refs_3_) | copy-start | bytes 1966084
  243.5 72.4 %collective-permute-start.16 = (bf16[2,640,256]{2,1,0:T(8,128)(2,1)}, bf16[2,640,256]{2,1,0:T(8,128)(2,1)S(1)}, u32[]{:S(2)}, u32[]{:S(2)}) collective-permute-start(bf16[2,640,256]{2,1,0:T(8,128)(2,1)} %get-tuple-element.124), channel_id=1, source_target_pairs={{2,0},{3,1},{4,2},{5,3},{6,4},{7,5},{8,6},{9,7},{10,8},{11,9},{12,... | collective-permute-start | bytes 1966088 | tf_op jit(solution)/shard_map/ppermute | solution.py:365
  247.5 1.9 copy-start.1
  247.5 69.7 %collective-permute-start.17 = (bf16[2,640,256]{2,1,0:T(8,128)(2,1)}, bf16[2,640,256]{2,1,0:T(8,128)(2,1)S(1)}, u32[]{:S(2)}, u32[]{:S(2)}) collective-permute-start(bf16[2,640,256]{2,1,0:T(8,128)(2,1)} %get-tuple-element.125), channel_id=1, source_target_pairs={{0,2},{1,3},{2,4},{3,5},{4,6},{5,7},{6,8},{7,9},{8,10},{9,11},{10,... | collective-permute-start | bytes 1966088 | tf_op jit(solution)/shard_map/ppermute | solution.py:365
  253.8 0.8 copy-start.20
  307.3 21.6 %collective-permute-start.19 = (bf16[2,640,256]{2,1,0:T(8,128)(2,1)}, bf16[2,640,256]{2,1,0:T(8,128)(2,1)S(1)}, u32[]{:S(2)}, u32[]{:S(2)}) collective-permute-start(bf16[2,640,256]{2,1,0:T(8,128)(2,1)} %get-tuple-element.132), channel_id=1, source_target_pairs={{2,0},{3,1},{4,2},{5,3},{6,4},{7,5},{8,6},{9,7},{10,8},{11,9},{12,... | collective-permute-start | bytes 1966088 | tf_op jit(solution)/shard_map/ppermute | solution.py:365
  313.9 16.9 %collective-permute-start.20 = (bf16[2,640,256]{2,1,0:T(8,128)(2,1)}, bf16[2,640,256]{2,1,0:T(8,128)(2,1)S(1)}, u32[]{:S(2)}, u32[]{:S(2)}) collective-permute-start(bf16[2,640,256]{2,1,0:T(8,128)(2,1)} %get-tuple-element.133), channel_id=1, source_target_pairs={{0,2},{1,3},{2,4},{3,5},{4,6},{5,7},{6,8},{7,9},{8,10},{9,11},{10,... | collective-permute-start | bytes 1966088 | tf_op jit(solution)/shard_map/ppermute | solution.py:365
  315.9 1.4 copy-start.2
  315.9 21.5 %collective-permute-start.21 = (bf16[2,768,256]{2,1,0:T(8,128)(2,1)}, bf16[2,768,256]{2,1,0:T(8,128)(2,1)}, u32[]{:S(2)}, u32[]{:S(2)}) collective-permute-start(bf16[2,768,256]{2,1,0:T(8,128)(2,1)} %get-tuple-element.137), channel_id=1, source_target_pairs={{0,1},{1,0},{2,3},{3,2},{4,5},{5,4},{6,7},{7,6},{8,9},{9,8},{10,11... | collective-permute-start | bytes 2359304 | tf_op jit(solution)/shard_map/ppermute | solution.py:365
  317.2 0.9 copy-start.3
  322.4 31.0 %collective-permute-start.22 = (bf16[2,768,256]{2,1,0:T(8,128)(2,1)}, bf16[2,768,256]{2,1,0:T(8,128)(2,1)S(1)}, u32[]{:S(2)}, u32[]{:S(2)}) collective-permute-start(bf16[2,768,256]{2,1,0:T(8,128)(2,1)} %get-tuple-element.143), channel_id=1, source_target_pairs={{0,1},{1,0},{2,3},{3,2},{4,5},{5,4},{6,7},{7,6},{8,9},{9,8},{10,11... | collective-permute-start | bytes 2359304 | tf_op jit(solution)/shard_map/ppermute | solution.py:365
  323.2 0.9 copy-start.8
  328.9 1.9 copy-start.4
  330.8 0.9 copy-start.5
  336.0 33.5 %collective-permute-start.23 = (bf16[2,768,256]{2,1,0:T(8,128)(2,1)}, bf16[2,768,256]{2,1,0:T(8,128)(2,1)S(1)}, u32[]{:S(2)}, u32[]{:S(2)}) collective-permute-start(bf16[2,768,256]{2,1,0:T(8,128)(2,1)} %get-tuple-element.149), channel_id=1, source_target_pairs={{0,1},{1,0},{2,3},{3,2},{4,5},{5,4},{6,7},{7,6},{8,9},{9,8},{10,11... | collective-permute-start | bytes 2359304 | tf_op jit(solution)/shard_map/ppermute | solution.py:365
  353.4 0.9 copy-start.10
  369.6 0.9 copy-start.11

commit v3 on v2

v3 whole, which is shorter than its diff:
```python
import math

import jax
import jax.numpy as jnp
from jax import lax
from jax.experimental import pallas as pl
from jax.experimental.pallas import tpu as pltpu
from jax.sharding import PartitionSpec as P

HEAD_DIM = 64
BLOCK = 256
HALF = 128
PAIR = 128
AXES = ("seqa", "seqb")
GROUPS = (1, 2, 3, 2)
ORDER = (
    ("pair", 0), ("cross", 0), ("pair", 1), ("cross", 1), ("pair", 2),
    ("attend", 0), ("cross", 2), ("pair", 3),
    ("attend", 1), ("cross", 3), ("back", 0),
    ("attend", 2), ("back", 1),
    ("attend", 3), ("back", 2), ("sum", 0), ("back", 3), ("sum", 1), ("sum", 2), ("sum", 3),
)
LIMIT = 60
LOG2E = math.log2(math.e)
BF16 = jnp.bfloat16
F32 = jnp.float32
NT = (((1,), (1,)), ((), ()))
NN = (((1,), (0,)), ((), ()))

BASE = (0, 1536, 2560, 3072)
ROWS = 3456

PIECES = ((768, 0), (384, 768), (384, 1152), (384, 1536))


def piece_starts(b):
    half = b // 2
    first = BASE[1] + half * 512 + (1 - (b - 2 * half)) * 128
    rows = (b * 256, first, BASE[2] + half * 128, BASE[3])
    return [r if isinstance(r, int) else pl.multiple_of(r, 128) for r in rows]


def dot(a, b, dims=NN):
    return lax.dot_general(a, b, dims, preferred_element_type=F32)


def mean_rows(ref, start, count, stride):
    total = ref[pl.ds(start, count, stride=stride), :]
    for i in range(1, stride):
        total = total + ref[pl.ds(start + i, count, stride=stride), :]
    return (total * (1.0 / stride)).astype(BF16)


def add_rows(ref, start, rows, stride):
    if stride == 1:
        at = slice(start, start + rows.shape[0])
        ref[at] = ref[at] + rows.astype(F32)
    else:
        spread_rows(ref, start, rows.astype(F32), stride)


def spread_rows(ref, start, rows, stride):
    for i in range(stride):
        at = pl.ds(start + i, rows.shape[0], stride=stride)
        ref[at, :] = ref[at, :] + rows


def attend_kernel(
    role, valid, q, k, v, do, hk, hv, bk, bv, ak, av,
    o, dq, gk, gv, rh, rup, rdown, token,
    kext, vext, kt, vt, e, x, qz, doz, qs, dos, acck, accv, inn, rls, ftmp, gtmp,
    cross, small, side, flag, oks,
):
    lane = lax.broadcasted_iota(jnp.int32, (256, PAIR), 1)
    first = lane < HEAD_DIM
    even = role[0] == 0
    odd = jnp.logical_not(even)
    pass_on(role, token)

    for which, (h, b, a) in enumerate(((hk, bk, ak), (hv, bv, av))):

        @pl.when(even)
        def _():
            cross[which] = b[...]
            small[which] = a[0:256]
            side[0, which] = b[0:512]
            side[1, which] = h[...]

        @pl.when(odd)
        def _():
            cross[which] = a[...]
            small[which] = b[0:256]
            side[0, which] = h[...]
            side[1, which] = a[0:512]

    for which, own, ext in ((0, k, kext), (1, v, vext)):
        low, up = side.at[0, which], side.at[1, which]
        ext[0:256] = low[0:256]
        ext[256:1280] = own[...]
        ext[1280:1536] = up[0:256]
        ftmp[...] = own[...].astype(F32)
        spans = mean_rows(ftmp, 0, 512, 2)
        b1 = BASE[1]
        ext[b1 + 256 : b1 + 384] = spans[384:512]
        ext[b1 + 384 : b1 + 512] = spans[256:384]
        ext[b1 + 512 : b1 + 640] = spans[128:256]
        ext[b1 + 640 : b1 + 768] = spans[0:128]
        ext[b1 + 128 : b1 + 256] = low[256:384]
        ext[b1 + 768 : b1 + 896] = up[256:384]
        b2 = BASE[2]
        ftmp[0:384] = low[0:384].astype(F32)
        ext[b1 : b1 + 128] = mean_rows(ftmp, 0, 128, 2)
        ext[b2 + 384 : b2 + 448] = mean_rows(ftmp, 256, 64, 2)
        ext[b2 + 448 : b2 + 512] = mean_rows(ftmp, 0, 64, 4)
        ftmp[0:384] = up[0:384].astype(F32)
        ext[b1 + 896 : b1 + 1024] = mean_rows(ftmp, 0, 128, 2)
        ext[b2 : b2 + 64] = mean_rows(ftmp, 0, 64, 4)
        ext[b2 + 64 : b2 + 128] = mean_rows(ftmp, 256, 64, 2)
        ext[b2 + 128 : b2 + 256] = low[384:512]
        ext[b2 + 256 : b2 + 384] = up[384:512]
        ext[BASE[3] : BASE[3] + 128] = cross[which, 512:640]
        ext[BASE[3] + 128 : ROWS] = small[which]

    low_ok, up_ok = valid[0], valid[1]
    for level, row, rows, ok in (
        (0, 0, 256, low_ok), (0, 256, 1024, 1.0), (0, 1280, 256, up_ok),
        (1, 0, 256, low_ok), (1, 256, 512, 1.0), (1, 768, 256, up_ok),
        (2, 0, 128, up_ok), (2, 128, 128, low_ok), (2, 256, 128, up_ok), (2, 384, 128, low_ok),
        (3, 0, 128, valid[2]), (3, 128, 128, valid[3]), (3, 256, 128, valid[4]),
    ):
        at = slice(BASE[level] + row, BASE[level] + row + rows)
        for i in range(at.start // 128, at.stop // 128):
            oks[i] = ok
        scale = float(2**level)
        kt[:, at] = (kext[at] * scale).astype(BF16).T
        vals = (vext[at] * scale).astype(BF16).T
        top = lax.broadcasted_iota(jnp.int32, (16, rows), 0) == 0
        ones = jnp.where(top, ok * scale, 0.0).astype(BF16)
        for h in range(2):
            vt[h, 0:64, at] = vals[h * 64 : h * 64 + 64]
            vt[h, 64:80, at] = ones

    acck[...] = jnp.zeros_like(acck)
    accv[...] = jnp.zeros_like(accv)

    def block_step(b, carry):
        at = pl.ds(pl.multiple_of(b * 256, 256), 256)
        starts = piece_starts(b)
        spots = [(pl.ds(r, n), slice(to, to + n)) for r, (n, to) in zip(starts, PIECES)]
        query, grad = q[at].astype(F32), do[at].astype(F32)
        heads = (slice(0, 256), slice(256, 512))
        for h in range(2):
            mine = first if h == 0 else ~first
            qz[heads[h]] = jnp.where(mine, query * 0.125, 0.0).astype(BF16)
            doz[heads[h]] = jnp.where(mine, grad, 0.0).astype(BF16)

        for rows, to in spots:
            for h in heads:
                s = dot(kext[rows], qz[h], NT)
                e[to, h] = jnp.exp2(s * LOG2E).astype(BF16)

        def forward():
            outs, recips = [], []
            least, most = None, None
            for h in range(2):
                acc = jnp.zeros((80, 256), F32)
                for rows, to in spots:
                    acc = acc + dot(vt[h, :, rows], e[to, heads[h]])
                total = acc[64:65]
                least = total if least is None else jnp.minimum(least, total)
                most = total if most is None else jnp.maximum(most, total)
                recip = 1.0 / total
                outs.append(acc[0:64] * recip)
                recips.append(recip)
            fine = (jnp.min(least) > 2.0**-60) & (jnp.max(most) < 2.0**60)
            flag[0] = jnp.where(fine, 0, 1)
            return outs, recips

        def settle(outs, recips):
            mixed = jnp.concatenate(outs, 0)
            o[at] = mixed.T.astype(BF16)
            prod = mixed.astype(BF16).astype(F32) * grad.T
            wide = jnp.concatenate([jnp.broadcast_to(r, (64, 256)) for r in recips], 0).T
            for h in range(2):
                inn[0:1, heads[h]] = jnp.sum(prod[h * 64 : h * 64 + 64], axis=0, keepdims=True)
                rls[0:1, heads[h]] = recips[h]
                mine = first if h == 0 else ~first
                dos[heads[h]] = jnp.where(mine, grad * wide, 0.0).astype(BF16)
                qs[heads[h]] = jnp.where(mine, query * (wide * 0.125), 0.0).astype(BF16)

        settle(*forward())

        @pl.when(flag[0] == 1)
        def _():
            for h in heads:

                def scores(row):
                    row = pl.multiple_of(row, 128)
                    s = dot(kext[pl.ds(row, 128)], qz[h], NT) * LOG2E
                    return jnp.where(oks[row // 128] > 0.5, s, -jnp.inf)

                highest = jnp.full((1, 256), -jnp.inf, F32)
                for r, (n, to) in zip(starts, PIECES):
                    highest = lax.fori_loop(
                        0,
                        n // 128,
                        lambda t, top: jnp.maximum(
                            top, jnp.max(scores(r + t * 128), axis=0, keepdims=True)
                        ),
                        highest,
                    )
                for r, (n, to) in zip(starts, PIECES):

                    def again(t, carry):
                        put = pl.ds(pl.multiple_of(to + t * 128, 128), 128)
                        e[put, h] = jnp.exp2(scores(r + t * 128) - highest).astype(BF16)
                        return carry

                    lax.fori_loop(0, n // 128, again, 0)
            settle(*forward())

        for rows, to in spots:
            for h in heads:
                dp = dot(vext[rows], doz[h], NT) - inn[0:1, h]
                x[to, h] = e[to, h] * dp.astype(BF16)

        outs = []
        for h in range(2):
            acc = jnp.zeros((64, 256), F32)
            for rows, to in spots:
                acc = acc + dot(kt[h * 64 : h * 64 + 64, rows], x[to, heads[h]])
            outs.append(acc * (rls[0:1, heads[h]] * 0.125))
        dq[at] = jnp.concatenate(outs, 0).T.astype(BF16)

        for rows, to in spots:
            acck[rows] = acck[rows] + dot(x[to], qs[...])
            accv[rows] = accv[rows] + dot(e[to], dos[...])
        return carry

    lax.fori_loop(0, 4, block_step, 0)

    b1, b2, b3 = BASE[1:]
    for which, acc, own in ((0, acck, gk), (1, accv, gv)):
        low, up = side.at[0, which], side.at[1, which]
        own[...] = acc[256:1280]
        for i, row in enumerate((640, 512, 384, 256)):
            spread_rows(own, i * 256, acc[b1 + row : b1 + row + 128], 2)
        gtmp[0:256] = acc[0:256]
        spread_rows(gtmp, 0, acc[b1 : b1 + 128], 2)
        spread_rows(gtmp, 0, acc[b2 + 448 : b2 + 512], 4)
        gtmp[256:384] = acc[b1 + 128 : b1 + 256]
        spread_rows(gtmp, 256, acc[b2 + 384 : b2 + 448], 2)
        gtmp[384:640] = acc[1280:1536]
        spread_rows(gtmp, 384, acc[b1 + 896 : b1 + 1024], 2)
        spread_rows(gtmp, 384, acc[b2 : b2 + 64], 4)
        gtmp[640:768] = acc[b1 + 768 : b1 + 896]
        spread_rows(gtmp, 640, acc[b2 + 64 : b2 + 128], 2)
        low[0:384] = gtmp[0:384].astype(BF16)
        up[0:384] = gtmp[384:768].astype(BF16)
        low[384:512] = acc[b2 + 128 : b2 + 256].astype(BF16)
        up[384:512] = acc[b2 + 256 : b2 + 384].astype(BF16)
        cross[which, 512:640] = acc[b3 : b3 + 128].astype(BF16)
        small[which] = acc[b3 + 128 : ROWS].astype(BF16)

        @pl.when(even)
        def _():
            rh[which] = up[...]
            rdown[which, 0:512] = low[...]
            rdown[which, 512:640] = cross[which, 512:640]
            rup[which, 0:256] = small[which]

        @pl.when(odd)
        def _():
            rh[which] = low[...]
            rup[which, 0:512] = up[...]
            rup[which, 512:640] = cross[which, 512:640]
            rdown[which, 0:256] = small[which]


def pass_on(role, token):
    token[0] = role[0]
    token[1] = role[1]


def add_down(ref, rows, own):
    add_rows(ref, 0, rows[0:256], 1)
    if own:
        add_rows(ref, 256, rows[256:384], 2)
        add_rows(ref, 512, rows[384:512], 4)
    else:
        add_rows(ref, 512, rows[256:384], 1)
        add_rows(ref, 640, rows[384:448], 2)
        add_rows(ref, 256, rows[448:512], 4)


def add_up(ref, rows, own):
    if own:
        add_rows(ref, 768, rows[0:256], 1)
        add_rows(ref, 512, rows[256:384], 2)
        add_rows(ref, 0, rows[384:512], 4)
    else:
        add_rows(ref, 256, rows[0:256], 1)
        add_rows(ref, 640, rows[256:384], 1)
        add_rows(ref, 0, rows[384:448], 4)
        add_rows(ref, 512, rows[448:512], 2)


def moved(array, pairs):
    return lax.ppermute(array, AXES, pairs)


def shape(*dims, dtype=BF16):
    return jax.ShapeDtypeStruct(dims, dtype)


def vmem(limit):
    return pltpu.CompilerParams(vmem_limit_bytes=limit * 2**20)


SMEM = pl.BlockSpec(memory_space=pltpu.SMEM)


def both(rows):
    return pl.BlockSpec((None, 2, rows, PAIR), lambda j: (j, 0, 0, 0))


def own_rows():
    return pl.BlockSpec((None, 1024, PAIR), lambda j: (j, 0, 0))


def columns(start):
    return pl.BlockSpec((1024, PAIR), lambda j: (0, start + j))


TOKEN = shape(2, dtype=jnp.int32)


def pair_rows(role, keys, values, start, pairs):
    def body(role, k, v, out, token, tmp):
        pass_on(role, token)
        for which, own in ((0, k), (1, v)):
            tmp[...] = own[256:768].astype(F32)
            out[which, 0:256] = own[0:256]
            out[which, 256:512] = own[768:1024]
            out[which, 512:768] = mean_rows(tmp, 0, 256, 2)

    return pl.pallas_call(
        body,
        grid=(pairs,),
        in_specs=[SMEM] + [columns(start)] * 2,
        out_specs=[both(768), SMEM],
        out_shape=[shape(pairs, 2, 768, PAIR), TOKEN],
        scratch_shapes=[pltpu.VMEM((512, PAIR), F32)],
        compiler_params=vmem(LIMIT),
        name="pair_rows",
    )(role, keys, values)


def cross_rows(role, keys, values, partner, start, pairs):
    def body(role, k, v, p, near, up_out, down_out, token, spans, tmp, ours):
        even, wrap = role[0] == 0, role[1]
        odd = jnp.logical_not(even)
        pass_on(role, token)

        for which, own in ((0, k), (1, v)):
            tmp[...] = p[which].astype(F32)
            ours[...] = own[...].astype(F32)
            spans[0:128] = mean_rows(ours, 0, 128, 8)
            spans[128:160] = mean_rows(tmp, 0, 32, 8)
            spans[160:192] = mean_rows(tmp, 512, 32, 4)
            spans[192:224] = mean_rows(tmp, 640, 32, 4)
            spans[224:256] = mean_rows(tmp, 256, 32, 8)

            def theirs_down(out):
                out[which, 0:256] = p[which, 0:256]
                out[which, 256:384] = p[which, 512:640]
                out[which, 384:448] = mean_rows(tmp, 640, 64, 2)
                out[which, 448:512] = mean_rows(tmp, 256, 64, 4)

            def theirs_up(out):
                out[which, 0:256] = p[which, 256:512]
                out[which, 256:384] = p[which, 640:768]
                out[which, 384:448] = mean_rows(tmp, 0, 64, 4)
                out[which, 448:512] = mean_rows(tmp, 512, 64, 2)

            @pl.when(even)
            def _():
                theirs_down(near)
                theirs_up(up_out)
                up_out[which, 512:640] = spans[0:128]
                down_out[which, 0:256] = spans[...]

            @pl.when(odd)
            def _():
                theirs_up(near)
                theirs_down(down_out)
                down_out[which, 512:640] = spans[0:128]
                up_out[which, 0:256] = spans[...]

            @pl.when((wrap == 1) & even)
            def _():
                down_out[which, 0:256] = own[0:256]
                down_out[which, 256:384] = mean_rows(ours, 256, 128, 2)
                down_out[which, 384:512] = mean_rows(ours, 512, 128, 4)
                down_out[which, 512:640] = spans[128:256]

            @pl.when((wrap == 1) & odd)
            def _():
                up_out[which, 0:256] = own[768:1024]
                up_out[which, 256:384] = mean_rows(ours, 512, 128, 2)
                up_out[which, 384:512] = mean_rows(ours, 0, 128, 4)
                up_out[which, 512:640] = spans[128:256]

            @pl.when((wrap == 2) & even)
            def _():
                up_out[which, 0:128] = spans[128:256]
                up_out[which, 128:256] = spans[0:128]

            @pl.when((wrap == 2) & odd)
            def _():
                down_out[which, 0:128] = spans[128:256]
                down_out[which, 128:256] = spans[0:128]

    return pl.pallas_call(
        body,
        grid=(pairs,),
        in_specs=[SMEM, columns(start), columns(start), both(768)],
        out_specs=[both(512), both(640), both(640), SMEM],
        out_shape=[shape(pairs, 2, rows, PAIR) for rows in (512, 640, 640)] + [TOKEN],
        scratch_shapes=[
            pltpu.VMEM((256, PAIR), BF16), pltpu.VMEM((768, PAIR), F32), pltpu.VMEM((1024, PAIR), F32),
        ],
        compiler_params=vmem(LIMIT),
        name="cross_rows",
    )(role, keys, values, partner)


def attend(role, valid, queries, keys, values, grad_out, came, before, start, pairs):

    def side(rows, which):
        return pl.BlockSpec((None, None, rows, PAIR), lambda j: (j, which, 0, 0))

    extra = 0 if before is None else 2

    def body(*refs):
        attend_kernel(*refs[:12], *refs[12 + extra :])

    heights = (512, 640, 640)
    whole = shape(1024, queries.shape[1])
    return pl.pallas_call(
        body,
        grid=(pairs,),
        in_specs=[SMEM, SMEM] + [columns(start)] * 4
        + [side(rows, which) for rows in heights for which in (0, 1)]
        + [pl.BlockSpec(memory_space=pl.ANY)] * extra,
        out_specs=[columns(start)] * 2 + [own_rows()] * 2 + [both(rows) for rows in heights]
        + [SMEM],
        out_shape=[whole, whole]
        + [shape(pairs, 1024, PAIR, dtype=F32)] * 2
        + [shape(pairs, 2, rows, PAIR) for rows in heights]
        + [TOKEN],
        input_output_aliases={12: 0, 13: 1} if extra else {},
        scratch_shapes=[
            pltpu.VMEM((ROWS, PAIR), BF16), pltpu.VMEM((ROWS, PAIR), BF16),
            pltpu.VMEM((PAIR, ROWS), BF16), pltpu.VMEM((2, 80, ROWS), BF16),
        ]
        + [pltpu.VMEM((1920, 512), BF16)] * 2
        + [pltpu.VMEM((512, PAIR), BF16)] * 4
        + [pltpu.VMEM((ROWS, PAIR), F32)] * 2
        + [pltpu.VMEM((8, 512), F32)] * 2
        + [
            pltpu.VMEM((1024, PAIR), F32), pltpu.VMEM((768, PAIR), F32),
            pltpu.VMEM((2, 640, PAIR), BF16), pltpu.VMEM((2, 256, PAIR), BF16),
            pltpu.VMEM((2, 2, 512, PAIR), BF16),
            pltpu.SMEM((1,), jnp.int32), pltpu.SMEM((ROWS // 128,), F32),
        ],
        compiler_params=vmem(LIMIT),
        cost_estimate=pl.CostEstimate(
            flops=pairs * 14 * 10**9, bytes_accessed=pairs * 4 * 10**6, transcendentals=0
        ),
        name="attend_pairs",
    )(
        role, valid, queries, keys, values, grad_out,
        *[part for pair in came for part in (pair, pair)], *(before or ()),
    )


def pair_grads(role, near, above, below, pairs):
    def body(role, near, above, below, out, token, tmp):
        even, wrap = role[0] == 0, role[1]
        odd = jnp.logical_not(even)
        pass_on(role, token)

        def add_span(rows):
            add_rows(tmp, 0, rows[0:32], 8)
            add_rows(tmp, 512, rows[32:64], 4)
            add_rows(tmp, 640, rows[64:96], 4)
            add_rows(tmp, 256, rows[96:128], 8)

        for which in (0, 1):
            tmp[...] = jnp.zeros_like(tmp)

            @pl.when(even)
            def _():
                add_down(tmp, near[which], False)

                @pl.when(wrap != 2)
                def _():
                    add_up(tmp, above[which, 0:512], False)

                @pl.when(wrap == 2)
                def _():
                    add_span(above[which, 0:128])

                @pl.when(wrap == 1)
                def _():
                    add_span(below[which, 512:640])

                @pl.when(wrap != 1)
                def _():
                    add_span(below[which, 128:256])

            @pl.when(odd)
            def _():
                add_up(tmp, near[which], False)

                @pl.when(wrap != 2)
                def _():
                    add_down(tmp, below[which, 0:512], False)

                @pl.when(wrap == 2)
                def _():
                    add_span(below[which, 0:128])

                @pl.when(wrap == 1)
                def _():
                    add_span(above[which, 512:640])

                @pl.when(wrap != 1)
                def _():
                    add_span(above[which, 128:256])

            out[which] = tmp[...].astype(BF16)

    return pl.pallas_call(
        body,
        grid=(pairs,),
        in_specs=[SMEM, both(512), both(640), both(640)],
        out_specs=[both(768), SMEM],
        out_shape=[shape(pairs, 2, 768, PAIR), TOKEN],
        scratch_shapes=[pltpu.VMEM((768, PAIR), F32)],
        compiler_params=vmem(LIMIT),
        name="pair_grads",
    )(role, near, above, below)


def finish(role, own_k, own_v, above, below, partner, before, start, pairs):
    extra = 0 if before is None else 2

    def body(*refs):
        role, gk, gv, above, below, got = refs[:6]
        dk, dv, token, tmp = refs[6 + extra :]
        even, wrap = role[0] == 0, role[1]
        odd = jnp.logical_not(even)
        pass_on(role, token)
        for which, own, out in ((0, gk, dk), (1, gv, dv)):
            tmp[...] = own[...]
            add_rows(tmp, 0, got[which, 0:256], 1)
            add_rows(tmp, 768, got[which, 256:512], 1)
            add_rows(tmp, 256, got[which, 512:768], 2)

            for here, large, small, add in ((even, above, below, add_down), (odd, below, above, add_up)):

                @pl.when(here & (wrap != 2))
                def _():
                    add_rows(tmp, 0, large[which, 512:640], 8)

                @pl.when(here & (wrap == 2))
                def _():
                    add_rows(tmp, 0, large[which, 128:256], 8)

                @pl.when(here & (wrap != 1))
                def _():
                    add_rows(tmp, 0, small[which, 0:128], 8)

                @pl.when(here & (wrap == 1))
                def _():
                    add(tmp, small[which, 0:512], True)

            out[...] = tmp[...].astype(BF16)

    whole = shape(1024, 1024)
    return pl.pallas_call(
        body,
        grid=(pairs,),
        in_specs=[SMEM] + [own_rows()] * 2 + [both(640), both(640), both(768)]
        + [pl.BlockSpec(memory_space=pl.ANY)] * extra,
        out_specs=[columns(start)] * 2 + [SMEM],
        out_shape=[whole, whole, TOKEN],
        input_output_aliases={6: 0, 7: 1} if extra else {},
        scratch_shapes=[pltpu.VMEM((1024, PAIR), F32)],
        compiler_params=vmem(LIMIT),
        name="sum_grads",
    )(role, own_k, own_v, above, below, partner, *(before or ()))


def routes(outer, inner):
    count = outer * inner
    up = {i: i + 2 for i in range(count - 2)}
    for a in range(1, outer - 1, 2):
        last = a * inner + inner - 2
        up[last], up[last + 1] = last + 3, last + 2
    return [(i, i ^ 1) for i in range(count)], sorted(up.items())


def local(queries, keys, values, grad_out):
    a, b = lax.axis_index(AXES[0]), lax.axis_index(AXES[1])
    outer, inner = lax.axis_size(AXES[0]), lax.axis_size(AXES[1])
    index = a * inner + b
    count = outer * inner
    partners, up = routes(outer, inner)
    down = [(j, i) for i, j in up]
    above = (a % 2 == 1) & (a < outer - 1) & (b >= inner - 2)
    below = (a % 2 == 0) & (a > 0) & (b < 2)
    ends = (b == 0) | (b == inner - 1)
    odd = index % 2
    wrap = jnp.where(above | below, jnp.where(ends, 1, 2), 0)
    token = jnp.stack([odd, wrap]).astype(jnp.int32)
    sign = 1 - 2 * odd

    def there(step):
        at = index + step * sign
        return (at >= 0) & (at < count)

    valid = jnp.stack(
        [index > 0, index < count - 1, there(-2), there(2), there(3)]
    ).astype(F32)

    starts = [sum(GROUPS[:i]) for i in range(len(GROUPS))]
    partner, came, grown, near, answers, returned = {}, {}, {}, {}, {}, {}
    mixed = grads = None
    for step, i in ORDER:
        start, pairs = starts[i], GROUPS[i]
        if step == "pair":
            rows, token = pair_rows(token, keys, values, start, pairs)
            partner[i] = moved(rows, partners)
        elif step == "cross":
            side, upward, downward, token = cross_rows(
                token, keys, values, partner[i], start, pairs
            )
            came[i] = (side, moved(upward, up), moved(downward, down))
        elif step == "attend":
            *mixed, gk, gv, near[i], upward, downward, token = attend(
                token, valid, queries, keys, values, grad_out, came[i], mixed, start, pairs
            )
            grown[i] = (gk, gv)
            answers[i] = (moved(downward, down), moved(upward, up))
        elif step == "back":
            rows, token = pair_grads(token, near[i], *answers[i], pairs)
            returned[i] = moved(rows, partners)
        else:
            *grads, token = finish(token, *grown[i], *answers[i], returned[i], grads, start, pairs)
    return (*mixed, *grads)


def solution(mesh):
    placed = P(AXES, None)
    return jax.shard_map(
        local,
        mesh=mesh,
        in_specs=(placed,) * 4,
        out_specs=(placed,) * 4,
        check_vma=False,
    )
```

time: 380 us -> 695 us (1.83)
  the two profiles are of different devices: /device:TPU:18 before, /device:TPU:36 now
where the time goes in v3:
time: 695 us; the launch traced here: 688 us
  Pallas kernels  541 us (78%)
  starting transfers between devices  78.6 us (11%)
  waiting for transfers between devices  55.8 us (8%)
  local copies, waits for them, and re-layouts  9.51 us (1%)
    pallas_call x4, Pallas kernels, attend(): pl.pallas_call(body, grid=(pairs,), in_specs=[SMEM, SMEM] + [columns(star...  489 us
    ppermute x24, starting transfers between devices, moved(): return lax.ppermute(array, AXES, pairs)  78.6 us
    ppermute x24, waiting for transfers between devices, moved(): return lax.ppermute(array, AXES, pairs)  55.8 us
    pallas_call x4, Pallas kernels, finish(): pl.pallas_call(body, grid=(pairs,), in_specs=[SMEM] + [own_rows()] * 2 +...  16.6 us
  transfers between devices with their start and end apart: 24, of which 4 were waited for; matrix products, arithmetic and copies ran while one was open for 0% of the time, Pallas kernels for 77%

profile of v3, /device:TPU:36, one launch (start us, length us, event | category | flops | bytes accessed | tf_op | source)
XLA Modules:
  0.0 687.9 jit_solution(3226513801652290850)
XLA Ops:
  1.3 1.9 pair_rows.4
  3.3 11.0 %collective-permute-done.p = bf16[1,2,768,128]{3,2,1,0:T(8,128)(2,1)S(1)} collective-permute-done((bf16[1,2,768,128]{3,2,1,0:T(8,128)(2,1)}, bf16[1,2,768,128]{3,2,1,0:T(8,128)(2,1)S(1)}, u32[]{:S(2)}, u32[]{:S(2)}) %collective-permute-start) | collective-permute-done | bytes 393248 | tf_op jit(solution)/shard_map/ppermute | solution.py:309
  15.0 2.6 cross_rows.4
  17.7 2.1 pair_rows.5
  20.1 3.4 collective-permute-start.2
  23.6 5.1 collective-permute-start.3
  29.4 9.0 %collective-permute-done.1.p = bf16[2,2,768,128]{3,2,1,0:T(8,128)(2,1)S(1)} collective-permute-done((bf16[2,2,768,128]{3,2,1,0:T(8,128)(2,1)}, bf16[2,2,768,128]{3,2,1,0:T(8,128)(2,1)S(1)}, u32[]{:S(2)}, u32[]{:S(2)}) %collective-permute-start.1) | collective-permute-done | bytes 786464 | tf_op jit(solution)/shard_map/ppermute | solution.py:309
  39.3 3.1 cross_rows.5
  42.4 3.5 collective-permute-start.5
  45.9 5.1 collective-permute-start.6
  51.0 3.3 pair_rows.6
  54.4 1.8 collective-permute-start.4
  57.0 62.5 %attend_pairs.4 = (bf16[1024,1024]{1,0:T(8,128)(2,1)}, bf16[1024,1024]{1,0:T(8,128)(2,1)}, f32[1,1024,128]{2,1,0:T(8,128)}, f32[1,1024,128]{2,1,0:T(8,128)}, bf1...) custom-call(s32[2]{0:T(128)} %get-tuple-element.85.refs_0_, ...), custom_call_target="tpu_custom_call" | custom-call | flops 14000000000 | bytes 4000000 | tf_op jit(solution)/shard_map/attend_pairs/pallas_call | solution.py:450
  119.5 1.9 collective-permute-start.8
  121.4 3.9 collective-permute-start.9
  125.4 1.0 copy-done.9
  126.4 4.8 cross_rows.6
  131.2 2.1 pair_rows.7
  133.5 1.9 collective-permute-start.10
  135.5 6.9 %collective-permute-start.11 = (bf16[3,2,640,128]{3,2,1,0:T(8,128)(2,1)S(1)}, bf16[3,2,640,128]{3,2,1,0:T(8,128)(2,1)}, u32[]{:S(2)}, u32[]{:S(2)}) collective-permute-start(bf16[3,2,640,128]{3,2,1,0:T(8,128)(2,1)S(1)} %copy-done.15), channel_id=1, source_target_pairs={{2,0},{3,1},{4,2},{5,3},{6,4},{7,5},{8,6},{9,7},{10,8},{11,9},{12,... | collective-permute-start | bytes 2949128 | tf_op jit(solution)/shard_map/ppermute | solution.py:309
  142.4 122.2 %attend_pairs.5 = (bf16[1024,1024]{1,0:T(8,128)(2,1)}, bf16[1024,1024]{1,0:T(8,128)(2,1)}, f32[2,1024,128]{2,1,0:T(8,128)}, f32[2,1024,128]{2,1,0:T(8,128)}, bf1...) custom-call(s32[2]{0:T(128)} %get-tuple-element.92.refs_0_, ...), custom_call_target="tpu_custom_call", output_to_operand_aliasing={{0}: (12, {}), {1}: (13, {})} | custom-call | flops 28000000000 | bytes 8000000 | tf_op jit(solution)/shard_map/attend_pairs/pallas_call | solution.py:450
  264.7 2.0 collective-permute-start.12
  266.7 3.2 cross_rows.7
  269.9 3.8 collective-permute-start.13
  273.7 1.9 collective-permute-start.14
  275.7 2.4 pair_grads.4
  278.1 6.6 collective-permute-start.15
  284.8 181.9 %attend_pairs.6 = (bf16[1024,1024]{1,0:T(8,128)(2,1)}, bf16[1024,1024]{1,0:T(8,128)(2,1)}, f32[3,1024,128]{2,1,0:T(8,128)}, f32[3,1024,128]{2,1,0:T(8,128)}, bf1...) custom-call(s32[2]{0:T(128)} %get-tuple-element.104.refs_0_, ...), custom_call_target="tpu_custom_call", output_to_operand_aliasing={{0}: (12, {}), {1}: (13, {})} | custom-call | flops 41999998976 | bytes 12000000 | tf_op jit(solution)/shard_map/attend_pairs/pallas_call | solution.py:450
  466.7 1.9 collective-permute-start.16
  468.6 12.5 %collective-permute-start.17 = (bf16[3,2,640,128]{3,2,1,0:T(8,128)(2,1)}, bf16[3,2,640,128]{3,2,1,0:T(8,128)(2,1)S(1)}, u32[]{:S(2)}, u32[]{:S(2)}) collective-permute-start(bf16[3,2,640,128]{3,2,1,0:T(8,128)(2,1)} %get-tuple-element.125), channel_id=1, source_target_pairs={{0,2},{1,3},{2,4},{3,5},{4,6},{5,7},{6,8},{7,9},{8,10},{9,11},{10,... | collective-permute-start | bytes 2949128 | tf_op jit(solution)/shard_map/ppermute | solution.py:309
  482.0 3.0 pair_grads.5
  485.0 122.2 %attend_pairs.7 = (bf16[1024,1024]{1,0:T(8,128)(2,1)}, bf16[1024,1024]{1,0:T(8,128)(2,1)}, f32[2,1024,128]{2,1,0:T(8,128)}, f32[2,1024,128]{2,1,0:T(8,128)}, bf1...) custom-call(s32[2]{0:T(128)} %get-tuple-element.114.refs_0_, ...), custom_call_target="tpu_custom_call", output_to_operand_aliasing={{0}: (12, {}), {1}: (13, {})} | custom-call | flops 28000000000 | bytes 8000000 | tf_op jit(solution)/shard_map/attend_pairs/pallas_call | solution.py:450
  607.2 4.6 collective-permute-start.19
  611.8 1.9 collective-permute-start.20
  613.8 5.3 collective-permute-start.18
  619.1 0.9 copy-done
  620.4 4.2 pair_grads.6
  624.6 2.0 collective-permute-start.21
  626.6 2.8 collective-permute-done.18.refs_5_
  629.4 3.3 sum_grads.4
  633.8 3.0 pair_grads.7
  636.8 1.6 collective-permute-start.23
  638.4 33.0 %collective-permute-done.21.refs_5_ = bf16[2,2,768,128]{3,2,1,0:T(8,128)(2,1)S(1)} collective-permute-done((bf16[2,2,768,128]{3,2,1,0:T(8,128)(2,1)}, bf16[2,2,768,128]{3,2,1,0:T(8,128)(2,1)S(1)}, u32[]{:S(2)}, u32[]{:S(2)}) %collective-permute-start.21) | collective-permute-done | bytes 786464 | tf_op jit(solution)/shard_map/ppermute | solution.py:309
  672.3 3.9 sum_grads.5
  676.3 1.0 copy-done.8
  677.3 5.5 sum_grads.6
  682.8 0.9 copy-done.11
  683.7 3.9 sum_grads.7
  (65 shorter events, 7.6 us)
Async XLA Ops:
  3.2 11.1 %collective-permute-start = (bf16[1,2,768,128]{3,2,1,0:T(8,128)(2,1)}, bf16[1,2,768,128]{3,2,1,0:T(8,128)(2,1)S(1)}, u32[]{:S(2)}, u32[]{:S(2)}) collective-permute-start(bf16[1,2,768,128]{3,2,1,0:T(8,128)(2,1)} %get-tuple-element.80), channel_id=1, source_target_pairs={{0,1},{1,0},{2,3},{3,2},{4,5},{5,4},{6,7},{7,6},{8,9},{9,8},{10,11... | collective-permute-start | bytes 1179656 | tf_op jit(solution)/shard_map/ppermute | solution.py:309
  14.3 0.7 copy-start.14
  17.6 2.5 copy-start.19
  17.6 5.9 copy-start.17
  19.8 18.6 %collective-permute-start.1 = (bf16[2,2,768,128]{3,2,1,0:T(8,128)(2,1)}, bf16[2,2,768,128]{3,2,1,0:T(8,128)(2,1)S(1)}, u32[]{:S(2)}, u32[]{:S(2)}) collective-permute-start(bf16[2,2,768,128]{3,2,1,0:T(8,128)(2,1)} %get-tuple-element.83), channel_id=1, source_target_pairs={{0,1},{1,0},{2,3},{3,2},{4,5},{5,4},{6,7},{7,6},{8,9},{9,8},{10,11... | collective-permute-start | bytes 2359304 | tf_op jit(solution)/shard_map/ppermute | solution.py:309
  20.1 36.0 %collective-permute-start.2 = (bf16[1,2,640,128]{3,2,1,0:T(8,128)(2,1)S(1)}, bf16[1,2,640,128]{3,2,1,0:T(8,128)(2,1)S(1)}, u32[]{:S(2)}, u32[]{:S(2)}) collective-permute-start(bf16[1,2,640,128]{3,2,1,0:T(8,128)(2,1)S(1)} %copy-done.19), channel_id=1, source_target_pairs={{0,2},{1,3},{2,4},{3,5},{4,6},{5,7},{6,8},{7,9},{8,10},{9,11},{10,... | collective-permute-start | bytes 983048 | tf_op jit(solution)/shard_map/ppermute | solution.py:309
  23.6 32.6 %collective-permute-start.3 = (bf16[1,2,640,128]{3,2,1,0:T(8,128)(2,1)S(1)}, bf16[1,2,640,128]{3,2,1,0:T(8,128)(2,1)S(1)}, u32[]{:S(2)}, u32[]{:S(2)}) collective-permute-start(bf16[1,2,640,128]{3,2,1,0:T(8,128)(2,1)S(1)} %copy-done.17), channel_id=1, source_target_pairs={{2,0},{3,1},{4,2},{5,3},{6,4},{7,5},{8,6},{9,7},{10,8},{11,9},{12,... | collective-permute-start | bytes 983048 | tf_op jit(solution)/shard_map/ppermute | solution.py:309
  38.4 0.9 copy-start.10
  42.4 91.1 %collective-permute-start.5 = (bf16[2,2,640,128]{3,2,1,0:T(8,128)(2,1)}, bf16[2,2,640,128]{3,2,1,0:T(8,128)(2,1)S(1)}, u32[]{:S(2)}, u32[]{:S(2)}) collective-permute-start(bf16[2,2,640,128]{3,2,1,0:T(8,128)(2,1)} %get-tuple-element.94), channel_id=1, source_target_pairs={{0,2},{1,3},{2,4},{3,5},{4,6},{5,7},{6,8},{7,9},{8,10},{9,11},{10,... | collective-permute-start | bytes 1966088 | tf_op jit(solution)/shard_map/ppermute | solution.py:309
  45.9 89.6 %collective-permute-start.6 = (bf16[2,2,640,128]{3,2,1,0:T(8,128)(2,1)}, bf16[2,2,640,128]{3,2,1,0:T(8,128)(2,1)}, u32[]{:S(2)}, u32[]{:S(2)}) collective-permute-start(bf16[2,2,640,128]{3,2,1,0:T(8,128)(2,1)} %get-tuple-element.95), channel_id=1, source_target_pairs={{2,0},{3,1},{4,2},{5,3},{6,4},{7,5},{8,6},{9,7},{10,8},{11,9},{12,... | collective-permute-start | bytes 1966088 | tf_op jit(solution)/shard_map/ppermute | solution.py:309
  54.4 71.0 %collective-permute-start.4 = (bf16[3,2,768,128]{3,2,1,0:T(8,128)(2,1)}, bf16[3,2,768,128]{3,2,1,0:T(8,128)(2,1)S(1)}, u32[]{:S(2)}, u32[]{:S(2)}) collective-permute-start(bf16[3,2,768,128]{3,2,1,0:T(8,128)(2,1)} %get-tuple-element.90), channel_id=1, source_target_pairs={{0,1},{1,0},{2,3},{3,2},{4,5},{5,4},{6,7},{7,6},{8,9},{9,8},{10,11... | collective-permute-start | bytes 3538952 | tf_op jit(solution)/shard_map/ppermute | solution.py:309
  56.2 0.7 copy-start.18
  56.2 0.8 copy-start.20
  119.5 150.3 %collective-permute-start.8 = (bf16[1,2,640,128]{3,2,1,0:T(8,128)(2,1)}, bf16[1,2,640,128]{3,2,1,0:T(8,128)(2,1)S(1)}, u32[]{:S(2)}, u32[]{:S(2)}) collective-permute-start(bf16[1,2,640,128]{3,2,1,0:T(8,128)(2,1)} %get-tuple-element.102), channel_id=1, source_target_pairs={{2,0},{3,1},{4,2},{5,3},{6,4},{7,5},{8,6},{9,7},{10,8},{11,9},{12,... | collective-permute-start | bytes 983048 | tf_op jit(solution)/shard_map/ppermute | solution.py:309
  121.4 152.3 %collective-permute-start.9 = (bf16[1,2,640,128]{3,2,1,0:T(8,128)(2,1)}, bf16[1,2,640,128]{3,2,1,0:T(8,128)(2,1)S(1)}, u32[]{:S(2)}, u32[]{:S(2)}) collective-permute-start(bf16[1,2,640,128]{3,2,1,0:T(8,128)(2,1)} %get-tuple-element.103), channel_id=1, source_target_pairs={{0,2},{1,3},{2,4},{3,5},{4,6},{5,7},{6,8},{7,9},{8,10},{9,11},{10,... | collective-permute-start | bytes 983048 | tf_op jit(solution)/shard_map/ppermute | solution.py:309
  125.4 1.0 copy-start.9
  131.2 4.3 copy-start.15
  133.3 131.3 %collective-permute-start.7 = (bf16[2,2,768,128]{3,2,1,0:T(8,128)(2,1)}, bf16[2,2,768,128]{3,2,1,0:T(8,128)(2,1)S(1)}, u32[]{:S(2)}, u32[]{:S(2)}) collective-permute-start(bf16[2,2,768,128]{3,2,1,0:T(8,128)(2,1)} %get-tuple-element.99), channel_id=1, source_target_pairs={{0,1},{1,0},{2,3},{3,2},{4,5},{5,4},{6,7},{7,6},{8,9},{9,8},{10,11... | collective-permute-start | bytes 2359304 | tf_op jit(solution)/shard_map/ppermute | solution.py:309
  133.5 8.9 %copy-start.16 = (bf16[2,2,640,128]{3,2,1,0:T(8,128)(2,1)}, bf16[2,2,640,128]{3,2,1,0:T(8,128)(2,1)S(1)}, u32[]{:S(2)}) copy-start(bf16[2,2,640,128]{3,2,1,0:T(8,128)(2,1)S(1)} %collective-permute-done.5.refs_8_.refs_9_) | copy-start | bytes 1966084
  133.5 144.6 %collective-permute-start.10 = (bf16[3,2,640,128]{3,2,1,0:T(8,128)(2,1)}, bf16[3,2,640,128]{3,2,1,0:T(8,128)(2,1)}, u32[]{:S(2)}, u32[]{:S(2)}) collective-permute-start(bf16[3,2,640,128]{3,2,1,0:T(8,128)(2,1)} %get-tuple-element.106), channel_id=1, source_target_pairs={{0,2},{1,3},{2,4},{3,5},{4,6},{5,7},{6,8},{7,9},{8,10},{9,11},{10,... | collective-permute-start | bytes 2949128 | tf_op jit(solution)/shard_map/ppermute | solution.py:309
  135.5 149.3 %collective-permute-start.11 = (bf16[3,2,640,128]{3,2,1,0:T(8,128)(2,1)S(1)}, bf16[3,2,640,128]{3,2,1,0:T(8,128)(2,1)}, u32[]{:S(2)}, u32[]{:S(2)}) collective-permute-start(bf16[3,2,640,128]{3,2,1,0:T(8,128)(2,1)S(1)} %copy-done.15), channel_id=1, source_target_pairs={{2,0},{3,1},{4,2},{5,3},{6,4},{7,5},{8,6},{9,7},{10,8},{11,9},{12,... | collective-permute-start | bytes 2949128 | tf_op jit(solution)/shard_map/ppermute | solution.py:309
  264.7 2.0 copy-start.13
  264.7 204.0 %collective-permute-start.12 = (bf16[2,2,640,128]{3,2,1,0:T(8,128)(2,1)}, bf16[2,2,640,128]{3,2,1,0:T(8,128)(2,1)S(1)}, u32[]{:S(2)}, u32[]{:S(2)}) collective-permute-start(bf16[2,2,640,128]{3,2,1,0:T(8,128)(2,1)} %get-tuple-element.112), channel_id=1, source_target_pairs={{2,0},{3,1},{4,2},{5,3},{6,4},{7,5},{8,6},{9,7},{10,8},{11,9},{12,... | collective-permute-start | bytes 1966088 | tf_op jit(solution)/shard_map/ppermute | solution.py:309
  269.9 5.8 copy-start.6
  269.9 211.3 %collective-permute-start.13 = (bf16[2,2,640,128]{3,2,1,0:T(8,128)(2,1)}, bf16[2,2,640,128]{3,2,1,0:T(8,128)(2,1)S(1)}, u32[]{:S(2)}, u32[]{:S(2)}) collective-permute-start(bf16[2,2,640,128]{3,2,1,0:T(8,128)(2,1)} %get-tuple-element.113), channel_id=1, source_target_pairs={{0,2},{1,3},{2,4},{3,5},{4,6},{5,7},{6,8},{7,9},{8,10},{9,11},{10,... | collective-permute-start | bytes 1966088 | tf_op jit(solution)/shard_map/ppermute | solution.py:309
  273.7 2.0 copy-start.7
  273.7 211.2 %collective-permute-start.14 = (bf16[2,2,640,128]{3,2,1,0:T(8,128)(2,1)}, bf16[2,2,640,128]{3,2,1,0:T(8,128)(2,1)}, u32[]{:S(2)}, u32[]{:S(2)}) collective-permute-start(bf16[2,2,640,128]{3,2,1,0:T(8,128)(2,1)} %get-tuple-element.116), channel_id=1, source_target_pairs={{0,2},{1,3},{2,4},{3,5},{4,6},{5,7},{6,8},{7,9},{8,10},{9,11},{10,... | collective-permute-start | bytes 1966088 | tf_op jit(solution)/shard_map/ppermute | solution.py:309
  278.1 206.9 %collective-permute-start.15 = (bf16[2,2,640,128]{3,2,1,0:T(8,128)(2,1)}, bf16[2,2,640,128]{3,2,1,0:T(8,128)(2,1)}, u32[]{:S(2)}, u32[]{:S(2)}) collective-permute-start(bf16[2,2,640,128]{3,2,1,0:T(8,128)(2,1)} %get-tuple-element.117), channel_id=1, source_target_pairs={{2,0},{3,1},{4,2},{5,3},{6,4},{7,5},{8,6},{9,7},{10,8},{11,9},{12,... | collective-permute-start | bytes 1966088 | tf_op jit(solution)/shard_map/ppermute | solution.py:309
  466.7 152.4 %collective-permute-start.16 = (bf16[3,2,640,128]{3,2,1,0:T(8,128)(2,1)}, bf16[3,2,640,128]{3,2,1,0:T(8,128)(2,1)S(1)}, u32[]{:S(2)}, u32[]{:S(2)}) collective-permute-start(bf16[3,2,640,128]{3,2,1,0:T(8,128)(2,1)} %get-tuple-element.124), channel_id=1, source_target_pairs={{2,0},{3,1},{4,2},{5,3},{6,4},{7,5},{8,6},{9,7},{10,8},{11,9},{12,... | collective-permute-start | bytes 2949128 | tf_op jit(solution)/shard_map/ppermute | solution.py:309
  468.6 12.6 %copy-start.2 = (bf16[2,2,640,128]{3,2,1,0:T(8,128)(2,1)}, bf16[2,2,640,128]{3,2,1,0:T(8,128)(2,1)S(1)}, u32[]{:S(2)}) copy-start(bf16[2,2,640,128]{3,2,1,0:T(8,128)(2,1)S(1)} %collective-permute-done.12.above.refs_3_) | copy-start | bytes 1966084
  468.6 150.4 %collective-permute-start.17 = (bf16[3,2,640,128]{3,2,1,0:T(8,128)(2,1)}, bf16[3,2,640,128]{3,2,1,0:T(8,128)(2,1)S(1)}, u32[]{:S(2)}, u32[]{:S(2)}) collective-permute-start(bf16[3,2,640,128]{3,2,1,0:T(8,128)(2,1)} %get-tuple-element.125), channel_id=1, source_target_pairs={{0,2},{1,3},{2,4},{3,5},{4,6},{5,7},{6,8},{7,9},{8,10},{9,11},{10,... | collective-permute-start | bytes 2949128 | tf_op jit(solution)/shard_map/ppermute | solution.py:309
  481.2 0.8 copy-start.3
  607.2 25.5 %collective-permute-start.19 = (bf16[2,2,640,128]{3,2,1,0:T(8,128)(2,1)}, bf16[2,2,640,128]{3,2,1,0:T(8,128)(2,1)S(1)}, u32[]{:S(2)}, u32[]{:S(2)}) collective-permute-start(bf16[2,2,640,128]{3,2,1,0:T(8,128)(2,1)} %get-tuple-element.132), channel_id=1, source_target_pairs={{2,0},{3,1},{4,2},{5,3},{6,4},{7,5},{8,6},{9,7},{10,8},{11,9},{12,... | collective-permute-start | bytes 1966088 | tf_op jit(solution)/shard_map/ppermute | solution.py:309
  611.8 20.9 %collective-permute-start.20 = (bf16[2,2,640,128]{3,2,1,0:T(8,128)(2,1)}, bf16[2,2,640,128]{3,2,1,0:T(8,128)(2,1)S(1)}, u32[]{:S(2)}, u32[]{:S(2)}) collective-permute-start(bf16[2,2,640,128]{3,2,1,0:T(8,128)(2,1)} %get-tuple-element.133), channel_id=1, source_target_pairs={{0,2},{1,3},{2,4},{3,5},{4,6},{5,7},{6,8},{7,9},{8,10},{9,11},{10,... | collective-permute-start | bytes 1966088 | tf_op jit(solution)/shard_map/ppermute | solution.py:309
  613.8 15.7 %collective-permute-start.18 = (bf16[1,2,768,128]{3,2,1,0:T(8,128)(2,1)}, bf16[1,2,768,128]{3,2,1,0:T(8,128)(2,1)}, u32[]{:S(2)}, u32[]{:S(2)}) collective-permute-start(bf16[1,2,768,128]{3,2,1,0:T(8,128)(2,1)} %get-tuple-element.129), channel_id=1, source_target_pairs={{0,1},{1,0},{2,3},{3,2},{4,5},{5,4},{6,7},{7,6},{8,9},{9,8},{10,11... | collective-permute-start | bytes 1179656 | tf_op jit(solution)/shard_map/ppermute | solution.py:309
  619.1 0.9 copy-start
  619.1 1.3 copy-start.1
  624.6 51.7 %collective-permute-start.22 = (bf16[3,2,768,128]{3,2,1,0:T(8,128)(2,1)}, bf16[3,2,768,128]{3,2,1,0:T(8,128)(2,1)S(1)}, u32[]{:S(2)}, u32[]{:S(2)}) collective-permute-start(bf16[3,2,768,128]{3,2,1,0:T(8,128)(2,1)} %get-tuple-element.143), channel_id=1, source_target_pairs={{0,1},{1,0},{2,3},{3,2},{4,5},{5,4},{6,7},{7,6},{8,9},{9,8},{10,11... | collective-permute-start | bytes 3538952 | tf_op jit(solution)/shard_map/ppermute | solution.py:309
  624.6 46.9 %collective-permute-start.21 = (bf16[2,2,768,128]{3,2,1,0:T(8,128)(2,1)}, bf16[2,2,768,128]{3,2,1,0:T(8,128)(2,1)S(1)}, u32[]{:S(2)}, u32[]{:S(2)}) collective-permute-start(bf16[2,2,768,128]{3,2,1,0:T(8,128)(2,1)} %get-tuple-element.137), channel_id=1, source_target_pairs={{0,1},{1,0},{2,3},{3,2},{4,5},{5,4},{6,7},{7,6},{8,9},{9,8},{10,11... | collective-permute-start | bytes 2359304 | tf_op jit(solution)/shard_map/ppermute | solution.py:309
  632.7 0.9 copy-start.4
  632.7 1.1 copy-start.5
  636.8 46.0 %collective-permute-start.23 = (bf16[2,2,768,128]{3,2,1,0:T(8,128)(2,1)}, bf16[2,2,768,128]{3,2,1,0:T(8,128)(2,1)S(1)}, u32[]{:S(2)}, u32[]{:S(2)}) collective-permute-start(bf16[2,2,768,128]{3,2,1,0:T(8,128)(2,1)} %get-tuple-element.149), channel_id=1, source_target_pairs={{0,1},{1,0},{2,3},{3,2},{4,5},{5,4},{6,7},{7,6},{8,9},{9,8},{10,11... | collective-permute-start | bytes 2359304 | tf_op jit(solution)/shard_map/ppermute | solution.py:309
  671.5 0.9 copy-start.12
  676.3 1.0 copy-start.8
  682.8 0.9 copy-start.11

commit v4 on v3

--- a/solution.py
+++ b/solution.py
@@ -12,10 +12,10 @@
 HALF = 128
 PAIR = 128
 AXES = ("seqa", "seqb")
-GROUPS = (1, 2, 3, 2)
+GROUPS = (2, 3, 2, 1)
 ORDER = (
-    ("pair", 0), ("cross", 0), ("pair", 1), ("cross", 1), ("pair", 2),
-    ("attend", 0), ("cross", 2), ("pair", 3),
+    ("pair", 0), ("cross", 0), ("pair", 1),
+    ("attend", 0), ("cross", 1), ("pair", 2), ("cross", 2), ("pair", 3),
     ("attend", 1), ("cross", 3), ("back", 0),
     ("attend", 2), ("back", 1),
     ("attend", 3), ("back", 2), ("sum", 0), ("back", 3), ("sum", 1), ("sum", 2), ("sum", 3),

time: 695 us -> 675 us (0.971)
  waiting for transfers between devices: 55.8 us -> 42.9 us
  starting transfers between devices: 78.6 us -> 70.6 us
    ppermute x24, waiting for transfers between devices: 55.8 us -> 42.9 us  [moved(): return lax.ppermute(array, AXES, pairs)]
    ppermute x24, starting transfers between devices: 78.6 us -> 70.6 us  [moved(): return lax.ppermute(array, AXES, pairs)]
  transfers between devices with their start and end apart: 24 -> 24, of which waited for: 4 -> 5; matrix products, arithmetic and copies ran while one was open for 0% -> 0% of each run, Pallas kernels for 77% -> 79%
where the time goes in v4:
time: 675 us; the launch traced here: 666 us
  Pallas kernels  541 us (80%)
  starting transfers between devices  70.6 us (10%)
  waiting for transfers between devices  42.9 us (6%)
  local copies, waits for them, and re-layouts  9.11 us (1%)
    pallas_call x4, Pallas kernels, attend(): pl.pallas_call(body, grid=(pairs,), in_specs=[SMEM, SMEM] + [columns(star...  489 us
    ppermute x24, starting transfers between devices, moved(): return lax.ppermute(array, AXES, pairs)  70.6 us
    ppermute x24, waiting for transfers between devices, moved(): return lax.ppermute(array, AXES, pairs)  42.9 us
    pallas_call x4, Pallas kernels, finish(): pl.pallas_call(body, grid=(pairs,), in_specs=[SMEM] + [own_rows()] * 2 +...  16.4 us
    pallas_call x4, Pallas kernels, cross_rows(): pl.pallas_call(body, grid=(pairs,), in_specs=[SMEM, columns(start), colum...  13.7 us
  transfers between devices with their start and end apart: 24, of which 5 were waited for; matrix products, arithmetic and copies ran while one was open for 0% of the time, Pallas kernels for 79%

profile of v4, /device:TPU:36, one launch (start us, length us, event | category | flops | bytes accessed | tf_op | source)
XLA Modules:
  0.0 666.2 jit_solution(12707092153998381025)
XLA Ops:
  1.3 2.1 pair_rows.4
  3.4 19.4 %collective-permute-done.p = bf16[2,2,768,128]{3,2,1,0:T(8,128)(2,1)S(1)} collective-permute-done((bf16[2,2,768,128]{3,2,1,0:T(8,128)(2,1)}, bf16[2,2,768,128]{3,2,1,0:T(8,128)(2,1)S(1)}, u32[]{:S(2)}, u32[]{:S(2)}) %collective-permute-start) | collective-permute-done | bytes 786464 | tf_op jit(solution)/shard_map/ppermute | solution.py:309
  23.7 3.1 cross_rows.4
  26.8 3.5 collective-permute-start.1
  30.3 5.1 collective-permute-start.2
  36.1 3.3 pair_rows.5
  39.4 1.6 collective-permute-start.3
  41.0 2.7 collective-permute-done.1.refs_8_.refs_9_
  43.7 4.0 collective-permute-done.2.refs_10_.refs_11_
  48.5 122.2 %attend_pairs.4 = (bf16[1024,1024]{1,0:T(8,128)(2,1)}, bf16[1024,1024]{1,0:T(8,128)(2,1)}, f32[2,1024,128]{2,1,0:T(8,128)}, f32[2,1024,128]{2,1,0:T(8,128)}, bf1...) custom-call(s32[2]{0:T(128)} %get-tuple-element.82.refs_0_, ...), custom_call_target="tpu_custom_call" | custom-call | flops 28000000000 | bytes 8000000 | tf_op jit(solution)/shard_map/attend_pairs/pallas_call | solution.py:450
  170.7 1.0 copy-done.9
  171.7 4.8 cross_rows.5
  176.5 3.5 collective-permute-start.5
  180.0 5.1 collective-permute-start.6
  185.1 2.1 pair_rows.6
  187.2 1.6 collective-permute-start.4
  188.8 1.9 collective-permute-start.8
  190.7 3.9 collective-permute-start.9
  194.7 11.9 %collective-permute-done.4.p = bf16[2,2,768,128]{3,2,1,0:T(8,128)(2,1)S(1)} collective-permute-done((bf16[2,2,768,128]{3,2,1,0:T(8,128)(2,1)}, bf16[2,2,768,128]{3,2,1,0:T(8,128)(2,1)S(1)}, u32[]{:S(2)}, u32[]{:S(2)}) %collective-permute-start.4) | collective-permute-done | bytes 786464 | tf_op jit(solution)/shard_map/ppermute | solution.py:309
  207.5 3.2 cross_rows.6
  210.6 1.9 pair_rows.7
  213.0 2.3 collective-permute-start.10
  215.3 6.5 collective-permute-start.11
  221.8 181.9 %attend_pairs.5 = (bf16[1024,1024]{1,0:T(8,128)(2,1)}, bf16[1024,1024]{1,0:T(8,128)(2,1)}, f32[3,1024,128]{2,1,0:T(8,128)}, f32[3,1024,128]{2,1,0:T(8,128)}, bf1...) custom-call(s32[2]{0:T(128)} %get-tuple-element.92.refs_0_, ...), custom_call_target="tpu_custom_call", output_to_operand_aliasing={{0}: (12, {}), {1}: (13, {})} | custom-call | flops 41999998976 | bytes 12000000 | tf_op jit(solution)/shard_map/attend_pairs/pallas_call | solution.py:450
  403.8 1.9 collective-permute-start.12
  405.7 2.6 cross_rows.7
  408.3 3.9 collective-permute-start.13
  412.3 1.9 collective-permute-start.14
  414.2 3.0 pair_grads.4
  417.2 6.6 collective-permute-start.15
  423.8 4.4 collective-permute-start.18
  428.2 122.2 %attend_pairs.6 = (bf16[1024,1024]{1,0:T(8,128)(2,1)}, bf16[1024,1024]{1,0:T(8,128)(2,1)}, f32[2,1024,128]{2,1,0:T(8,128)}, f32[2,1024,128]{2,1,0:T(8,128)}, bf1...) custom-call(s32[2]{0:T(128)} %get-tuple-element.104.refs_0_, ...), custom_call_target="tpu_custom_call", output_to_operand_aliasing={{0}: (12, {}), {1}: (13, {})} | custom-call | flops 28000000000 | bytes 8000000 | tf_op jit(solution)/shard_map/attend_pairs/pallas_call | solution.py:450
  550.5 1.9 collective-permute-start.16
  552.4 3.9 collective-permute-start.17
  556.4 4.2 pair_grads.5
  560.6 62.7 %attend_pairs.7 = (bf16[1024,1024]{1,0:T(8,128)(2,1)}, bf16[1024,1024]{1,0:T(8,128)(2,1)}, f32[1,1024,128]{2,1,0:T(8,128)}, f32[1,1024,128]{2,1,0:T(8,128)}, bf1...) custom-call(s32[2]{0:T(128)} %get-tuple-element.114.refs_0_, ...), custom_call_target="tpu_custom_call", output_to_operand_aliasing={{0}: (12, {}), {1}: (13, {})} | custom-call | flops 14000000000 | bytes 4000000 | tf_op jit(solution)/shard_map/attend_pairs/pallas_call | solution.py:450
  624.4 3.0 pair_grads.6
  627.4 1.8 collective-permute-start.22
  629.2 4.1 collective-permute-start.19
  633.3 1.9 collective-permute-start.20
  636.1 3.9 sum_grads.4
  640.0 4.9 collective-permute-done.20.below.refs_4_
  645.6 2.4 pair_grads.7
  648.0 2.6 collective-permute-start.23
  650.7 1.1 copy-done.8
  651.8 5.5 sum_grads.5
  658.2 3.9 sum_grads.6
  662.9 3.1 sum_grads.7
  (61 shorter events, 8.8 us)
Async XLA Ops:
  3.3 19.5 %collective-permute-start = (bf16[2,2,768,128]{3,2,1,0:T(8,128)(2,1)}, bf16[2,2,768,128]{3,2,1,0:T(8,128)(2,1)S(1)}, u32[]{:S(2)}, u32[]{:S(2)}) collective-permute-start(bf16[2,2,768,128]{3,2,1,0:T(8,128)(2,1)} %get-tuple-element.80), channel_id=1, source_target_pairs={{0,1},{1,0},{2,3},{3,2},{4,5},{5,4},{6,7},{7,6},{8,9},{9,8},{10,11... | collective-permute-start | bytes 2359304 | tf_op jit(solution)/shard_map/ppermute | solution.py:309
  22.8 0.9 copy-start.13
  26.8 16.9 %collective-permute-start.1 = (bf16[2,2,640,128]{3,2,1,0:T(8,128)(2,1)}, bf16[2,2,640,128]{3,2,1,0:T(8,128)(2,1)S(1)}, u32[]{:S(2)}, u32[]{:S(2)}) collective-permute-start(bf16[2,2,640,128]{3,2,1,0:T(8,128)(2,1)} %get-tuple-element.84), channel_id=1, source_target_pairs={{0,2},{1,3},{2,4},{3,5},{4,6},{5,7},{6,8},{7,9},{8,10},{9,11},{10,... | collective-permute-start | bytes 1966088 | tf_op jit(solution)/shard_map/ppermute | solution.py:309
  30.3 17.4 %collective-permute-start.2 = (bf16[2,2,640,128]{3,2,1,0:T(8,128)(2,1)}, bf16[2,2,640,128]{3,2,1,0:T(8,128)(2,1)S(1)}, u32[]{:S(2)}, u32[]{:S(2)}) collective-permute-start(bf16[2,2,640,128]{3,2,1,0:T(8,128)(2,1)} %get-tuple-element.85), channel_id=1, source_target_pairs={{2,0},{3,1},{4,2},{5,3},{6,4},{7,5},{8,6},{9,7},{10,8},{11,9},{12,... | collective-permute-start | bytes 1966088 | tf_op jit(solution)/shard_map/ppermute | solution.py:309
  39.4 131.3 %collective-permute-start.3 = (bf16[3,2,768,128]{3,2,1,0:T(8,128)(2,1)}, bf16[3,2,768,128]{3,2,1,0:T(8,128)(2,1)S(1)}, u32[]{:S(2)}, u32[]{:S(2)}) collective-permute-start(bf16[3,2,768,128]{3,2,1,0:T(8,128)(2,1)} %get-tuple-element.87), channel_id=1, source_target_pairs={{0,1},{1,0},{2,3},{3,2},{4,5},{5,4},{6,7},{7,6},{8,9},{9,8},{10,11... | collective-permute-start | bytes 3538952 | tf_op jit(solution)/shard_map/ppermute | solution.py:309
  43.7 4.0 copy-start.17
  47.7 0.8 copy-start.18
  170.7 1.0 copy-start.9
  176.5 36.5 %collective-permute-start.5 = (bf16[3,2,640,128]{3,2,1,0:T(8,128)(2,1)}, bf16[3,2,640,128]{3,2,1,0:T(8,128)(2,1)S(1)}, u32[]{:S(2)}, u32[]{:S(2)}) collective-permute-start(bf16[3,2,640,128]{3,2,1,0:T(8,128)(2,1)} %get-tuple-element.94), channel_id=1, source_target_pairs={{0,2},{1,3},{2,4},{3,5},{4,6},{5,7},{6,8},{7,9},{8,10},{9,11},{10,... | collective-permute-start | bytes 2949128 | tf_op jit(solution)/shard_map/ppermute | solution.py:309
  180.0 35.3 %collective-permute-start.6 = (bf16[3,2,640,128]{3,2,1,0:T(8,128)(2,1)}, bf16[3,2,640,128]{3,2,1,0:T(8,128)(2,1)}, u32[]{:S(2)}, u32[]{:S(2)}) collective-permute-start(bf16[3,2,640,128]{3,2,1,0:T(8,128)(2,1)} %get-tuple-element.95), channel_id=1, source_target_pairs={{2,0},{3,1},{4,2},{5,3},{6,4},{7,5},{8,6},{9,7},{10,8},{11,9},{12,... | collective-permute-start | bytes 2949128 | tf_op jit(solution)/shard_map/ppermute | solution.py:309
  187.2 19.4 %collective-permute-start.4 = (bf16[2,2,768,128]{3,2,1,0:T(8,128)(2,1)}, bf16[2,2,768,128]{3,2,1,0:T(8,128)(2,1)S(1)}, u32[]{:S(2)}, u32[]{:S(2)}) collective-permute-start(bf16[2,2,768,128]{3,2,1,0:T(8,128)(2,1)} %get-tuple-element.90), channel_id=1, source_target_pairs={{0,1},{1,0},{2,3},{3,2},{4,5},{5,4},{6,7},{7,6},{8,9},{9,8},{10,11... | collective-permute-start | bytes 2359304 | tf_op jit(solution)/shard_map/ppermute | solution.py:309
  188.8 219.5 %collective-permute-start.8 = (bf16[2,2,640,128]{3,2,1,0:T(8,128)(2,1)}, bf16[2,2,640,128]{3,2,1,0:T(8,128)(2,1)S(1)}, u32[]{:S(2)}, u32[]{:S(2)}) collective-permute-start(bf16[2,2,640,128]{3,2,1,0:T(8,128)(2,1)} %get-tuple-element.102), channel_id=1, source_target_pairs={{2,0},{3,1},{4,2},{5,3},{6,4},{7,5},{8,6},{9,7},{10,8},{11,9},{12,... | collective-permute-start | bytes 1966088 | tf_op jit(solution)/shard_map/ppermute | solution.py:309
  190.7 221.5 %collective-permute-start.9 = (bf16[2,2,640,128]{3,2,1,0:T(8,128)(2,1)}, bf16[2,2,640,128]{3,2,1,0:T(8,128)(2,1)S(1)}, u32[]{:S(2)}, u32[]{:S(2)}) collective-permute-start(bf16[2,2,640,128]{3,2,1,0:T(8,128)(2,1)} %get-tuple-element.103), channel_id=1, source_target_pairs={{0,2},{1,3},{2,4},{3,5},{4,6},{5,7},{6,8},{7,9},{8,10},{9,11},{10,... | collective-permute-start | bytes 1966088 | tf_op jit(solution)/shard_map/ppermute | solution.py:309
  206.6 0.9 copy-start.12
  212.5 191.2 %collective-permute-start.7 = (bf16[1,2,768,128]{3,2,1,0:T(8,128)(2,1)}, bf16[1,2,768,128]{3,2,1,0:T(8,128)(2,1)S(1)}, u32[]{:S(2)}, u32[]{:S(2)}) collective-permute-start(bf16[1,2,768,128]{3,2,1,0:T(8,128)(2,1)} %get-tuple-element.99), channel_id=1, source_target_pairs={{0,1},{1,0},{2,3},{3,2},{4,5},{5,4},{6,7},{7,6},{8,9},{9,8},{10,11... | collective-permute-start | bytes 1179656 | tf_op jit(solution)/shard_map/ppermute | solution.py:309
  213.0 8.8 %copy-start.16 = (bf16[3,2,640,128]{3,2,1,0:T(8,128)(2,1)}, bf16[3,2,640,128]{3,2,1,0:T(8,128)(2,1)S(1)}, u32[]{:S(2)}) copy-start(bf16[3,2,640,128]{3,2,1,0:T(8,128)(2,1)S(1)} %collective-permute-done.5.refs_8_.refs_9_) | copy-start | bytes 2949124
  213.0 204.2 %collective-permute-start.10 = (bf16[2,2,640,128]{3,2,1,0:T(8,128)(2,1)}, bf16[2,2,640,128]{3,2,1,0:T(8,128)(2,1)}, u32[]{:S(2)}, u32[]{:S(2)}) collective-permute-start(bf16[2,2,640,128]{3,2,1,0:T(8,128)(2,1)} %get-tuple-element.106), channel_id=1, source_target_pairs={{0,2},{1,3},{2,4},{3,5},{4,6},{5,7},{6,8},{7,9},{8,10},{9,11},{10,... | collective-permute-start | bytes 1966088 | tf_op jit(solution)/shard_map/ppermute | solution.py:309
  215.3 208.5 %collective-permute-start.11 = (bf16[2,2,640,128]{3,2,1,0:T(8,128)(2,1)}, bf16[2,2,640,128]{3,2,1,0:T(8,128)(2,1)}, u32[]{:S(2)}, u32[]{:S(2)}) collective-permute-start(bf16[2,2,640,128]{3,2,1,0:T(8,128)(2,1)} %get-tuple-element.107), channel_id=1, source_target_pairs={{2,0},{3,1},{4,2},{5,3},{6,4},{7,5},{8,6},{9,7},{10,8},{11,9},{12,... | collective-permute-start | bytes 1966088 | tf_op jit(solution)/shard_map/ppermute | solution.py:309
  403.7 1.9 copy-start.15
  403.8 146.7 %collective-permute-start.12 = (bf16[3,2,640,128]{3,2,1,0:T(8,128)(2,1)}, bf16[3,2,640,128]{3,2,1,0:T(8,128)(2,1)S(1)}, u32[]{:S(2)}, u32[]{:S(2)}) collective-permute-start(bf16[3,2,640,128]{3,2,1,0:T(8,128)(2,1)} %get-tuple-element.112), channel_id=1, source_target_pairs={{2,0},{3,1},{4,2},{5,3},{6,4},{7,5},{8,6},{9,7},{10,8},{11,9},{12,... | collective-permute-start | bytes 2949128 | tf_op jit(solution)/shard_map/ppermute | solution.py:309
  408.3 5.9 copy-start.4
  408.3 144.1 %collective-permute-start.13 = (bf16[3,2,640,128]{3,2,1,0:T(8,128)(2,1)}, bf16[3,2,640,128]{3,2,1,0:T(8,128)(2,1)S(1)}, u32[]{:S(2)}, u32[]{:S(2)}) collective-permute-start(bf16[3,2,640,128]{3,2,1,0:T(8,128)(2,1)} %get-tuple-element.113), channel_id=1, source_target_pairs={{0,2},{1,3},{2,4},{3,5},{4,6},{5,7},{6,8},{7,9},{8,10},{9,11},{10,... | collective-permute-start | bytes 2949128 | tf_op jit(solution)/shard_map/ppermute | solution.py:309
  412.3 2.0 copy-start.5
  412.3 148.3 %collective-permute-start.14 = (bf16[1,2,640,128]{3,2,1,0:T(8,128)(2,1)}, bf16[1,2,640,128]{3,2,1,0:T(8,128)(2,1)}, u32[]{:S(2)}, u32[]{:S(2)}) collective-permute-start(bf16[1,2,640,128]{3,2,1,0:T(8,128)(2,1)} %get-tuple-element.116), channel_id=1, source_target_pairs={{0,2},{1,3},{2,4},{3,5},{4,6},{5,7},{6,8},{7,9},{8,10},{9,11},{10,... | collective-permute-start | bytes 983048 | tf_op jit(solution)/shard_map/ppermute | solution.py:309
  417.2 143.4 %collective-permute-start.15 = (bf16[1,2,640,128]{3,2,1,0:T(8,128)(2,1)}, bf16[1,2,640,128]{3,2,1,0:T(8,128)(2,1)}, u32[]{:S(2)}, u32[]{:S(2)}) collective-permute-start(bf16[1,2,640,128]{3,2,1,0:T(8,128)(2,1)} %get-tuple-element.117), channel_id=1, source_target_pairs={{2,0},{3,1},{4,2},{5,3},{6,4},{7,5},{8,6},{9,7},{10,8},{11,9},{12,... | collective-permute-start | bytes 983048 | tf_op jit(solution)/shard_map/ppermute | solution.py:309
  423.8 211.3 %collective-permute-start.18 = (bf16[2,2,768,128]{3,2,1,0:T(8,128)(2,1)}, bf16[2,2,768,128]{3,2,1,0:T(8,128)(2,1)S(1)}, u32[]{:S(2)}, u32[]{:S(2)}) collective-permute-start(bf16[2,2,768,128]{3,2,1,0:T(8,128)(2,1)} %get-tuple-element.129), channel_id=1, source_target_pairs={{0,1},{1,0},{2,3},{3,2},{4,5},{5,4},{6,7},{7,6},{8,9},{9,8},{10,11... | collective-permute-start | bytes 2359304 | tf_op jit(solution)/shard_map/ppermute | solution.py:309
  550.5 5.9 copy-start
  550.5 72.9 %collective-permute-start.16 = (bf16[2,2,640,128]{3,2,1,0:T(8,128)(2,1)}, bf16[2,2,640,128]{3,2,1,0:T(8,128)(2,1)S(1)}, u32[]{:S(2)}, u32[]{:S(2)}) collective-permute-start(bf16[2,2,640,128]{3,2,1,0:T(8,128)(2,1)} %get-tuple-element.124), channel_id=1, source_target_pairs={{2,0},{3,1},{4,2},{5,3},{6,4},{7,5},{8,6},{9,7},{10,8},{11,9},{12,... | collective-permute-start | bytes 1966088 | tf_op jit(solution)/shard_map/ppermute | solution.py:309
  552.4 4.0 copy-start.1
  552.4 70.9 %collective-permute-start.17 = (bf16[2,2,640,128]{3,2,1,0:T(8,128)(2,1)}, bf16[2,2,640,128]{3,2,1,0:T(8,128)(2,1)S(1)}, u32[]{:S(2)}, u32[]{:S(2)}) collective-permute-start(bf16[2,2,640,128]{3,2,1,0:T(8,128)(2,1)} %get-tuple-element.125), channel_id=1, source_target_pairs={{0,2},{1,3},{2,4},{3,5},{4,6},{5,7},{6,8},{7,9},{8,10},{9,11},{10,... | collective-permute-start | bytes 1966088 | tf_op jit(solution)/shard_map/ppermute | solution.py:309
  560.6 90.1 %collective-permute-start.21 = (bf16[3,2,768,128]{3,2,1,0:T(8,128)(2,1)}, bf16[3,2,768,128]{3,2,1,0:T(8,128)(2,1)S(1)}, u32[]{:S(2)}, u32[]{:S(2)}) collective-permute-start(bf16[3,2,768,128]{3,2,1,0:T(8,128)(2,1)} %get-tuple-element.137), channel_id=1, source_target_pairs={{0,1},{1,0},{2,3},{3,2},{4,5},{5,4},{6,7},{7,6},{8,9},{9,8},{10,11... | collective-permute-start | bytes 3538952 | tf_op jit(solution)/shard_map/ppermute | solution.py:309
  623.3 0.9 copy-start.2
  623.4 1.1 copy-start.3
  627.4 29.9 %collective-permute-start.22 = (bf16[2,2,768,128]{3,2,1,0:T(8,128)(2,1)}, bf16[2,2,768,128]{3,2,1,0:T(8,128)(2,1)S(1)}, u32[]{:S(2)}, u32[]{:S(2)}) collective-permute-start(bf16[2,2,768,128]{3,2,1,0:T(8,128)(2,1)} %get-tuple-element.143), channel_id=1, source_target_pairs={{0,1},{1,0},{2,3},{3,2},{4,5},{5,4},{6,7},{7,6},{8,9},{9,8},{10,11... | collective-permute-start | bytes 2359304 | tf_op jit(solution)/shard_map/ppermute | solution.py:309
  629.2 10.8 %collective-permute-start.19 = (bf16[1,2,640,128]{3,2,1,0:T(8,128)(2,1)}, bf16[1,2,640,128]{3,2,1,0:T(8,128)(2,1)S(1)}, u32[]{:S(2)}, u32[]{:S(2)}) collective-permute-start(bf16[1,2,640,128]{3,2,1,0:T(8,128)(2,1)} %get-tuple-element.132), channel_id=1, source_target_pairs={{2,0},{3,1},{4,2},{5,3},{6,4},{7,5},{8,6},{9,7},{10,8},{11,9},{12,... | collective-permute-start | bytes 983048 | tf_op jit(solution)/shard_map/ppermute | solution.py:309
  633.3 11.6 %collective-permute-start.20 = (bf16[1,2,640,128]{3,2,1,0:T(8,128)(2,1)}, bf16[1,2,640,128]{3,2,1,0:T(8,128)(2,1)S(1)}, u32[]{:S(2)}, u32[]{:S(2)}) collective-permute-start(bf16[1,2,640,128]{3,2,1,0:T(8,128)(2,1)} %get-tuple-element.133), channel_id=1, source_target_pairs={{0,2},{1,3},{2,4},{3,5},{4,6},{5,7},{6,8},{7,9},{8,10},{9,11},{10,... | collective-permute-start | bytes 983048 | tf_op jit(solution)/shard_map/ppermute | solution.py:309
  635.2 0.9 copy-start.10
  640.0 4.9 copy-start.6
  644.9 0.7 copy-start.7
  648.0 14.1 %collective-permute-start.23 = (bf16[1,2,768,128]{3,2,1,0:T(8,128)(2,1)}, bf16[1,2,768,128]{3,2,1,0:T(8,128)(2,1)S(1)}, u32[]{:S(2)}, u32[]{:S(2)}) collective-permute-start(bf16[1,2,768,128]{3,2,1,0:T(8,128)(2,1)} %get-tuple-element.149), channel_id=1, source_target_pairs={{0,1},{1,0},{2,3},{3,2},{4,5},{5,4},{6,7},{7,6},{8,9},{9,8},{10,11... | collective-permute-start | bytes 1179656 | tf_op jit(solution)/shard_map/ppermute | solution.py:309
  650.7 1.1 copy-start.8
  657.3 0.9 copy-start.11
  662.1 0.8 copy-start.14

commit v5 on v4

--- a/solution.py
+++ b/solution.py
@@ -15,8 +15,8 @@
 GROUPS = (2, 3, 2, 1)
 ORDER = (
     ("pair", 0), ("cross", 0), ("pair", 1),
-    ("attend", 0), ("cross", 1), ("pair", 2), ("cross", 2), ("pair", 3),
-    ("attend", 1), ("cross", 3), ("back", 0),
+    ("attend", 0), ("cross", 1), ("pair", 2), ("pair", 3),
+    ("attend", 1), ("cross", 2), ("cross", 3), ("back", 0),
     ("attend", 2), ("back", 1),
     ("attend", 3), ("back", 2), ("sum", 0), ("back", 3), ("sum", 1), ("sum", 2), ("sum", 3),
 )

time: 675 us -> 682 us (1.010)
  transfers between devices with their start and end apart: 24 -> 24, of which waited for: 5 -> 8; matrix products, arithmetic and copies ran while one was open for 0% -> 0% of each run, Pallas kernels for 79% -> 79%
where the time goes in v5:
time: 682 us; the launch traced here: 672 us
  Pallas kernels  541 us (79%)
  starting transfers between devices  71.3 us (10%)
  waiting for transfers between devices  48.2 us (7%)
  local copies, waits for them, and re-layouts  9.08 us (1%)
    pallas_call x4, Pallas kernels, attend(): pl.pallas_call(body, grid=(pairs,), in_specs=[SMEM, SMEM] + [columns(star...  489 us
    ppermute x24, starting transfers between devices, moved(): return lax.ppermute(array, AXES, pairs)  71.3 us
    ppermute x24, waiting for transfers between devices, moved(): return lax.ppermute(array, AXES, pairs)  48.2 us
    pallas_call x4, Pallas kernels, finish(): pl.pallas_call(body, grid=(pairs,), in_specs=[SMEM] + [own_rows()] * 2 +...  16.4 us
    pallas_call x4, Pallas kernels, cross_rows(): pl.pallas_call(body, grid=(pairs,), in_specs=[SMEM, columns(start), colum...  13.7 us
  transfers between devices with their start and end apart: 24, of which 8 were waited for; matrix products, arithmetic and copies ran while one was open for 0% of the time, Pallas kernels for 79%

profile of v5, /device:TPU:36, one launch (start us, length us, event | category | flops | bytes accessed | tf_op | source)
XLA Modules:
  0.0 672.2 jit_solution(14237465187234067901)
XLA Ops:
  1.3 2.1 pair_rows.4
  3.4 19.4 %collective-permute-done.p = bf16[2,2,768,128]{3,2,1,0:T(8,128)(2,1)S(1)} collective-permute-done((bf16[2,2,768,128]{3,2,1,0:T(8,128)(2,1)}, bf16[2,2,768,128]{3,2,1,0:T(8,128)(2,1)S(1)}, u32[]{:S(2)}, u32[]{:S(2)}) %collective-permute-start) | collective-permute-done | bytes 786464 | tf_op jit(solution)/shard_map/ppermute | solution.py:309
  23.7 3.1 cross_rows.4
  26.8 3.5 collective-permute-start.1
  30.3 5.1 collective-permute-start.2
  36.0 3.3 pair_rows.5
  39.3 1.6 collective-permute-start.3
  40.9 2.7 collective-permute-done.1.refs_8_.refs_9_
  43.7 4.0 collective-permute-done.2.refs_10_.refs_11_
  48.5 122.2 %attend_pairs.4 = (bf16[1024,1024]{1,0:T(8,128)(2,1)}, bf16[1024,1024]{1,0:T(8,128)(2,1)}, f32[2,1024,128]{2,1,0:T(8,128)}, f32[2,1024,128]{2,1,0:T(8,128)}, bf1...) custom-call(s32[2]{0:T(128)} %get-tuple-element.82.refs_0_, ...), custom_call_target="tpu_custom_call" | custom-call | flops 28000000000 | bytes 8000000 | tf_op jit(solution)/shard_map/attend_pairs/pallas_call | solution.py:450
  171.7 4.8 cross_rows.5
  176.5 3.5 collective-permute-start.4
  180.0 5.1 collective-permute-start.5
  185.1 1.9 collective-permute-start.8
  187.0 3.9 collective-permute-start.9
  191.0 2.1 pair_rows.6
  193.1 1.9 pair_rows.7
  195.0 1.9 collective-permute-start.6
  196.9 5.6 collective-permute-done.4.refs_8_.refs_9_
  202.5 5.1 collective-permute-done.5.refs_10_.refs_11_
  207.6 181.9 %attend_pairs.5 = (bf16[1024,1024]{1,0:T(8,128)(2,1)}, bf16[1024,1024]{1,0:T(8,128)(2,1)}, f32[3,1024,128]{2,1,0:T(8,128)}, f32[3,1024,128]{2,1,0:T(8,128)}, bf1...) custom-call(s32[2]{0:T(128)} %get-tuple-element.90.refs_0_, ...), custom_call_target="tpu_custom_call", output_to_operand_aliasing={{0}: (12, {}), {1}: (13, {})} | custom-call | flops 41999998976 | bytes 12000000 | tf_op jit(solution)/shard_map/attend_pairs/pallas_call | solution.py:450
  390.4 3.2 cross_rows.6
  393.6 3.8 collective-permute-start.10
  397.4 4.7 collective-permute-start.11
  403.6 6.4 collective-permute-done.7.p
  410.1 1.9 collective-permute-start.12
  412.0 2.6 cross_rows.7
  414.6 3.9 collective-permute-start.13
  418.5 6.3 collective-permute-start.14
  424.9 3.0 pair_grads.4
  427.8 2.3 collective-permute-start.15
  430.1 4.0 collective-permute-start.18
  434.1 122.2 %attend_pairs.6 = (bf16[1024,1024]{1,0:T(8,128)(2,1)}, bf16[1024,1024]{1,0:T(8,128)(2,1)}, f32[2,1024,128]{2,1,0:T(8,128)}, f32[2,1024,128]{2,1,0:T(8,128)}, bf1...) custom-call(s32[2]{0:T(128)} %get-tuple-element.104.refs_0_, ...), custom_call_target="tpu_custom_call", output_to_operand_aliasing={{0}: (12, {}), {1}: (13, {})} | custom-call | flops 28000000000 | bytes 8000000 | tf_op jit(solution)/shard_map/attend_pairs/pallas_call | solution.py:450
  556.4 1.9 collective-permute-start.16
  558.3 3.9 collective-permute-start.17
  562.3 4.2 pair_grads.5
  566.5 62.7 %attend_pairs.7 = (bf16[1024,1024]{1,0:T(8,128)(2,1)}, bf16[1024,1024]{1,0:T(8,128)(2,1)}, f32[1,1024,128]{2,1,0:T(8,128)}, f32[1,1024,128]{2,1,0:T(8,128)}, bf1...) custom-call(s32[2]{0:T(128)} %get-tuple-element.114.refs_0_, ...), custom_call_target="tpu_custom_call", output_to_operand_aliasing={{0}: (12, {}), {1}: (13, {})} | custom-call | flops 14000000000 | bytes 4000000 | tf_op jit(solution)/shard_map/attend_pairs/pallas_call | solution.py:450
  630.3 2.9 pair_grads.6
  633.3 1.8 collective-permute-start.22
  635.1 4.1 collective-permute-start.19
  639.1 1.9 collective-permute-start.20
  642.0 3.9 sum_grads.4
  646.8 4.0 collective-permute-done.20.below.refs_4_
  651.6 2.4 pair_grads.7
  654.0 2.6 collective-permute-start.23
  657.8 5.5 sum_grads.5
  664.2 3.9 sum_grads.6
  668.8 3.1 sum_grads.7
  (63 shorter events, 12.8 us)
Async XLA Ops:
  3.3 19.5 %collective-permute-start = (bf16[2,2,768,128]{3,2,1,0:T(8,128)(2,1)}, bf16[2,2,768,128]{3,2,1,0:T(8,128)(2,1)S(1)}, u32[]{:S(2)}, u32[]{:S(2)}) collective-permute-start(bf16[2,2,768,128]{3,2,1,0:T(8,128)(2,1)} %get-tuple-element.80), channel_id=1, source_target_pairs={{0,1},{1,0},{2,3},{3,2},{4,5},{5,4},{6,7},{7,6},{8,9},{9,8},{10,11... | collective-permute-start | bytes 2359304 | tf_op jit(solution)/shard_map/ppermute | solution.py:309
  22.8 0.9 copy-start.13
  26.8 16.9 %collective-permute-start.1 = (bf16[2,2,640,128]{3,2,1,0:T(8,128)(2,1)}, bf16[2,2,640,128]{3,2,1,0:T(8,128)(2,1)S(1)}, u32[]{:S(2)}, u32[]{:S(2)}) collective-permute-start(bf16[2,2,640,128]{3,2,1,0:T(8,128)(2,1)} %get-tuple-element.84), channel_id=1, source_target_pairs={{0,2},{1,3},{2,4},{3,5},{4,6},{5,7},{6,8},{7,9},{8,10},{9,11},{10,... | collective-permute-start | bytes 1966088 | tf_op jit(solution)/shard_map/ppermute | solution.py:309
  30.3 17.4 %collective-permute-start.2 = (bf16[2,2,640,128]{3,2,1,0:T(8,128)(2,1)}, bf16[2,2,640,128]{3,2,1,0:T(8,128)(2,1)S(1)}, u32[]{:S(2)}, u32[]{:S(2)}) collective-permute-start(bf16[2,2,640,128]{3,2,1,0:T(8,128)(2,1)} %get-tuple-element.85), channel_id=1, source_target_pairs={{2,0},{3,1},{4,2},{5,3},{6,4},{7,5},{8,6},{9,7},{10,8},{11,9},{12,... | collective-permute-start | bytes 1966088 | tf_op jit(solution)/shard_map/ppermute | solution.py:309
  39.3 131.4 %collective-permute-start.3 = (bf16[3,2,768,128]{3,2,1,0:T(8,128)(2,1)}, bf16[3,2,768,128]{3,2,1,0:T(8,128)(2,1)S(1)}, u32[]{:S(2)}, u32[]{:S(2)}) collective-permute-start(bf16[3,2,768,128]{3,2,1,0:T(8,128)(2,1)} %get-tuple-element.87), channel_id=1, source_target_pairs={{0,1},{1,0},{2,3},{3,2},{4,5},{5,4},{6,7},{7,6},{8,9},{9,8},{10,11... | collective-permute-start | bytes 3538952 | tf_op jit(solution)/shard_map/ppermute | solution.py:309
  43.7 4.0 copy-start.17
  47.7 0.8 copy-start.18
  170.7 1.0 copy-start.9
  176.5 26.0 %collective-permute-start.4 = (bf16[3,2,640,128]{3,2,1,0:T(8,128)(2,1)}, bf16[3,2,640,128]{3,2,1,0:T(8,128)(2,1)S(1)}, u32[]{:S(2)}, u32[]{:S(2)}) collective-permute-start(bf16[3,2,640,128]{3,2,1,0:T(8,128)(2,1)} %get-tuple-element.92), channel_id=1, source_target_pairs={{0,2},{1,3},{2,4},{3,5},{4,6},{5,7},{6,8},{7,9},{8,10},{9,11},{10,... | collective-permute-start | bytes 2949128 | tf_op jit(solution)/shard_map/ppermute | solution.py:309
  180.0 27.6 %collective-permute-start.5 = (bf16[3,2,640,128]{3,2,1,0:T(8,128)(2,1)}, bf16[3,2,640,128]{3,2,1,0:T(8,128)(2,1)}, u32[]{:S(2)}, u32[]{:S(2)}) collective-permute-start(bf16[3,2,640,128]{3,2,1,0:T(8,128)(2,1)} %get-tuple-element.93), channel_id=1, source_target_pairs={{2,0},{3,1},{4,2},{5,3},{6,4},{7,5},{8,6},{9,7},{10,8},{11,9},{12,... | collective-permute-start | bytes 2949128 | tf_op jit(solution)/shard_map/ppermute | solution.py:309
  185.1 229.5 %collective-permute-start.8 = (bf16[2,2,640,128]{3,2,1,0:T(8,128)(2,1)}, bf16[2,2,640,128]{3,2,1,0:T(8,128)(2,1)S(1)}, u32[]{:S(2)}, u32[]{:S(2)}) collective-permute-start(bf16[2,2,640,128]{3,2,1,0:T(8,128)(2,1)} %get-tuple-element.102), channel_id=1, source_target_pairs={{2,0},{3,1},{4,2},{5,3},{6,4},{7,5},{8,6},{9,7},{10,8},{11,9},{12,... | collective-permute-start | bytes 1966088 | tf_op jit(solution)/shard_map/ppermute | solution.py:309
  187.0 231.5 %collective-permute-start.9 = (bf16[2,2,640,128]{3,2,1,0:T(8,128)(2,1)}, bf16[2,2,640,128]{3,2,1,0:T(8,128)(2,1)S(1)}, u32[]{:S(2)}, u32[]{:S(2)}) collective-permute-start(bf16[2,2,640,128]{3,2,1,0:T(8,128)(2,1)} %get-tuple-element.103), channel_id=1, source_target_pairs={{0,2},{1,3},{2,4},{3,5},{4,6},{5,7},{6,8},{7,9},{8,10},{9,11},{10,... | collective-permute-start | bytes 1966088 | tf_op jit(solution)/shard_map/ppermute | solution.py:309
  195.0 194.5 %collective-permute-start.6 = (bf16[2,2,768,128]{3,2,1,0:T(8,128)(2,1)}, bf16[2,2,768,128]{3,2,1,0:T(8,128)(2,1)S(1)}, u32[]{:S(2)}, u32[]{:S(2)}) collective-permute-start(bf16[2,2,768,128]{3,2,1,0:T(8,128)(2,1)} %get-tuple-element.97), channel_id=1, source_target_pairs={{0,1},{1,0},{2,3},{3,2},{4,5},{5,4},{6,7},{7,6},{8,9},{9,8},{10,11... | collective-permute-start | bytes 2359304 | tf_op jit(solution)/shard_map/ppermute | solution.py:309
  202.5 5.1 copy-start.16
  389.5 0.9 copy-start.12
  390.3 11.8 %copy-start.19 = (bf16[1,2,768,128]{3,2,1,0:T(8,128)(2,1)S(1)}, bf16[1,2,768,128]{3,2,1,0:T(8,128)(2,1)}, u32[]{:S(2)}) copy-start(bf16[1,2,768,128]{3,2,1,0:T(8,128)(2,1)} %get-tuple-element.99) | copy-start | bytes 1179652
  393.6 34.3 %collective-permute-start.10 = (bf16[2,2,640,128]{3,2,1,0:T(8,128)(2,1)}, bf16[2,2,640,128]{3,2,1,0:T(8,128)(2,1)}, u32[]{:S(2)}, u32[]{:S(2)}) collective-permute-start(bf16[2,2,640,128]{3,2,1,0:T(8,128)(2,1)} %get-tuple-element.106), channel_id=1, source_target_pairs={{0,2},{1,3},{2,4},{3,5},{4,6},{5,7},{6,8},{7,9},{8,10},{9,11},{10,... | collective-permute-start | bytes 1966088 | tf_op jit(solution)/shard_map/ppermute | solution.py:309
  397.4 32.7 %collective-permute-start.11 = (bf16[2,2,640,128]{3,2,1,0:T(8,128)(2,1)}, bf16[2,2,640,128]{3,2,1,0:T(8,128)(2,1)}, u32[]{:S(2)}, u32[]{:S(2)}) collective-permute-start(bf16[2,2,640,128]{3,2,1,0:T(8,128)(2,1)} %get-tuple-element.107), channel_id=1, source_target_pairs={{2,0},{3,1},{4,2},{5,3},{6,4},{7,5},{8,6},{9,7},{10,8},{11,9},{12,... | collective-permute-start | bytes 1966088 | tf_op jit(solution)/shard_map/ppermute | solution.py:309
  402.2 7.9 %collective-permute-start.7 = (bf16[1,2,768,128]{3,2,1,0:T(8,128)(2,1)S(1)}, bf16[1,2,768,128]{3,2,1,0:T(8,128)(2,1)S(1)}, u32[]{:S(2)}, u32[]{:S(2)}) collective-permute-start(bf16[1,2,768,128]{3,2,1,0:T(8,128)(2,1)S(1)} %copy-done.19), channel_id=1, source_target_pairs={{0,1},{1,0},{2,3},{3,2},{4,5},{5,4},{6,7},{7,6},{8,9},{9,8},{10,11... | collective-permute-start | bytes 1179656 | tf_op jit(solution)/shard_map/ppermute | solution.py:309
  410.0 1.9 copy-start.15
  410.1 146.3 %collective-permute-start.12 = (bf16[3,2,640,128]{3,2,1,0:T(8,128)(2,1)}, bf16[3,2,640,128]{3,2,1,0:T(8,128)(2,1)S(1)}, u32[]{:S(2)}, u32[]{:S(2)}) collective-permute-start(bf16[3,2,640,128]{3,2,1,0:T(8,128)(2,1)} %get-tuple-element.112), channel_id=1, source_target_pairs={{2,0},{3,1},{4,2},{5,3},{6,4},{7,5},{8,6},{9,7},{10,8},{11,9},{12,... | collective-permute-start | bytes 2949128 | tf_op jit(solution)/shard_map/ppermute | solution.py:309
  414.6 10.3 %copy-start.4 = (bf16[2,2,640,128]{3,2,1,0:T(8,128)(2,1)}, bf16[2,2,640,128]{3,2,1,0:T(8,128)(2,1)S(1)}, u32[]{:S(2)}) copy-start(bf16[2,2,640,128]{3,2,1,0:T(8,128)(2,1)S(1)} %collective-permute-done.8.above.refs_3_) | copy-start | bytes 1966084
  414.6 143.7 %collective-permute-start.13 = (bf16[3,2,640,128]{3,2,1,0:T(8,128)(2,1)}, bf16[3,2,640,128]{3,2,1,0:T(8,128)(2,1)S(1)}, u32[]{:S(2)}, u32[]{:S(2)}) collective-permute-start(bf16[3,2,640,128]{3,2,1,0:T(8,128)(2,1)} %get-tuple-element.113), channel_id=1, source_target_pairs={{0,2},{1,3},{2,4},{3,5},{4,6},{5,7},{6,8},{7,9},{8,10},{9,11},{10,... | collective-permute-start | bytes 2949128 | tf_op jit(solution)/shard_map/ppermute | solution.py:309
  418.5 6.3 copy-start.5
  418.5 147.9 %collective-permute-start.14 = (bf16[1,2,640,128]{3,2,1,0:T(8,128)(2,1)}, bf16[1,2,640,128]{3,2,1,0:T(8,128)(2,1)}, u32[]{:S(2)}, u32[]{:S(2)}) collective-permute-start(bf16[1,2,640,128]{3,2,1,0:T(8,128)(2,1)} %get-tuple-element.116), channel_id=1, source_target_pairs={{0,2},{1,3},{2,4},{3,5},{4,6},{5,7},{6,8},{7,9},{8,10},{9,11},{10,... | collective-permute-start | bytes 983048 | tf_op jit(solution)/shard_map/ppermute | solution.py:309
  427.8 138.7 %collective-permute-start.15 = (bf16[1,2,640,128]{3,2,1,0:T(8,128)(2,1)}, bf16[1,2,640,128]{3,2,1,0:T(8,128)(2,1)}, u32[]{:S(2)}, u32[]{:S(2)}) collective-permute-start(bf16[1,2,640,128]{3,2,1,0:T(8,128)(2,1)} %get-tuple-element.117), channel_id=1, source_target_pairs={{2,0},{3,1},{4,2},{5,3},{6,4},{7,5},{8,6},{9,7},{10,8},{11,9},{12,... | collective-permute-start | bytes 983048 | tf_op jit(solution)/shard_map/ppermute | solution.py:309
  430.1 211.0 %collective-permute-start.18 = (bf16[2,2,768,128]{3,2,1,0:T(8,128)(2,1)}, bf16[2,2,768,128]{3,2,1,0:T(8,128)(2,1)S(1)}, u32[]{:S(2)}, u32[]{:S(2)}) collective-permute-start(bf16[2,2,768,128]{3,2,1,0:T(8,128)(2,1)} %get-tuple-element.129), channel_id=1, source_target_pairs={{0,1},{1,0},{2,3},{3,2},{4,5},{5,4},{6,7},{7,6},{8,9},{9,8},{10,11... | collective-permute-start | bytes 2359304 | tf_op jit(solution)/shard_map/ppermute | solution.py:309
  556.3 5.9 copy-start
  556.4 72.9 %collective-permute-start.16 = (bf16[2,2,640,128]{3,2,1,0:T(8,128)(2,1)}, bf16[2,2,640,128]{3,2,1,0:T(8,128)(2,1)S(1)}, u32[]{:S(2)}, u32[]{:S(2)}) collective-permute-start(bf16[2,2,640,128]{3,2,1,0:T(8,128)(2,1)} %get-tuple-element.124), channel_id=1, source_target_pairs={{2,0},{3,1},{4,2},{5,3},{6,4},{7,5},{8,6},{9,7},{10,8},{11,9},{12,... | collective-permute-start | bytes 1966088 | tf_op jit(solution)/shard_map/ppermute | solution.py:309
  558.3 4.0 copy-start.1
  558.3 71.0 %collective-permute-start.17 = (bf16[2,2,640,128]{3,2,1,0:T(8,128)(2,1)}, bf16[2,2,640,128]{3,2,1,0:T(8,128)(2,1)S(1)}, u32[]{:S(2)}, u32[]{:S(2)}) collective-permute-start(bf16[2,2,640,128]{3,2,1,0:T(8,128)(2,1)} %get-tuple-element.125), channel_id=1, source_target_pairs={{0,2},{1,3},{2,4},{3,5},{4,6},{5,7},{6,8},{7,9},{8,10},{9,11},{10,... | collective-permute-start | bytes 1966088 | tf_op jit(solution)/shard_map/ppermute | solution.py:309
  566.5 90.2 %collective-permute-start.21 = (bf16[3,2,768,128]{3,2,1,0:T(8,128)(2,1)}, bf16[3,2,768,128]{3,2,1,0:T(8,128)(2,1)S(1)}, u32[]{:S(2)}, u32[]{:S(2)}) collective-permute-start(bf16[3,2,768,128]{3,2,1,0:T(8,128)(2,1)} %get-tuple-element.137), channel_id=1, source_target_pairs={{0,1},{1,0},{2,3},{3,2},{4,5},{5,4},{6,7},{7,6},{8,9},{9,8},{10,11... | collective-permute-start | bytes 3538952 | tf_op jit(solution)/shard_map/ppermute | solution.py:309
  629.2 0.9 copy-start.2
  629.3 1.0 copy-start.3
  633.3 30.0 %collective-permute-start.22 = (bf16[2,2,768,128]{3,2,1,0:T(8,128)(2,1)}, bf16[2,2,768,128]{3,2,1,0:T(8,128)(2,1)S(1)}, u32[]{:S(2)}, u32[]{:S(2)}) collective-permute-start(bf16[2,2,768,128]{3,2,1,0:T(8,128)(2,1)} %get-tuple-element.143), channel_id=1, source_target_pairs={{0,1},{1,0},{2,3},{3,2},{4,5},{5,4},{6,7},{7,6},{8,9},{9,8},{10,11... | collective-permute-start | bytes 2359304 | tf_op jit(solution)/shard_map/ppermute | solution.py:309
  635.1 11.8 %collective-permute-start.19 = (bf16[1,2,640,128]{3,2,1,0:T(8,128)(2,1)}, bf16[1,2,640,128]{3,2,1,0:T(8,128)(2,1)S(1)}, u32[]{:S(2)}, u32[]{:S(2)}) collective-permute-start(bf16[1,2,640,128]{3,2,1,0:T(8,128)(2,1)} %get-tuple-element.132), channel_id=1, source_target_pairs={{2,0},{3,1},{4,2},{5,3},{6,4},{7,5},{8,6},{9,7},{10,8},{11,9},{12,... | collective-permute-start | bytes 983048 | tf_op jit(solution)/shard_map/ppermute | solution.py:309
  639.1 11.7 %collective-permute-start.20 = (bf16[1,2,640,128]{3,2,1,0:T(8,128)(2,1)}, bf16[1,2,640,128]{3,2,1,0:T(8,128)(2,1)S(1)}, u32[]{:S(2)}, u32[]{:S(2)}) collective-permute-start(bf16[1,2,640,128]{3,2,1,0:T(8,128)(2,1)} %get-tuple-element.133), channel_id=1, source_target_pairs={{0,2},{1,3},{2,4},{3,5},{4,6},{5,7},{6,8},{7,9},{8,10},{9,11},{10,... | collective-permute-start | bytes 983048 | tf_op jit(solution)/shard_map/ppermute | solution.py:309
  641.1 0.9 copy-start.10
  646.8 4.0 copy-start.6
  650.9 0.7 copy-start.7
  654.0 14.1 %collective-permute-start.23 = (bf16[1,2,768,128]{3,2,1,0:T(8,128)(2,1)}, bf16[1,2,768,128]{3,2,1,0:T(8,128)(2,1)S(1)}, u32[]{:S(2)}, u32[]{:S(2)}) collective-permute-start(bf16[1,2,768,128]{3,2,1,0:T(8,128)(2,1)} %get-tuple-element.149), channel_id=1, source_target_pairs={{0,1},{1,0},{2,3},{3,2},{4,5},{5,4},{6,7},{7,6},{8,9},{9,8},{10,11... | collective-permute-start | bytes 1179656 | tf_op jit(solution)/shard_map/ppermute | solution.py:309
  656.7 1.1 copy-start.8
  663.3 0.9 copy-start.11
  668.1 0.7 copy-start.14

commit v6 on v4

--- a/solution.py
+++ b/solution.py
@@ -12,7 +12,7 @@
 HALF = 128
 PAIR = 128
 AXES = ("seqa", "seqb")
-GROUPS = (2, 3, 2, 1)
+GROUPS = (1, 3, 3, 1)
 ORDER = (
     ("pair", 0), ("cross", 0), ("pair", 1),
     ("attend", 0), ("cross", 1), ("pair", 2), ("cross", 2), ("pair", 3),

time: 675 us -> 684 us (1.013)
  transfers between devices with their start and end apart: 24 -> 24, of which waited for: 5 -> 3; matrix products, arithmetic and copies ran while one was open for 0% -> 0% of each run, Pallas kernels for 79% -> 79%
where the time goes in v6:
time: 684 us; the launch traced here: 673 us
  Pallas kernels  545 us (80%)
  starting transfers between devices  68.1 us (10%)
  waiting for transfers between devices  46.7 us (7%)
  local copies, waits for them, and re-layouts  10.4 us (2%)
    pallas_call x4, Pallas kernels, attend(): pl.pallas_call(body, grid=(pairs,), in_specs=[SMEM, SMEM] + [columns(star...  489 us
    ppermute x24, starting transfers between devices, moved(): return lax.ppermute(array, AXES, pairs)  68.1 us
    ppermute x24, waiting for transfers between devices, moved(): return lax.ppermute(array, AXES, pairs)  46.7 us
    pallas_call x4, Pallas kernels, finish(): pl.pallas_call(body, grid=(pairs,), in_specs=[SMEM] + [own_rows()] * 2 +...  17.2 us
    pallas_call x4, Pallas kernels, cross_rows(): pl.pallas_call(body, grid=(pairs,), in_specs=[SMEM, columns(start), colum...  14.8 us
  transfers between devices with their start and end apart: 24, of which 3 were waited for; matrix products, arithmetic and copies ran while one was open for 0% of the time, Pallas kernels for 79%

profile of v6, /device:TPU:36, one launch (start us, length us, event | category | flops | bytes accessed | tf_op | source)
XLA Modules:
  0.0 672.9 jit_solution(6169112298573459828)
XLA Ops:
  1.3 1.9 pair_rows.4
  3.3 11.0 %collective-permute-done.p = bf16[1,2,768,128]{3,2,1,0:T(8,128)(2,1)S(1)} collective-permute-done((bf16[1,2,768,128]{3,2,1,0:T(8,128)(2,1)}, bf16[1,2,768,128]{3,2,1,0:T(8,128)(2,1)S(1)}, u32[]{:S(2)}, u32[]{:S(2)}) %collective-permute-start) | collective-permute-done | bytes 393248 | tf_op jit(solution)/shard_map/ppermute | solution.py:309
  15.0 2.6 cross_rows.4
  17.6 3.5 collective-permute-start.1
  21.1 5.1 collective-permute-start.2
  26.9 3.3 pair_rows.5
  30.3 1.5 collective-permute-start.3
  32.6 62.5 %attend_pairs.4 = (bf16[1024,1024]{1,0:T(8,128)(2,1)}, bf16[1024,1024]{1,0:T(8,128)(2,1)}, f32[1,1024,128]{2,1,0:T(8,128)}, f32[1,1024,128]{2,1,0:T(8,128)}, bf1...) custom-call(s32[2]{0:T(128)} %get-tuple-element.82.refs_0_, ...), custom_call_target="tpu_custom_call" | custom-call | flops 14000000000 | bytes 4000000 | tf_op jit(solution)/shard_map/attend_pairs/pallas_call | solution.py:450
  95.2 1.0 copy-done.10
  96.2 4.8 cross_rows.5
  101.0 3.4 pair_rows.6
  105.1 2.9 collective-permute-start.5
  108.0 6.1 collective-permute-start.6
  114.1 3.4 collective-permute-start.8
  117.5 2.5 collective-permute-start.9
  119.9 13.1 %collective-permute-done.4.p = bf16[3,2,768,128]{3,2,1,0:T(8,128)(2,1)S(1)} collective-permute-done((bf16[3,2,768,128]{3,2,1,0:T(8,128)(2,1)}, bf16[3,2,768,128]{3,2,1,0:T(8,128)(2,1)S(1)}, u32[]{:S(2)}, u32[]{:S(2)}) %collective-permute-start.4) | collective-permute-done | bytes 1179680 | tf_op jit(solution)/shard_map/ppermute | solution.py:309
  133.0 1.0 copy-done.11
  134.0 4.8 cross_rows.6
  138.9 2.0 pair_rows.7
  141.2 1.9 collective-permute-start.10
  143.1 6.9 %collective-permute-start.11 = (bf16[3,2,640,128]{3,2,1,0:T(8,128)(2,1)S(1)}, bf16[3,2,640,128]{3,2,1,0:T(8,128)(2,1)}, u32[]{:S(2)}, u32[]{:S(2)}) collective-permute-start(bf16[3,2,640,128]{3,2,1,0:T(8,128)(2,1)S(1)} %copy-done.16), channel_id=1, source_target_pairs={{2,0},{3,1},{4,2},{5,3},{6,4},{7,5},{8,6},{9,7},{10,8},{11,9},{12,... | collective-permute-start | bytes 2949128 | tf_op jit(solution)/shard_map/ppermute | solution.py:309
  150.0 181.9 %attend_pairs.5 = (bf16[1024,1024]{1,0:T(8,128)(2,1)}, bf16[1024,1024]{1,0:T(8,128)(2,1)}, f32[3,1024,128]{2,1,0:T(8,128)}, f32[3,1024,128]{2,1,0:T(8,128)}, bf1...) custom-call(s32[2]{0:T(128)} %get-tuple-element.92.refs_0_, ...), custom_call_target="tpu_custom_call", output_to_operand_aliasing={{0}: (12, {}), {1}: (13, {})} | custom-call | flops 41999998976 | bytes 12000000 | tf_op jit(solution)/shard_map/attend_pairs/pallas_call | solution.py:450
  331.9 2.5 collective-permute-start.12
  334.4 2.6 cross_rows.7
  337.0 3.4 collective-permute-start.13
  340.4 1.9 collective-permute-start.14
  342.4 2.4 pair_grads.4
  344.8 7.0 %collective-permute-start.15 = (bf16[1,2,640,128]{3,2,1,0:T(8,128)(2,1)}, bf16[1,2,640,128]{3,2,1,0:T(8,128)(2,1)}, u32[]{:S(2)}, u32[]{:S(2)}) collective-permute-start(bf16[1,2,640,128]{3,2,1,0:T(8,128)(2,1)} %get-tuple-element.117), channel_id=1, source_target_pairs={{2,0},{3,1},{4,2},{5,3},{6,4},{7,5},{8,6},{9,7},{10,8},{11,9},{12,... | collective-permute-start | bytes 983048 | tf_op jit(solution)/shard_map/ppermute | solution.py:309
  351.9 181.9 %attend_pairs.6 = (bf16[1024,1024]{1,0:T(8,128)(2,1)}, bf16[1024,1024]{1,0:T(8,128)(2,1)}, f32[3,1024,128]{2,1,0:T(8,128)}, f32[3,1024,128]{2,1,0:T(8,128)}, bf1...) custom-call(s32[2]{0:T(128)} %get-tuple-element.104.refs_0_, ...), custom_call_target="tpu_custom_call", output_to_operand_aliasing={{0}: (12, {}), {1}: (13, {})} | custom-call | flops 41999998976 | bytes 12000000 | tf_op jit(solution)/shard_map/attend_pairs/pallas_call | solution.py:450
  533.8 1.9 collective-permute-start.16
  535.7 3.9 collective-permute-start.17
  539.7 0.9 copy-done.1
  540.6 4.3 pair_grads.5
  544.9 3.9 collective-permute-start.21
  548.8 62.7 %attend_pairs.7 = (bf16[1024,1024]{1,0:T(8,128)(2,1)}, bf16[1024,1024]{1,0:T(8,128)(2,1)}, f32[1,1024,128]{2,1,0:T(8,128)}, f32[1,1024,128]{2,1,0:T(8,128)}, bf1...) custom-call(s32[2]{0:T(128)} %get-tuple-element.114.refs_0_, ...), custom_call_target="tpu_custom_call", output_to_operand_aliasing={{0}: (12, {}), {1}: (13, {})} | custom-call | flops 14000000000 | bytes 4000000 | tf_op jit(solution)/shard_map/attend_pairs/pallas_call | solution.py:450
  611.6 0.9 copy-done.2
  612.9 4.2 pair_grads.6
  617.2 2.0 collective-permute-start.18
  619.2 4.4 collective-permute-start.19
  623.6 1.9 collective-permute-start.20
  625.6 22.6 %collective-permute-done.18.refs_5_ = bf16[1,2,768,128]{3,2,1,0:T(8,128)(2,1)S(1)} collective-permute-done((bf16[1,2,768,128]{3,2,1,0:T(8,128)(2,1)}, bf16[1,2,768,128]{3,2,1,0:T(8,128)(2,1)S(1)}, u32[]{:S(2)}, u32[]{:S(2)}) %collective-permute-start.18) | collective-permute-done | bytes 393248 | tf_op jit(solution)/shard_map/ppermute | solution.py:309
  648.9 3.1 sum_grads.4
  652.8 2.4 pair_grads.7
  655.6 1.0 copy-done.8
  656.6 5.5 sum_grads.5
  662.2 1.1 copy-done.9
  663.2 5.5 sum_grads.6
  669.5 3.1 sum_grads.7
  (65 shorter events, 7.2 us)
Async XLA Ops:
  3.2 11.1 %collective-permute-start = (bf16[1,2,768,128]{3,2,1,0:T(8,128)(2,1)}, bf16[1,2,768,128]{3,2,1,0:T(8,128)(2,1)S(1)}, u32[]{:S(2)}, u32[]{:S(2)}) collective-permute-start(bf16[1,2,768,128]{3,2,1,0:T(8,128)(2,1)} %get-tuple-element.80), channel_id=1, source_target_pairs={{0,1},{1,0},{2,3},{3,2},{4,5},{5,4},{6,7},{7,6},{8,9},{9,8},{10,11... | collective-permute-start | bytes 1179656 | tf_op jit(solution)/shard_map/ppermute | solution.py:309
  14.3 0.7 copy-start.15
  17.6 14.2 %collective-permute-start.1 = (bf16[1,2,640,128]{3,2,1,0:T(8,128)(2,1)}, bf16[1,2,640,128]{3,2,1,0:T(8,128)(2,1)S(1)}, u32[]{:S(2)}, u32[]{:S(2)}) collective-permute-start(bf16[1,2,640,128]{3,2,1,0:T(8,128)(2,1)} %get-tuple-element.84), channel_id=1, source_target_pairs={{0,2},{1,3},{2,4},{3,5},{4,6},{5,7},{6,8},{7,9},{8,10},{9,11},{10,... | collective-permute-start | bytes 983048 | tf_op jit(solution)/shard_map/ppermute | solution.py:309
  21.1 10.7 %collective-permute-start.2 = (bf16[1,2,640,128]{3,2,1,0:T(8,128)(2,1)}, bf16[1,2,640,128]{3,2,1,0:T(8,128)(2,1)S(1)}, u32[]{:S(2)}, u32[]{:S(2)}) collective-permute-start(bf16[1,2,640,128]{3,2,1,0:T(8,128)(2,1)} %get-tuple-element.85), channel_id=1, source_target_pairs={{2,0},{3,1},{4,2},{5,3},{6,4},{7,5},{8,6},{9,7},{10,8},{11,9},{12,... | collective-permute-start | bytes 983048 | tf_op jit(solution)/shard_map/ppermute | solution.py:309
  30.3 64.9 %collective-permute-start.3 = (bf16[3,2,768,128]{3,2,1,0:T(8,128)(2,1)}, bf16[3,2,768,128]{3,2,1,0:T(8,128)(2,1)S(1)}, u32[]{:S(2)}, u32[]{:S(2)}) collective-permute-start(bf16[3,2,768,128]{3,2,1,0:T(8,128)(2,1)} %get-tuple-element.87), channel_id=1, source_target_pairs={{0,1},{1,0},{2,3},{3,2},{4,5},{5,4},{6,7},{7,6},{8,9},{9,8},{10,11... | collective-permute-start | bytes 3538952 | tf_op jit(solution)/shard_map/ppermute | solution.py:309
  31.8 0.7 copy-start.19
  31.8 0.8 copy-start.20
  95.2 1.0 copy-start.10
  101.0 13.1 %copy-start.18 = (bf16[1,2,640,128]{3,2,1,0:T(8,128)(2,1)S(1)}, bf16[1,2,640,128]{3,2,1,0:T(8,128)(2,1)}, u32[]{:S(2)}) copy-start(bf16[1,2,640,128]{3,2,1,0:T(8,128)(2,1)} %get-tuple-element.102) | copy-start | bytes 983044
  101.0 16.5 %copy-start.17 = (bf16[1,2,640,128]{3,2,1,0:T(8,128)(2,1)S(1)}, bf16[1,2,640,128]{3,2,1,0:T(8,128)(2,1)}, u32[]{:S(2)}) copy-start(bf16[1,2,640,128]{3,2,1,0:T(8,128)(2,1)} %get-tuple-element.103) | copy-start | bytes 983044
  104.4 28.6 %collective-permute-start.4 = (bf16[3,2,768,128]{3,2,1,0:T(8,128)(2,1)}, bf16[3,2,768,128]{3,2,1,0:T(8,128)(2,1)S(1)}, u32[]{:S(2)}, u32[]{:S(2)}) collective-permute-start(bf16[3,2,768,128]{3,2,1,0:T(8,128)(2,1)} %get-tuple-element.90), channel_id=1, source_target_pairs={{0,1},{1,0},{2,3},{3,2},{4,5},{5,4},{6,7},{7,6},{8,9},{9,8},{10,11... | collective-permute-start | bytes 3538952 | tf_op jit(solution)/shard_map/ppermute | solution.py:309
  105.1 36.1 %collective-permute-start.5 = (bf16[3,2,640,128]{3,2,1,0:T(8,128)(2,1)}, bf16[3,2,640,128]{3,2,1,0:T(8,128)(2,1)}, u32[]{:S(2)}, u32[]{:S(2)}) collective-permute-start(bf16[3,2,640,128]{3,2,1,0:T(8,128)(2,1)} %get-tuple-element.94), channel_id=1, source_target_pairs={{0,2},{1,3},{2,4},{3,5},{4,6},{5,7},{6,8},{7,9},{8,10},{9,11},{10,... | collective-permute-start | bytes 2949128 | tf_op jit(solution)/shard_map/ppermute | solution.py:309
  108.0 35.1 %collective-permute-start.6 = (bf16[3,2,640,128]{3,2,1,0:T(8,128)(2,1)}, bf16[3,2,640,128]{3,2,1,0:T(8,128)(2,1)}, u32[]{:S(2)}, u32[]{:S(2)}) collective-permute-start(bf16[3,2,640,128]{3,2,1,0:T(8,128)(2,1)} %get-tuple-element.95), channel_id=1, source_target_pairs={{2,0},{3,1},{4,2},{5,3},{6,4},{7,5},{8,6},{9,7},{10,8},{11,9},{12,... | collective-permute-start | bytes 2949128 | tf_op jit(solution)/shard_map/ppermute | solution.py:309
  114.1 222.9 %collective-permute-start.8 = (bf16[1,2,640,128]{3,2,1,0:T(8,128)(2,1)S(1)}, bf16[1,2,640,128]{3,2,1,0:T(8,128)(2,1)S(1)}, u32[]{:S(2)}, u32[]{:S(2)}) collective-permute-start(bf16[1,2,640,128]{3,2,1,0:T(8,128)(2,1)S(1)} %copy-done.18), channel_id=1, source_target_pairs={{2,0},{3,1},{4,2},{5,3},{6,4},{7,5},{8,6},{9,7},{10,8},{11,9},{12,... | collective-permute-start | bytes 983048 | tf_op jit(solution)/shard_map/ppermute | solution.py:309
  117.5 223.0 %collective-permute-start.9 = (bf16[1,2,640,128]{3,2,1,0:T(8,128)(2,1)S(1)}, bf16[1,2,640,128]{3,2,1,0:T(8,128)(2,1)S(1)}, u32[]{:S(2)}, u32[]{:S(2)}) collective-permute-start(bf16[1,2,640,128]{3,2,1,0:T(8,128)(2,1)S(1)} %copy-done.17), channel_id=1, source_target_pairs={{0,2},{1,3},{2,4},{3,5},{4,6},{5,7},{6,8},{7,9},{8,10},{9,11},{10,... | collective-permute-start | bytes 983048 | tf_op jit(solution)/shard_map/ppermute | solution.py:309
  133.0 1.0 copy-start.11
  138.9 4.2 copy-start.16
  140.8 191.0 %collective-permute-start.7 = (bf16[1,2,768,128]{3,2,1,0:T(8,128)(2,1)}, bf16[1,2,768,128]{3,2,1,0:T(8,128)(2,1)S(1)}, u32[]{:S(2)}, u32[]{:S(2)}) collective-permute-start(bf16[1,2,768,128]{3,2,1,0:T(8,128)(2,1)} %get-tuple-element.99), channel_id=1, source_target_pairs={{0,1},{1,0},{2,3},{3,2},{4,5},{5,4},{6,7},{7,6},{8,9},{9,8},{10,11... | collective-permute-start | bytes 1179656 | tf_op jit(solution)/shard_map/ppermute | solution.py:309
  141.2 203.6 %collective-permute-start.10 = (bf16[3,2,640,128]{3,2,1,0:T(8,128)(2,1)}, bf16[3,2,640,128]{3,2,1,0:T(8,128)(2,1)}, u32[]{:S(2)}, u32[]{:S(2)}) collective-permute-start(bf16[3,2,640,128]{3,2,1,0:T(8,128)(2,1)} %get-tuple-element.106), channel_id=1, source_target_pairs={{0,2},{1,3},{2,4},{3,5},{4,6},{5,7},{6,8},{7,9},{8,10},{9,11},{10,... | collective-permute-start | bytes 2949128 | tf_op jit(solution)/shard_map/ppermute | solution.py:309
  143.1 208.8 %collective-permute-start.11 = (bf16[3,2,640,128]{3,2,1,0:T(8,128)(2,1)S(1)}, bf16[3,2,640,128]{3,2,1,0:T(8,128)(2,1)}, u32[]{:S(2)}, u32[]{:S(2)}) collective-permute-start(bf16[3,2,640,128]{3,2,1,0:T(8,128)(2,1)S(1)} %copy-done.16), channel_id=1, source_target_pairs={{2,0},{3,1},{4,2},{5,3},{6,4},{7,5},{8,6},{9,7},{10,8},{11,9},{12,... | collective-permute-start | bytes 2949128 | tf_op jit(solution)/shard_map/ppermute | solution.py:309
  331.9 2.5 copy-start.13
  331.9 203.8 %collective-permute-start.12 = (bf16[3,2,640,128]{3,2,1,0:T(8,128)(2,1)}, bf16[3,2,640,128]{3,2,1,0:T(8,128)(2,1)S(1)}, u32[]{:S(2)}, u32[]{:S(2)}) collective-permute-start(bf16[3,2,640,128]{3,2,1,0:T(8,128)(2,1)} %get-tuple-element.112), channel_id=1, source_target_pairs={{2,0},{3,1},{4,2},{5,3},{6,4},{7,5},{8,6},{9,7},{10,8},{11,9},{12,... | collective-permute-start | bytes 2949128 | tf_op jit(solution)/shard_map/ppermute | solution.py:309
  337.0 5.4 copy-start.6
  337.0 202.7 %collective-permute-start.13 = (bf16[3,2,640,128]{3,2,1,0:T(8,128)(2,1)}, bf16[3,2,640,128]{3,2,1,0:T(8,128)(2,1)S(1)}, u32[]{:S(2)}, u32[]{:S(2)}) collective-permute-start(bf16[3,2,640,128]{3,2,1,0:T(8,128)(2,1)} %get-tuple-element.113), channel_id=1, source_target_pairs={{0,2},{1,3},{2,4},{3,5},{4,6},{5,7},{6,8},{7,9},{8,10},{9,11},{10,... | collective-permute-start | bytes 2949128 | tf_op jit(solution)/shard_map/ppermute | solution.py:309
  340.4 2.0 copy-start.7
  340.4 208.4 %collective-permute-start.14 = (bf16[1,2,640,128]{3,2,1,0:T(8,128)(2,1)}, bf16[1,2,640,128]{3,2,1,0:T(8,128)(2,1)}, u32[]{:S(2)}, u32[]{:S(2)}) collective-permute-start(bf16[1,2,640,128]{3,2,1,0:T(8,128)(2,1)} %get-tuple-element.116), channel_id=1, source_target_pairs={{0,2},{1,3},{2,4},{3,5},{4,6},{5,7},{6,8},{7,9},{8,10},{9,11},{10,... | collective-permute-start | bytes 983048 | tf_op jit(solution)/shard_map/ppermute | solution.py:309
  344.8 204.0 %collective-permute-start.15 = (bf16[1,2,640,128]{3,2,1,0:T(8,128)(2,1)}, bf16[1,2,640,128]{3,2,1,0:T(8,128)(2,1)}, u32[]{:S(2)}, u32[]{:S(2)}) collective-permute-start(bf16[1,2,640,128]{3,2,1,0:T(8,128)(2,1)} %get-tuple-element.117), channel_id=1, source_target_pairs={{2,0},{3,1},{4,2},{5,3},{6,4},{7,5},{8,6},{9,7},{10,8},{11,9},{12,... | collective-permute-start | bytes 983048 | tf_op jit(solution)/shard_map/ppermute | solution.py:309
  533.8 77.8 %collective-permute-start.16 = (bf16[3,2,640,128]{3,2,1,0:T(8,128)(2,1)}, bf16[3,2,640,128]{3,2,1,0:T(8,128)(2,1)S(1)}, u32[]{:S(2)}, u32[]{:S(2)}) collective-permute-start(bf16[3,2,640,128]{3,2,1,0:T(8,128)(2,1)} %get-tuple-element.124), channel_id=1, source_target_pairs={{2,0},{3,1},{4,2},{5,3},{6,4},{7,5},{8,6},{9,7},{10,8},{11,9},{12,... | collective-permute-start | bytes 2949128 | tf_op jit(solution)/shard_map/ppermute | solution.py:309
  535.7 4.0 copy-start
  535.7 75.8 %collective-permute-start.17 = (bf16[3,2,640,128]{3,2,1,0:T(8,128)(2,1)}, bf16[3,2,640,128]{3,2,1,0:T(8,128)(2,1)S(1)}, u32[]{:S(2)}, u32[]{:S(2)}) collective-permute-start(bf16[3,2,640,128]{3,2,1,0:T(8,128)(2,1)} %get-tuple-element.125), channel_id=1, source_target_pairs={{0,2},{1,3},{2,4},{3,5},{4,6},{5,7},{6,8},{7,9},{8,10},{9,11},{10,... | collective-permute-start | bytes 2949128 | tf_op jit(solution)/shard_map/ppermute | solution.py:309
  539.7 1.0 copy-start.1
  544.9 110.6 %collective-permute-start.21 = (bf16[3,2,768,128]{3,2,1,0:T(8,128)(2,1)}, bf16[3,2,768,128]{3,2,1,0:T(8,128)(2,1)S(1)}, u32[]{:S(2)}, u32[]{:S(2)}) collective-permute-start(bf16[3,2,768,128]{3,2,1,0:T(8,128)(2,1)} %get-tuple-element.137), channel_id=1, source_target_pairs={{0,1},{1,0},{2,3},{3,2},{4,5},{5,4},{6,7},{7,6},{8,9},{9,8},{10,11... | collective-permute-start | bytes 3538952 | tf_op jit(solution)/shard_map/ppermute | solution.py:309
  611.6 1.0 copy-start.2
  611.6 1.4 copy-start.3
  617.2 45.0 %collective-permute-start.22 = (bf16[3,2,768,128]{3,2,1,0:T(8,128)(2,1)}, bf16[3,2,768,128]{3,2,1,0:T(8,128)(2,1)S(1)}, u32[]{:S(2)}, u32[]{:S(2)}) collective-permute-start(bf16[3,2,768,128]{3,2,1,0:T(8,128)(2,1)} %get-tuple-element.143), channel_id=1, source_target_pairs={{0,1},{1,0},{2,3},{3,2},{4,5},{5,4},{6,7},{7,6},{8,9},{9,8},{10,11... | collective-permute-start | bytes 3538952 | tf_op jit(solution)/shard_map/ppermute | solution.py:309
  617.2 30.9 %collective-permute-start.18 = (bf16[1,2,768,128]{3,2,1,0:T(8,128)(2,1)}, bf16[1,2,768,128]{3,2,1,0:T(8,128)(2,1)S(1)}, u32[]{:S(2)}, u32[]{:S(2)}) collective-permute-start(bf16[1,2,768,128]{3,2,1,0:T(8,128)(2,1)} %get-tuple-element.129), channel_id=1, source_target_pairs={{0,1},{1,0},{2,3},{3,2},{4,5},{5,4},{6,7},{7,6},{8,9},{9,8},{10,11... | collective-permute-start | bytes 1179656 | tf_op jit(solution)/shard_map/ppermute | solution.py:309
  619.2 32.7 %collective-permute-start.19 = (bf16[1,2,640,128]{3,2,1,0:T(8,128)(2,1)}, bf16[1,2,640,128]{3,2,1,0:T(8,128)(2,1)S(1)}, u32[]{:S(2)}, u32[]{:S(2)}) collective-permute-start(bf16[1,2,640,128]{3,2,1,0:T(8,128)(2,1)} %get-tuple-element.132), channel_id=1, source_target_pairs={{2,0},{3,1},{4,2},{5,3},{6,4},{7,5},{8,6},{9,7},{10,8},{11,9},{12,... | collective-permute-start | bytes 983048 | tf_op jit(solution)/shard_map/ppermute | solution.py:309
  623.6 28.4 %collective-permute-start.20 = (bf16[1,2,640,128]{3,2,1,0:T(8,128)(2,1)}, bf16[1,2,640,128]{3,2,1,0:T(8,128)(2,1)S(1)}, u32[]{:S(2)}, u32[]{:S(2)}) collective-permute-start(bf16[1,2,640,128]{3,2,1,0:T(8,128)(2,1)} %get-tuple-element.133), channel_id=1, source_target_pairs={{0,2},{1,3},{2,4},{3,5},{4,6},{5,7},{6,8},{7,9},{8,10},{9,11},{10,... | collective-permute-start | bytes 983048 | tf_op jit(solution)/shard_map/ppermute | solution.py:309
  648.1 0.7 copy-start.14
  652.0 0.7 copy-start.4
  652.0 0.9 copy-start.5
  655.3 13.5 %collective-permute-start.23 = (bf16[1,2,768,128]{3,2,1,0:T(8,128)(2,1)}, bf16[1,2,768,128]{3,2,1,0:T(8,128)(2,1)S(1)}, u32[]{:S(2)}, u32[]{:S(2)}) collective-permute-start(bf16[1,2,768,128]{3,2,1,0:T(8,128)(2,1)} %get-tuple-element.149), channel_id=1, source_target_pairs={{0,1},{1,0},{2,3},{3,2},{4,5},{5,4},{6,7},{7,6},{8,9},{9,8},{10,11... | collective-permute-start | bytes 1179656 | tf_op jit(solution)/shard_map/ppermute | solution.py:309
  655.6 1.1 copy-start.8
  662.2 1.1 copy-start.9
  668.8 0.7 copy-start.12

commit v7 on v4

--- a/solution.py
+++ b/solution.py
@@ -237,7 +237,7 @@
             accv[rows] = accv[rows] + dot(e[to], dos[...])
         return carry
 
-    lax.fori_loop(0, 4, block_step, 0)
+    lax.fori_loop(0, 4, block_step, 0, unroll=2)
 
     b1, b2, b3 = BASE[1:]
     for which, acc, own in ((0, acck, gk), (1, accv, gv)):

time: 675 us -> 673 us (level)
  no operation moved by 1% of the time
where the time goes in v7:
time: 673 us; the launch traced here: 663 us
  Pallas kernels  538 us (80%)
  starting transfers between devices  70.5 us (10%)
  waiting for transfers between devices  42.5 us (6%)
  local copies, waits for them, and re-layouts  9.11 us (1%)
    pallas_call x4, Pallas kernels, attend(): pl.pallas_call(body, grid=(pairs,), in_specs=[SMEM, SMEM] + [columns(star...  486 us
    ppermute x24, starting transfers between devices, moved(): return lax.ppermute(array, AXES, pairs)  70.5 us
    ppermute x24, waiting for transfers between devices, moved(): return lax.ppermute(array, AXES, pairs)  42.5 us
    pallas_call x4, Pallas kernels, finish(): pl.pallas_call(body, grid=(pairs,), in_specs=[SMEM] + [own_rows()] * 2 +...  16.4 us
    pallas_call x4, Pallas kernels, cross_rows(): pl.pallas_call(body, grid=(pairs,), in_specs=[SMEM, columns(start), colum...  13.7 us
  transfers between devices with their start and end apart: 24, of which 5 were waited for; matrix products, arithmetic and copies ran while one was open for 0% of the time, Pallas kernels for 79%

profile of v7, /device:TPU:36, one launch (start us, length us, event | category | flops | bytes accessed | tf_op | source)
XLA Modules:
  0.0 663.0 jit_solution(16816959423668642817)
XLA Ops:
  1.3 2.1 pair_rows.4
  3.4 19.4 %collective-permute-done.p = bf16[2,2,768,128]{3,2,1,0:T(8,128)(2,1)S(1)} collective-permute-done((bf16[2,2,768,128]{3,2,1,0:T(8,128)(2,1)}, bf16[2,2,768,128]{3,2,1,0:T(8,128)(2,1)S(1)}, u32[]{:S(2)}, u32[]{:S(2)}) %collective-permute-start) | collective-permute-done | bytes 786464 | tf_op jit(solution)/shard_map/ppermute | solution.py:309
  23.7 3.1 cross_rows.4
  26.8 3.5 collective-permute-start.1
  30.3 5.1 collective-permute-start.2
  36.1 3.3 pair_rows.5
  39.4 1.6 collective-permute-start.3
  41.0 2.7 collective-permute-done.1.refs_8_.refs_9_
  43.7 4.0 collective-permute-done.2.refs_10_.refs_11_
  48.5 121.4 %attend_pairs.4 = (bf16[1024,1024]{1,0:T(8,128)(2,1)}, bf16[1024,1024]{1,0:T(8,128)(2,1)}, f32[2,1024,128]{2,1,0:T(8,128)}, f32[2,1024,128]{2,1,0:T(8,128)}, bf1...) custom-call(s32[2]{0:T(128)} %get-tuple-element.82.refs_0_, ...), custom_call_target="tpu_custom_call" | custom-call | flops 28000000000 | bytes 8000000 | tf_op jit(solution)/shard_map/attend_pairs/pallas_call | solution.py:450
  170.0 1.0 copy-done.9
  171.0 4.8 cross_rows.5
  175.8 3.5 collective-permute-start.5
  179.2 5.1 collective-permute-start.6
  184.3 2.1 pair_rows.6
  186.4 1.6 collective-permute-start.4
  188.1 1.9 collective-permute-start.8
  190.0 4.3 collective-permute-start.9
  194.2 11.6 %collective-permute-done.4.p = bf16[2,2,768,128]{3,2,1,0:T(8,128)(2,1)S(1)} collective-permute-done((bf16[2,2,768,128]{3,2,1,0:T(8,128)(2,1)}, bf16[2,2,768,128]{3,2,1,0:T(8,128)(2,1)S(1)}, u32[]{:S(2)}, u32[]{:S(2)}) %collective-permute-start.4) | collective-permute-done | bytes 786464 | tf_op jit(solution)/shard_map/ppermute | solution.py:309
  206.7 3.2 cross_rows.6
  209.9 1.9 pair_rows.7
  212.2 2.3 collective-permute-start.10
  214.5 6.3 collective-permute-start.11
  220.8 180.8 %attend_pairs.5 = (bf16[1024,1024]{1,0:T(8,128)(2,1)}, bf16[1024,1024]{1,0:T(8,128)(2,1)}, f32[3,1024,128]{2,1,0:T(8,128)}, f32[3,1024,128]{2,1,0:T(8,128)}, bf1...) custom-call(s32[2]{0:T(128)} %get-tuple-element.92.refs_0_, ...), custom_call_target="tpu_custom_call", output_to_operand_aliasing={{0}: (12, {}), {1}: (13, {})} | custom-call | flops 41999998976 | bytes 12000000 | tf_op jit(solution)/shard_map/attend_pairs/pallas_call | solution.py:450
  401.6 1.9 collective-permute-start.12
  403.6 2.6 cross_rows.7
  406.2 3.9 collective-permute-start.13
  410.2 2.1 collective-permute-start.14
  412.3 3.0 pair_grads.4
  415.2 6.6 collective-permute-start.15
  421.9 4.0 collective-permute-start.18
  425.8 121.4 %attend_pairs.6 = (bf16[1024,1024]{1,0:T(8,128)(2,1)}, bf16[1024,1024]{1,0:T(8,128)(2,1)}, f32[2,1024,128]{2,1,0:T(8,128)}, f32[2,1024,128]{2,1,0:T(8,128)}, bf1...) custom-call(s32[2]{0:T(128)} %get-tuple-element.104.refs_0_, ...), custom_call_target="tpu_custom_call", output_to_operand_aliasing={{0}: (12, {}), {1}: (13, {})} | custom-call | flops 28000000000 | bytes 8000000 | tf_op jit(solution)/shard_map/attend_pairs/pallas_call | solution.py:450
  547.3 1.9 collective-permute-start.16
  549.3 4.1 collective-permute-start.17
  553.4 4.2 pair_grads.5
  557.7 62.4 %attend_pairs.7 = (bf16[1024,1024]{1,0:T(8,128)(2,1)}, bf16[1024,1024]{1,0:T(8,128)(2,1)}, f32[1,1024,128]{2,1,0:T(8,128)}, f32[1,1024,128]{2,1,0:T(8,128)}, bf1...) custom-call(s32[2]{0:T(128)} %get-tuple-element.114.refs_0_, ...), custom_call_target="tpu_custom_call", output_to_operand_aliasing={{0}: (12, {}), {1}: (13, {})} | custom-call | flops 14000000000 | bytes 4000000 | tf_op jit(solution)/shard_map/attend_pairs/pallas_call | solution.py:450
  621.2 3.0 pair_grads.6
  624.1 1.8 collective-permute-start.22
  625.9 4.1 collective-permute-start.19
  630.0 1.9 collective-permute-start.20
  632.9 3.9 sum_grads.4
  636.8 4.9 collective-permute-done.20.below.refs_4_
  642.4 2.4 pair_grads.7
  644.8 2.4 collective-permute-start.23
  647.2 1.1 copy-done.8
  648.3 5.5 sum_grads.5
  654.8 3.9 sum_grads.6
  659.4 3.1 sum_grads.7
  (61 shorter events, 8.8 us)
Async XLA Ops:
  3.3 19.5 %collective-permute-start = (bf16[2,2,768,128]{3,2,1,0:T(8,128)(2,1)}, bf16[2,2,768,128]{3,2,1,0:T(8,128)(2,1)S(1)}, u32[]{:S(2)}, u32[]{:S(2)}) collective-permute-start(bf16[2,2,768,128]{3,2,1,0:T(8,128)(2,1)} %get-tuple-element.80), channel_id=1, source_target_pairs={{0,1},{1,0},{2,3},{3,2},{4,5},{5,4},{6,7},{7,6},{8,9},{9,8},{10,11... | collective-permute-start | bytes 2359304 | tf_op jit(solution)/shard_map/ppermute | solution.py:309
  22.8 0.9 copy-start.13
  26.8 16.9 %collective-permute-start.1 = (bf16[2,2,640,128]{3,2,1,0:T(8,128)(2,1)}, bf16[2,2,640,128]{3,2,1,0:T(8,128)(2,1)S(1)}, u32[]{:S(2)}, u32[]{:S(2)}) collective-permute-start(bf16[2,2,640,128]{3,2,1,0:T(8,128)(2,1)} %get-tuple-element.84), channel_id=1, source_target_pairs={{0,2},{1,3},{2,4},{3,5},{4,6},{5,7},{6,8},{7,9},{8,10},{9,11},{10,... | collective-permute-start | bytes 1966088 | tf_op jit(solution)/shard_map/ppermute | solution.py:309
  30.3 17.4 %collective-permute-start.2 = (bf16[2,2,640,128]{3,2,1,0:T(8,128)(2,1)}, bf16[2,2,640,128]{3,2,1,0:T(8,128)(2,1)S(1)}, u32[]{:S(2)}, u32[]{:S(2)}) collective-permute-start(bf16[2,2,640,128]{3,2,1,0:T(8,128)(2,1)} %get-tuple-element.85), channel_id=1, source_target_pairs={{2,0},{3,1},{4,2},{5,3},{6,4},{7,5},{8,6},{9,7},{10,8},{11,9},{12,... | collective-permute-start | bytes 1966088 | tf_op jit(solution)/shard_map/ppermute | solution.py:309
  39.4 130.5 %collective-permute-start.3 = (bf16[3,2,768,128]{3,2,1,0:T(8,128)(2,1)}, bf16[3,2,768,128]{3,2,1,0:T(8,128)(2,1)S(1)}, u32[]{:S(2)}, u32[]{:S(2)}) collective-permute-start(bf16[3,2,768,128]{3,2,1,0:T(8,128)(2,1)} %get-tuple-element.87), channel_id=1, source_target_pairs={{0,1},{1,0},{2,3},{3,2},{4,5},{5,4},{6,7},{7,6},{8,9},{9,8},{10,11... | collective-permute-start | bytes 3538952 | tf_op jit(solution)/shard_map/ppermute | solution.py:309
  43.7 4.0 copy-start.17
  47.7 0.8 copy-start.18
  169.9 1.0 copy-start.9
  175.8 36.5 %collective-permute-start.5 = (bf16[3,2,640,128]{3,2,1,0:T(8,128)(2,1)}, bf16[3,2,640,128]{3,2,1,0:T(8,128)(2,1)S(1)}, u32[]{:S(2)}, u32[]{:S(2)}) collective-permute-start(bf16[3,2,640,128]{3,2,1,0:T(8,128)(2,1)} %get-tuple-element.94), channel_id=1, source_target_pairs={{0,2},{1,3},{2,4},{3,5},{4,6},{5,7},{6,8},{7,9},{8,10},{9,11},{10,... | collective-permute-start | bytes 2949128 | tf_op jit(solution)/shard_map/ppermute | solution.py:309
  179.2 35.3 %collective-permute-start.6 = (bf16[3,2,640,128]{3,2,1,0:T(8,128)(2,1)}, bf16[3,2,640,128]{3,2,1,0:T(8,128)(2,1)}, u32[]{:S(2)}, u32[]{:S(2)}) collective-permute-start(bf16[3,2,640,128]{3,2,1,0:T(8,128)(2,1)} %get-tuple-element.95), channel_id=1, source_target_pairs={{2,0},{3,1},{4,2},{5,3},{6,4},{7,5},{8,6},{9,7},{10,8},{11,9},{12,... | collective-permute-start | bytes 2949128 | tf_op jit(solution)/shard_map/ppermute | solution.py:309
  186.4 19.4 %collective-permute-start.4 = (bf16[2,2,768,128]{3,2,1,0:T(8,128)(2,1)}, bf16[2,2,768,128]{3,2,1,0:T(8,128)(2,1)S(1)}, u32[]{:S(2)}, u32[]{:S(2)}) collective-permute-start(bf16[2,2,768,128]{3,2,1,0:T(8,128)(2,1)} %get-tuple-element.90), channel_id=1, source_target_pairs={{0,1},{1,0},{2,3},{3,2},{4,5},{5,4},{6,7},{7,6},{8,9},{9,8},{10,11... | collective-permute-start | bytes 2359304 | tf_op jit(solution)/shard_map/ppermute | solution.py:309
  188.1 218.1 %collective-permute-start.8 = (bf16[2,2,640,128]{3,2,1,0:T(8,128)(2,1)}, bf16[2,2,640,128]{3,2,1,0:T(8,128)(2,1)S(1)}, u32[]{:S(2)}, u32[]{:S(2)}) collective-permute-start(bf16[2,2,640,128]{3,2,1,0:T(8,128)(2,1)} %get-tuple-element.102), channel_id=1, source_target_pairs={{2,0},{3,1},{4,2},{5,3},{6,4},{7,5},{8,6},{9,7},{10,8},{11,9},{12,... | collective-permute-start | bytes 1966088 | tf_op jit(solution)/shard_map/ppermute | solution.py:309
  190.0 220.2 %collective-permute-start.9 = (bf16[2,2,640,128]{3,2,1,0:T(8,128)(2,1)}, bf16[2,2,640,128]{3,2,1,0:T(8,128)(2,1)S(1)}, u32[]{:S(2)}, u32[]{:S(2)}) collective-permute-start(bf16[2,2,640,128]{3,2,1,0:T(8,128)(2,1)} %get-tuple-element.103), channel_id=1, source_target_pairs={{0,2},{1,3},{2,4},{3,5},{4,6},{5,7},{6,8},{7,9},{8,10},{9,11},{10,... | collective-permute-start | bytes 1966088 | tf_op jit(solution)/shard_map/ppermute | solution.py:309
  205.8 0.9 copy-start.12
  211.8 189.8 %collective-permute-start.7 = (bf16[1,2,768,128]{3,2,1,0:T(8,128)(2,1)}, bf16[1,2,768,128]{3,2,1,0:T(8,128)(2,1)S(1)}, u32[]{:S(2)}, u32[]{:S(2)}) collective-permute-start(bf16[1,2,768,128]{3,2,1,0:T(8,128)(2,1)} %get-tuple-element.99), channel_id=1, source_target_pairs={{0,1},{1,0},{2,3},{3,2},{4,5},{5,4},{6,7},{7,6},{8,9},{9,8},{10,11... | collective-permute-start | bytes 1179656 | tf_op jit(solution)/shard_map/ppermute | solution.py:309
  212.2 8.6 %copy-start.16 = (bf16[3,2,640,128]{3,2,1,0:T(8,128)(2,1)}, bf16[3,2,640,128]{3,2,1,0:T(8,128)(2,1)S(1)}, u32[]{:S(2)}) copy-start(bf16[3,2,640,128]{3,2,1,0:T(8,128)(2,1)S(1)} %collective-permute-done.5.refs_8_.refs_9_) | copy-start | bytes 2949124
  212.2 203.0 %collective-permute-start.10 = (bf16[2,2,640,128]{3,2,1,0:T(8,128)(2,1)}, bf16[2,2,640,128]{3,2,1,0:T(8,128)(2,1)}, u32[]{:S(2)}, u32[]{:S(2)}) collective-permute-start(bf16[2,2,640,128]{3,2,1,0:T(8,128)(2,1)} %get-tuple-element.106), channel_id=1, source_target_pairs={{0,2},{1,3},{2,4},{3,5},{4,6},{5,7},{6,8},{7,9},{8,10},{9,11},{10,... | collective-permute-start | bytes 1966088 | tf_op jit(solution)/shard_map/ppermute | solution.py:309
  214.5 207.4 %collective-permute-start.11 = (bf16[2,2,640,128]{3,2,1,0:T(8,128)(2,1)}, bf16[2,2,640,128]{3,2,1,0:T(8,128)(2,1)}, u32[]{:S(2)}, u32[]{:S(2)}) collective-permute-start(bf16[2,2,640,128]{3,2,1,0:T(8,128)(2,1)} %get-tuple-element.107), channel_id=1, source_target_pairs={{2,0},{3,1},{4,2},{5,3},{6,4},{7,5},{8,6},{9,7},{10,8},{11,9},{12,... | collective-permute-start | bytes 1966088 | tf_op jit(solution)/shard_map/ppermute | solution.py:309
  401.6 1.9 copy-start.15
  401.6 145.7 %collective-permute-start.12 = (bf16[3,2,640,128]{3,2,1,0:T(8,128)(2,1)}, bf16[3,2,640,128]{3,2,1,0:T(8,128)(2,1)S(1)}, u32[]{:S(2)}, u32[]{:S(2)}) collective-permute-start(bf16[3,2,640,128]{3,2,1,0:T(8,128)(2,1)} %get-tuple-element.112), channel_id=1, source_target_pairs={{2,0},{3,1},{4,2},{5,3},{6,4},{7,5},{8,6},{9,7},{10,8},{11,9},{12,... | collective-permute-start | bytes 2949128 | tf_op jit(solution)/shard_map/ppermute | solution.py:309
  406.2 6.1 copy-start.4
  406.2 143.0 %collective-permute-start.13 = (bf16[3,2,640,128]{3,2,1,0:T(8,128)(2,1)}, bf16[3,2,640,128]{3,2,1,0:T(8,128)(2,1)S(1)}, u32[]{:S(2)}, u32[]{:S(2)}) collective-permute-start(bf16[3,2,640,128]{3,2,1,0:T(8,128)(2,1)} %get-tuple-element.113), channel_id=1, source_target_pairs={{0,2},{1,3},{2,4},{3,5},{4,6},{5,7},{6,8},{7,9},{8,10},{9,11},{10,... | collective-permute-start | bytes 2949128 | tf_op jit(solution)/shard_map/ppermute | solution.py:309
  410.2 2.1 copy-start.5
  410.2 147.5 %collective-permute-start.14 = (bf16[1,2,640,128]{3,2,1,0:T(8,128)(2,1)}, bf16[1,2,640,128]{3,2,1,0:T(8,128)(2,1)}, u32[]{:S(2)}, u32[]{:S(2)}) collective-permute-start(bf16[1,2,640,128]{3,2,1,0:T(8,128)(2,1)} %get-tuple-element.116), channel_id=1, source_target_pairs={{0,2},{1,3},{2,4},{3,5},{4,6},{5,7},{6,8},{7,9},{8,10},{9,11},{10,... | collective-permute-start | bytes 983048 | tf_op jit(solution)/shard_map/ppermute | solution.py:309
  415.2 142.4 %collective-permute-start.15 = (bf16[1,2,640,128]{3,2,1,0:T(8,128)(2,1)}, bf16[1,2,640,128]{3,2,1,0:T(8,128)(2,1)}, u32[]{:S(2)}, u32[]{:S(2)}) collective-permute-start(bf16[1,2,640,128]{3,2,1,0:T(8,128)(2,1)} %get-tuple-element.117), channel_id=1, source_target_pairs={{2,0},{3,1},{4,2},{5,3},{6,4},{7,5},{8,6},{9,7},{10,8},{11,9},{12,... | collective-permute-start | bytes 983048 | tf_op jit(solution)/shard_map/ppermute | solution.py:309
  421.9 210.1 %collective-permute-start.18 = (bf16[2,2,768,128]{3,2,1,0:T(8,128)(2,1)}, bf16[2,2,768,128]{3,2,1,0:T(8,128)(2,1)S(1)}, u32[]{:S(2)}, u32[]{:S(2)}) collective-permute-start(bf16[2,2,768,128]{3,2,1,0:T(8,128)(2,1)} %get-tuple-element.129), channel_id=1, source_target_pairs={{0,1},{1,0},{2,3},{3,2},{4,5},{5,4},{6,7},{7,6},{8,9},{9,8},{10,11... | collective-permute-start | bytes 2359304 | tf_op jit(solution)/shard_map/ppermute | solution.py:309
  547.3 6.1 copy-start
  547.3 72.8 %collective-permute-start.16 = (bf16[2,2,640,128]{3,2,1,0:T(8,128)(2,1)}, bf16[2,2,640,128]{3,2,1,0:T(8,128)(2,1)S(1)}, u32[]{:S(2)}, u32[]{:S(2)}) collective-permute-start(bf16[2,2,640,128]{3,2,1,0:T(8,128)(2,1)} %get-tuple-element.124), channel_id=1, source_target_pairs={{2,0},{3,1},{4,2},{5,3},{6,4},{7,5},{8,6},{9,7},{10,8},{11,9},{12,... | collective-permute-start | bytes 1966088 | tf_op jit(solution)/shard_map/ppermute | solution.py:309
  549.3 4.2 copy-start.1
  549.3 70.8 %collective-permute-start.17 = (bf16[2,2,640,128]{3,2,1,0:T(8,128)(2,1)}, bf16[2,2,640,128]{3,2,1,0:T(8,128)(2,1)S(1)}, u32[]{:S(2)}, u32[]{:S(2)}) collective-permute-start(bf16[2,2,640,128]{3,2,1,0:T(8,128)(2,1)} %get-tuple-element.125), channel_id=1, source_target_pairs={{0,2},{1,3},{2,4},{3,5},{4,6},{5,7},{6,8},{7,9},{8,10},{9,11},{10,... | collective-permute-start | bytes 1966088 | tf_op jit(solution)/shard_map/ppermute | solution.py:309
  557.7 89.6 %collective-permute-start.21 = (bf16[3,2,768,128]{3,2,1,0:T(8,128)(2,1)}, bf16[3,2,768,128]{3,2,1,0:T(8,128)(2,1)S(1)}, u32[]{:S(2)}, u32[]{:S(2)}) collective-permute-start(bf16[3,2,768,128]{3,2,1,0:T(8,128)(2,1)} %get-tuple-element.137), channel_id=1, source_target_pairs={{0,1},{1,0},{2,3},{3,2},{4,5},{5,4},{6,7},{7,6},{8,9},{9,8},{10,11... | collective-permute-start | bytes 3538952 | tf_op jit(solution)/shard_map/ppermute | solution.py:309
  620.1 0.9 copy-start.2
  620.1 1.1 copy-start.3
  624.1 29.7 %collective-permute-start.22 = (bf16[2,2,768,128]{3,2,1,0:T(8,128)(2,1)}, bf16[2,2,768,128]{3,2,1,0:T(8,128)(2,1)S(1)}, u32[]{:S(2)}, u32[]{:S(2)}) collective-permute-start(bf16[2,2,768,128]{3,2,1,0:T(8,128)(2,1)} %get-tuple-element.143), channel_id=1, source_target_pairs={{0,1},{1,0},{2,3},{3,2},{4,5},{5,4},{6,7},{7,6},{8,9},{9,8},{10,11... | collective-permute-start | bytes 2359304 | tf_op jit(solution)/shard_map/ppermute | solution.py:309
  625.9 10.8 %collective-permute-start.19 = (bf16[1,2,640,128]{3,2,1,0:T(8,128)(2,1)}, bf16[1,2,640,128]{3,2,1,0:T(8,128)(2,1)S(1)}, u32[]{:S(2)}, u32[]{:S(2)}) collective-permute-start(bf16[1,2,640,128]{3,2,1,0:T(8,128)(2,1)} %get-tuple-element.132), channel_id=1, source_target_pairs={{2,0},{3,1},{4,2},{5,3},{6,4},{7,5},{8,6},{9,7},{10,8},{11,9},{12,... | collective-permute-start | bytes 983048 | tf_op jit(solution)/shard_map/ppermute | solution.py:309
  630.0 11.6 %collective-permute-start.20 = (bf16[1,2,640,128]{3,2,1,0:T(8,128)(2,1)}, bf16[1,2,640,128]{3,2,1,0:T(8,128)(2,1)S(1)}, u32[]{:S(2)}, u32[]{:S(2)}) collective-permute-start(bf16[1,2,640,128]{3,2,1,0:T(8,128)(2,1)} %get-tuple-element.133), channel_id=1, source_target_pairs={{0,2},{1,3},{2,4},{3,5},{4,6},{5,7},{6,8},{7,9},{8,10},{9,11},{10,... | collective-permute-start | bytes 983048 | tf_op jit(solution)/shard_map/ppermute | solution.py:309
  632.0 0.9 copy-start.10
  636.8 4.9 copy-start.6
  641.6 0.7 copy-start.7
  644.8 13.9 %collective-permute-start.23 = (bf16[1,2,768,128]{3,2,1,0:T(8,128)(2,1)}, bf16[1,2,768,128]{3,2,1,0:T(8,128)(2,1)S(1)}, u32[]{:S(2)}, u32[]{:S(2)}) collective-permute-start(bf16[1,2,768,128]{3,2,1,0:T(8,128)(2,1)} %get-tuple-element.149), channel_id=1, source_target_pairs={{0,1},{1,0},{2,3},{3,2},{4,5},{5,4},{6,7},{7,6},{8,9},{9,8},{10,11... | collective-permute-start | bytes 1179656 | tf_op jit(solution)/shard_map/ppermute | solution.py:309
  647.2 1.1 copy-start.8
  653.9 0.9 copy-start.11
  658.7 0.8 copy-start.14
